TPU v7x, 128 devices: a whole 4x4x4 slice. The times are simulated.
128 devices in a mesh: row: 8 (over x, core), col: 16 (over z, y).
Axes of the slice: x: 4, y: 4, z: 4, core: 2. Of those that a mesh axis runs over, the one named last changes fastest.
Arguments:
- factor_trail: bfloat16 [256, 4, 1024, 1024], P(('row', 'col')), may hold values from -0.09375 to 0.09375
- pattern: int32 [256, 4], P(('row', 'col')), may hold values 0 or 1
- rhs_trail: bfloat16 [256, 1024, 512], P(('row', 'col')), may hold values from -6 to 6
- coupling: bfloat16 [4, 4, 1024, 1024], P(None, None, 'row', 'col'), may hold values from -0.125 to 0.125
- diag_inverse: float32 [4, 1024, 1024], P(None, 'col', 'row'), may hold values from -1.5 to 1.5, as said below
- rhs_super: float32 [4, 1024, 512], P(None, 'row'), may hold values from -6 to 6
Outputs:
- solved_blocks: bfloat16 [4, 1024, 512], P(None, 'col')
- updated_trail: float32 [256, 1024, 512], P(('row', 'col'))
Inputs may be any that keep to these rules, and one draw needn't show every extreme that they name: Each diag_inverse[j] is lower triangular with diagonal entries between 0.75 and 1.35.
All inputs are finite; a program needn't handle non-finite values. No bound on the sum of `pattern` on one device may be relied on, other than what follows from the above.
Results may differ from a plain program's by a relative error of at most 0.0049.
Values may be sent and summed in bfloat16 or wider, within the bound.
No kernel may reach another device: no remote copies, remote signals or barrier semaphores. Data moves between devices by JAX's collectives and lax.ppermute only.
A program may use at most 128 MiB of HBM per device.

v0:
```python
import jax
import jax.numpy as jnp
from jax import lax
from jax.sharding import PartitionSpec as P


def per_device(factor_trail, pattern, rhs_trail, coupling, diag_inverse, rhs_super):
    columns_total = rhs_super.shape[0]
    weights = pattern.astype(jnp.bfloat16)
    pieces = []
    solved = []
    for column in range(columns_total):
        right_block = rhs_super[column]
        if column > 0:
            partial_value = jnp.zeros(right_block.shape, jnp.float32)
            for earlier in range(column):
                partial_value = partial_value + jnp.dot(
                    coupling[column, earlier], pieces[earlier], preferred_element_type=jnp.float32
                )
            right_block = right_block - lax.psum(partial_value, "col")
        own_part = jnp.dot(
            diag_inverse[column],
            right_block,
            precision=lax.Precision.HIGHEST,
            preferred_element_type=jnp.float32,
        )
        solved_piece = lax.psum(own_part, "row").astype(jnp.bfloat16)
        pieces.append(solved_piece)
        whole_block = lax.all_gather(solved_piece, "col", axis=0, tiled=True)
        solved.append(whole_block)
    stacked = jnp.stack(solved)
    masked_all = weights[:, :, None, None] * stacked[None]
    updates_sum = jnp.einsum(
        "rjab,rjbn->ran", factor_trail, masked_all, preferred_element_type=jnp.float32
    )
    updated_trail = rhs_trail.astype(jnp.float32) - updates_sum
    solved_blocks = jnp.stack(pieces)
    return (solved_blocks, updated_trail)


def solution(mesh):
    return jax.shard_map(
        per_device,
        mesh=mesh,
        in_specs=(
            P(("row", "col"), None, None, None),
            P(("row", "col"), None),
            P(("row", "col"), None, None),
            P(None, None, "row", "col"),
            P(None, "col", "row"),
            P(None, "row", None),
        ),
        out_specs=(P(None, "col", None), P(("row", "col"), None, None)),
        check_vma=False,
    )
```

profile of v0, /device:TPU:1, one launch (start us, length us, event | category | flops | bytes accessed | tf_op | source)
XLA Modules:
  0.0 558.2 jit_solution(13726806331283339757)
XLA Ops:
  7.2 0.0 copy-start.6
  7.2 0.0 copy-start.9
  7.2 0.0 copy-start.2
  7.2 0.0 all-reduce.8.cloned.1.call-start
  7.2 1.4 fusion.8
  8.6 24.8 %all-reduce.13 = bf16[64,512]{1,0:T(8,128)(2,1)S(1)} all-reduce(f32[64,512]{1,0:T(8,128)S(1)} %fusion.8), channel_id=1, replica_groups=mesh['row'=8,'col'=16] {'row'}, use_global_device_ids=true, to_apply=%region_0.0 | all-reduce | flops 32768 | bytes 196608 | tf_op jit(solution)/shard_map/psum | solution.py:27
  33.4 0.0 copy-start
  33.4 1.7 convolution_bitcast_fusion
  35.1 0.0 all-reduce.8.cloned.1.call-update
  35.1 0.0 all-reduce.10.cloned.1.call-start
  35.2 0.9 fusion.27
  36.1 85.1 %all-reduce.8.cloned.1.call-done = f32[128,512]{1,0:T(8,128)} async-done(((f32[128,512]{1,0:T(8,128)}), f32[128,512]{1,0:T(8,128)}) %all-reduce.8.cloned.1.call-update) | async-done | bytes 262160 | tf_op jit(solution)/shard_map/psum | solution.py:20
  121.2 2.0 convolution_bitcast_fusion.3
  123.2 24.4 %all-reduce.14 = bf16[64,512]{1,0:T(8,128)(2,1)S(1)} all-reduce(f32[64,512]{1,0:T(8,128)} %convolution_bitcast_fusion.3), channel_id=1, replica_groups=mesh['row'=8,'col'=16] {'row'}, use_global_device_ids=true, to_apply=%region_2.0 | all-reduce | flops 32768 | bytes 196608 | tf_op jit(solution)/shard_map/psum | solution.py:27
  147.6 0.0 copy-start.4
  147.6 1.7 fusion.7
  149.3 0.0 all-reduce.10.cloned.1.call-update
  149.3 0.0 all-reduce.12.cloned.1.call-start
  149.4 0.9 fusion.24
  150.3 0.9 convolution_add_fusion.1
  151.3 80.5 %all-reduce.10.cloned.1.call-done = f32[128,512]{1,0:T(8,128)} async-done(((f32[128,512]{1,0:T(8,128)}), f32[128,512]{1,0:T(8,128)}) %all-reduce.10.cloned.1.call-update) | async-done | bytes 262160 | tf_op jit(solution)/shard_map/psum | solution.py:20
  231.8 0.0 copy-done.6
  231.8 1.9 convolution_bitcast_fusion.2
  233.7 25.0 %all-reduce.15 = bf16[64,512]{1,0:T(8,128)(2,1)} all-reduce(f32[64,512]{1,0:T(8,128)} %convolution_bitcast_fusion.2), channel_id=1, replica_groups=mesh['row'=8,'col'=16] {'row'}, use_global_device_ids=true, to_apply=%region_4.0 | all-reduce | flops 32768 | bytes 196608 | tf_op jit(solution)/shard_map/psum | solution.py:27
  258.7 1.8 fusion.6
  260.4 0.0 copy-start.7
  260.4 0.0 all-reduce.12.cloned.1.call-update
  260.5 0.0 all-gather.5.cloned.1.call-start
  260.5 0.0 copy-done
  260.5 0.5 all-gather.5.cloned.1.call-update
  261.0 0.0 copy-start.1
  261.0 0.0 all-gather.7.cloned.1.call-start
  261.1 0.0 copy-done.4
  261.1 0.5 all-gather.7.cloned.1.call-update
  261.6 0.0 copy-start.5
  261.6 0.0 all-gather.9.cloned.1.call-start
  261.7 0.5 all-gather.9.cloned.1.call-update
  262.2 0.0 all-gather.11.cloned.1.call-start
  262.3 80.7 %all-reduce.12.cloned.1.call-done = f32[128,512]{1,0:T(8,128)} async-done(((f32[128,512]{1,0:T(8,128)}), f32[128,512]{1,0:T(8,128)}) %all-reduce.12.cloned.1.call-update) | async-done | bytes 262160 | tf_op jit(solution)/shard_map/psum | solution.py:20
  342.9 1.3 convolution_bitcast_fusion.1
  344.2 24.4 %all-reduce.16 = bf16[64,512]{1,0:T(8,128)(2,1)} all-reduce(f32[64,512]{1,0:T(8,128)S(1)} %convolution_bitcast_fusion.1), channel_id=1, replica_groups=mesh['row'=8,'col'=16] {'row'}, use_global_device_ids=true, to_apply=%region_6.0 | all-reduce | flops 32768 | bytes 196608 | tf_op jit(solution)/shard_map/psum | solution.py:27
  368.6 0.0 copy-start.8
  368.6 0.0 all-gather.11.cloned.1.call-update
  368.7 0.0 copy-done.9
  368.7 0.0 copy-done.2
  368.7 2.5 copy.8
  371.2 0.0 copy-done.7
  371.2 0.0 copy-done.1
  371.2 0.0 copy-done.5
  371.2 0.0 copy-done.8
  371.2 0.7 pad_maximum_fusion.1
  372.0 15.2 %all-gather.5.cloned.1.call-done = bf16[1024,512]{1,0:T(8,128)(2,1)} async-done(((bf16[64,512]{1,0:T(8,128)(2,1)}), bf16[1024,512]{1,0:T(8,128)(2,1)}) %all-gather.5.cloned.1.call-update) | async-done | bytes 1048592 | tf_op jit(solution)/shard_map/all_gather | solution.py:29
  387.1 44.4 %all-gather.7.cloned.1.call-done = bf16[1024,512]{1,0:T(8,128)(2,1)} async-done(((bf16[64,512]{1,0:T(8,128)(2,1)}), bf16[1024,512]{1,0:T(8,128)(2,1)}) %all-gather.7.cloned.1.call-update) | async-done | bytes 1048592 | tf_op jit(solution)/shard_map/all_gather | solution.py:29
  431.5 44.9 %all-gather.9.cloned.1.call-done = bf16[1024,512]{1,0:T(8,128)(2,1)} async-done(((bf16[64,512]{1,0:T(8,128)(2,1)}), bf16[1024,512]{1,0:T(8,128)(2,1)}) %all-gather.9.cloned.1.call-update) | async-done | bytes 1048592 | tf_op jit(solution)/shard_map/all_gather | solution.py:29
  476.4 44.5 %all-gather.11.cloned.1.call-done = bf16[1024,512]{1,0:T(8,128)(2,1)} async-done(((bf16[64,512]{1,0:T(8,128)(2,1)}), bf16[1024,512]{1,0:T(8,128)(2,1)}) %all-gather.11.cloned.1.call-update) | async-done | bytes 1048592 | tf_op jit(solution)/shard_map/all_gather | solution.py:29
  520.9 3.8 pad_maximum_fusion
  524.7 0.0 copy-start.3
  524.7 6.4 %copy.9 = bf16[4,1024,512]{1,2,0:T(8,128)(2,1)} copy(bf16[4,1024,512]{2,1,0:T(8,128)(2,1)} %pad_maximum_fusion) | data formatting | bytes 8388608 | tf_op jit(solution)/shard_map/stack | solution.py:31
  531.2 0.0 copy-done.3
  531.2 14.8 %bitcast_subtract_fusion = f32[2,1024,512]{1,2,0:T(8,128)} fusion(bf16[2,1024,512]{1,2,0:T(8,128)(2,1)S(1)} %copy-done.3, bf16[2,4,1024,1024]{3,2,1,0:T(8,128)(2,1)} %param.6, bf16[4,1024,512]{1,2,0:T(8,128)(2,1)} %copy.9, bf16[2,4]{1,0:T(2,128)(2,1)S(1)} %convert_element_type.23), kind=kOutput, calls=%fused_computation.3 | convolution fusion | flops 8596226048 | bytes 27262992 | tf_op jit(solution)/shard_map/rjab,rjbn->ran/dot_general | solution.py:33
  546.0 5.4 copy.10
  (1 shorter events, 0.0 us)
Async XLA Ops:
  7.2 224.6 %copy-start.6 = (f32[4,128,512]{2,1,0:T(8,128)S(1)}, f32[4,128,512]{2,1,0:T(8,128)}, u32[]{:S(2)}) copy-start(f32[4,128,512]{2,1,0:T(8,128)} %param.11) | copy-start | bytes 3145732
  7.2 361.5 %copy-start.9 = (s32[2,4]{1,0:T(2,128)S(1)}, s32[2,4]{1,0:T(2,128)}, u32[]{:S(2)}) copy-start(s32[2,4]{1,0:T(2,128)} %param.7) | copy-start | bytes 100
  7.2 361.5 %copy-start.2 = (bf16[2,1024,512]{2,1,0:T(8,128)(2,1)S(1)}, bf16[2,1024,512]{2,1,0:T(8,128)(2,1)}, u32[]{:S(2)}) copy-start(bf16[2,1024,512]{2,1,0:T(8,128)(2,1)} %param.8) | copy-start | bytes 6291460
  7.2 114.0 %all-reduce.8.cloned.1.call-start = ((), (), s32[]{:S(2)}) async-start(), calls=%async_computation | async-start | bytes 524288 | tf_op jit(solution)/shard_map/psum | solution.py:20
  33.4 227.1 %copy-start = (bf16[64,512]{1,0:T(8,128)(2,1)}, bf16[64,512]{1,0:T(8,128)(2,1)S(1)}, u32[]{:S(2)}) copy-start(bf16[64,512]{1,0:T(8,128)(2,1)S(1)} %all-reduce.13) | copy-start | bytes 196612
  35.1 196.7 %all-reduce.10.cloned.1.call-start = ((), (), s32[]{:S(2)}) async-start(), calls=%async_computation.1 | async-start | bytes 524288 | tf_op jit(solution)/shard_map/psum | solution.py:20
  147.6 113.5 %copy-start.4 = (bf16[64,512]{1,0:T(8,128)(2,1)}, bf16[64,512]{1,0:T(8,128)(2,1)S(1)}, u32[]{:S(2)}) copy-start(bf16[64,512]{1,0:T(8,128)(2,1)S(1)} %all-reduce.14) | copy-start | bytes 196612
  149.3 193.6 %all-reduce.12.cloned.1.call-start = ((), (), s32[]{:S(2)}) async-start(), calls=%async_computation.2 | async-start | bytes 524288 | tf_op jit(solution)/shard_map/psum | solution.py:20
  260.4 110.8 %copy-start.7 = (bf16[64,512]{1,0:T(8,128)(2,1)S(1)}, bf16[64,512]{1,0:T(8,128)(2,1)}, u32[]{:S(2)}) copy-start(bf16[64,512]{1,0:T(8,128)(2,1)} %all-reduce.15) | copy-start | bytes 196612
  260.5 126.7 %all-gather.5.cloned.1.call-start = ((), (), s32[]{:S(2)}) async-start(), calls=%async_computation.3 | async-start | bytes 1114112 | tf_op jit(solution)/shard_map/all_gather | solution.py:29
  261.0 110.2 %copy-start.1 = (bf16[64,512]{1,0:T(8,128)(2,1)S(1)}, bf16[64,512]{1,0:T(8,128)(2,1)}, u32[]{:S(2)}) copy-start(bf16[64,512]{1,0:T(8,128)(2,1)} %copy-done) | copy-start | bytes 196612
  261.0 170.5 %all-gather.7.cloned.1.call-start = ((), (), s32[]{:S(2)}) async-start(), calls=%async_computation.4 | async-start | bytes 1114112 | tf_op jit(solution)/shard_map/all_gather | solution.py:29
  261.6 109.6 %copy-start.5 = (bf16[64,512]{1,0:T(8,128)(2,1)S(1)}, bf16[64,512]{1,0:T(8,128)(2,1)}, u32[]{:S(2)}) copy-start(bf16[64,512]{1,0:T(8,128)(2,1)} %copy-done.4) | copy-start | bytes 196612
  261.6 214.8 %all-gather.9.cloned.1.call-start = ((), (), s32[]{:S(2)}) async-start(), calls=%async_computation.5 | async-start | bytes 1114112 | tf_op jit(solution)/shard_map/all_gather | solution.py:29
  262.2 258.7 %all-gather.11.cloned.1.call-start = ((), (), s32[]{:S(2)}) async-start(), calls=%async_computation.6 | async-start | bytes 1114112 | tf_op jit(solution)/shard_map/all_gather | solution.py:29
  368.6 2.6 copy-start.8
  524.7 6.5 %copy-start.3 = (bf16[2,1024,512]{1,2,0:T(8,128)(2,1)S(1)}, bf16[2,1024,512]{1,2,0:T(8,128)(2,1)}, u32[]{:S(2)}) copy-start(bf16[2,1024,512]{1,2,0:T(8,128)(2,1)} %copy.8) | copy-start | bytes 6291460
Sparse Core Ops, SparseCore 0:
  35.3 85.9 all-reduce.7
  149.5 82.2 all-reduce.9
  260.6 82.3 all-reduce.11
  345.2 41.9 all-gather.4
  389.4 42.0 all-gather.6
  434.3 42.0 all-gather.8
  478.8 42.0 all-gather.10
where the time goes:
time: 560 us; the launch traced here: 558 us
  waiting for transfers between devices  397 us (71%)
  blocking collectives  98.6 us (18%)
  matrix products  29.3 us (5%)
  local copies, waits for them, and re-layouts  14.4 us (3%)
  between operations  14.3 us (3%)
    psum x3, waiting for transfers between devices, per_device(): right_block = right_block - lax.psum(partial_value, 'col')  246 us
    all_gather x4, waiting for transfers between devices, per_device(): whole_block = lax.all_gather(solved_piece, 'col', axis=0, tiled=True)  149 us
    psum x4, blocking collectives, per_device(): solved_piece = lax.psum(own_part, 'row').astype(jnp.bfloat16)  98.6 us
    dot_general x1, matrix products, per_device(): jnp.einsum('rjab,rjbn->ran', factor_trail, masked_all, preferred_element_...  14.8 us
  transfers between devices with their start and end apart: 7, of which 7 were waited for; matrix products, arithmetic and copies ran while one was open for 1% of the time, Pallas kernels for 0%

commit v1 on v0

v1 whole, which is shorter than its diff:
```python
import jax
import jax.numpy as jnp
from jax import lax
from jax.experimental import pallas as pl
from jax.experimental.pallas import tpu as pltpu
from jax.sharding import Mesh
from jax.sharding import PartitionSpec as P

NT = (((1,), (1,)), ((), ()))
NN = (((1,), (0,)), ((), ()))
VMEM_LIMIT = 48 * 1024 * 1024


def dot(a, b, dims):
    return lax.dot_general(a, b, dims, preferred_element_type=jnp.float32)


def split(value):
    high = value.astype(jnp.bfloat16)
    low = (value - high.astype(jnp.float32)).astype(jnp.bfloat16)
    return high, low


def apply_inverse(right, high_ref_value, low_ref_value):
    high, low = split(right)
    return (
        dot(high, high_ref_value, NT)
        + dot(low, high_ref_value, NT)
        + dot(high, low_ref_value, NT)
    )


def first_kernel(right_ref, inverse_ref, out_ref):
    rows = inverse_ref.shape[0] * inverse_ref.shape[2]
    depth = inverse_ref.shape[3]
    high = inverse_ref[:, 0].reshape(rows, depth)
    low = inverse_ref[:, 1].reshape(rows, depth)
    out_ref[...] = apply_inverse(right_ref[...], high, low)


def step_kernel(column, at, n_parts, *refs):
    part_refs = refs[:n_parts]
    right_ref = refs[n_parts]
    mine_ref, other_ref = refs[n_parts + 1 : n_parts + 3]
    earlier_refs = refs[n_parts + 3 : n_parts + 3 + column - 1]
    solved_ref, out_ref = refs[-2:]
    total = part_refs[0][...]
    for part in part_refs[1:]:
        total = total + part[...]
    solved = total.astype(jnp.bfloat16)
    solved_ref[...] = solved
    before = [ref[...] for ref in earlier_refs] + [solved]
    out = None
    for side, ref in enumerate((mine_ref, other_ref)):
        rows = ref.shape[0] * ref.shape[2]
        depth = ref.shape[3]
        right = right_ref[side]
        for i, block in enumerate(before):
            right = right - dot(block, ref[:, at + 2 + i].reshape(rows, depth), NN)
        term = apply_inverse(
            right, ref[:, at].reshape(rows, depth), ref[:, at + 1].reshape(rows, depth)
        )
        out = term if out is None else out + term
    out_ref[...] = out


def last_kernel(*refs):
    total = refs[0][...]
    for part in refs[1:-1]:
        total = total + part[...]
    refs[-1][...] = total.astype(jnp.bfloat16)


def trail_kernel(first, pattern_ref, base_ref, factor_ref, *refs):
    solved_refs, out_ref = refs[:-1], refs[-1]
    row = pl.program_id(0)
    total = base_ref[0].astype(jnp.float32)
    for k, ref in enumerate(solved_refs):
        weight = pattern_ref[row, first + k].astype(jnp.float32)
        total = total - weight * dot(factor_ref[0, k], ref[...], NT)
    out_ref[0] = total


def trail(first, pattern, base, factor, solved, tile):
    count = len(solved)
    n_rows, height, width = base.shape
    depth = factor.shape[3]
    full = pl.BlockSpec((width, depth), lambda r, a: (0, 0))
    block = first // count
    return pl.pallas_call(
        lambda *refs: trail_kernel(first, *refs),
        grid=(n_rows, height // tile),
        in_specs=[
            pl.BlockSpec(memory_space=pltpu.SMEM),
            pl.BlockSpec((1, tile, width), lambda r, a: (r, a, 0)),
            pl.BlockSpec((1, count, tile, depth), lambda r, a: (r, block, a, 0)),
        ]
        + [full] * count,
        out_specs=pl.BlockSpec((1, tile, width), lambda r, a: (r, a, 0)),
        out_shape=jax.ShapeDtypeStruct(base.shape, jnp.float32),
        compiler_params=pltpu.CompilerParams(vmem_limit_bytes=VMEM_LIMIT),
        cost_estimate=pl.CostEstimate(
            flops=2 * n_rows * height * width * depth * count,
            bytes_accessed=2 * n_rows * height * depth * count,
            transcendentals=0,
        ),
        name="trail",
    )(pattern, base, factor, *solved)


def small_call(kernel, outs, *operands, name):
    return pl.pallas_call(
        kernel,
        out_shape=outs,
        in_specs=[pl.BlockSpec(memory_space=pltpu.VMEM)] * len(operands),
        out_specs=jax.tree.map(lambda _: pl.BlockSpec(memory_space=pltpu.VMEM), outs),
        compiler_params=pltpu.CompilerParams(vmem_limit_bytes=VMEM_LIMIT),
        cost_estimate=pl.CostEstimate(
            flops=2**28, bytes_accessed=2**21, transcendentals=0
        ),
        name=name,
    )(*operands)


def make(sizes):
    n_x, n_core, n_z, n_y = sizes
    n_col = n_z * n_y
    n_part = n_core * n_col

    def swap(value):
        return lax.ppermute(value, "core", [(i, n_core - 1 - i) for i in range(n_core)])

    def spread(value, axes, count):
        return lax.all_to_all(
            jnp.broadcast_to(value[None], (count, *value.shape)), axes, 0, 0
        )

    def parts_over_x(value):
        return [value] + [
            lax.ppermute(value, "x", [(i, (i + k) % n_x) for i in range(n_x)])
            for k in (1, n_x - 1, 2)
        ]

    def per_device(factor, pattern, rhs_trail, coupling, inverse, rhs):
        columns, height, width = rhs.shape
        share = width // n_part
        core = lax.axis_index("core")
        col = lax.axis_index("z") * n_y + lax.axis_index("y")

        def columns_of(which):
            at = (which * n_col + col) * share
            return lax.dynamic_slice(
                rhs, (0, 0, at), (columns, height, share)
            ).transpose(0, 2, 1)

        high = lax.reduce_precision(inverse, 8, 7)
        low = (inverse - high).astype(jnp.bfloat16)
        high = high.astype(jnp.bfloat16)
        across = coupling.transpose(0, 1, 3, 2)

        def pack(column):
            return [high[column], low[column]] + [across[column, i] for i in range(column)]

        mine_right = columns_of(core)
        other_right = columns_of(1 - core)
        inverse0 = spread(jnp.stack(pack(0)), ("z", "y"), n_col)
        group1 = spread(jnp.stack(pack(1)), ("z", "y"), n_col)
        group2 = spread(jnp.stack(pack(2) + pack(3)), ("z", "y"), n_col)
        rights = jnp.stack([mine_right, swap(other_right)], axis=1)
        block = n_col * inverse.shape[1]
        partial_shape = jax.ShapeDtypeStruct((share, block), jnp.float32)
        solved_shape = jax.ShapeDtypeStruct((share, block), jnp.bfloat16)

        both = small_call(
            first_kernel,
            jax.ShapeDtypeStruct((2 * share, block), jnp.float32),
            jnp.concatenate([mine_right[0], other_right[0]], axis=0),
            inverse0,
            name="first",
        )
        partial_sum = both[:share] + swap(both[share:])
        groups = {1: (group1, swap(group1), 0), 2: (group2, swap(group2), 0)}
        groups[3] = (*groups[2][:2], 4)
        pieces, whole = [], []
        for column in range(1, columns):
            mine, other, at = groups[column]
            parts = parts_over_x(partial_sum)
            solved, partial_sum = small_call(
                lambda *refs, c=column, a=at, n=len(parts): step_kernel(c, a, n, *refs),
                (solved_shape, partial_shape),
                *parts,
                rights[column],
                mine,
                other,
                *pieces,
                name="step",
            )
            pieces.append(solved)
            whole.append(spread(solved, ("core", "z", "y"), n_part).reshape(width, block))
        last = small_call(
            last_kernel, solved_shape, *parts_over_x(partial_sum), name="last"
        )
        base = trail(0, pattern, rhs_trail, factor, whole, 256)
        whole.append(spread(last, ("core", "z", "y"), n_part).reshape(width, block))
        updated = trail(3, pattern, base, factor, whole[3:], 512)
        own = block // n_col
        solved_blocks = jnp.stack(
            [lax.dynamic_slice(w, (0, col * own), (width, own)).T for w in whole]
        )
        return solved_blocks, updated

    return per_device


def solution(mesh):
    row, col = mesh.shape["row"], mesh.shape["col"]
    n_x, n_z = row // 2, 4
    n_y = col // n_z
    sizes = (n_x, 2, n_z, n_y)
    fine = Mesh(mesh.devices.reshape(sizes), ("x", "core", "z", "y"))
    r, c = ("x", "core"), ("z", "y")
    return jax.shard_map(
        make(sizes),
        mesh=fine,
        in_specs=(
            P(r + c, None, None, None),
            P(r + c, None),
            P(r + c, None, None),
            P(None, None, r, c),
            P(None, c, r),
            P(None, r, None),
        ),
        out_specs=(P(None, c, None), P(r + c, None, None)),
        check_vma=False,
    )
```

time: 560 us -> 204 us (0.36)
  waiting for transfers between devices: 397 us -> 87.7 us
  blocking collectives: 98.6 us -> 0 us
  starting transfers between devices: 0.28 us -> 57.3 us
  matrix products: 29.3 us -> 0 us
  Pallas kernels: 0 us -> 27.4 us
  between operations: 14.3 us -> 0.8 us
  local copies, waits for them, and re-layouts: 14.4 us -> 26.2 us
    psum x3 -> x0, waiting for transfers between devices: 246 us -> none  [per_device(): right_block = right_block - lax.psum(partial_value, 'col')]
    all_gather x4 -> x0, waiting for transfers between devices: 149 us -> none  [per_device(): whole_block = lax.all_gather(solved_piece, 'col', axis=0, tiled=True)]
    psum x4 -> x0, blocking collectives: 98.6 us -> none  [per_device(): solved_piece = lax.psum(own_part, 'row').astype(jnp.bfloat16)]
    all_to_all x0 -> x7, waiting for transfers between devices: none -> 69.8 us  [spread(): lax.all_to_all(jnp.broadcast_to(value[None], (count, *value.shape)), axes...]
    all_to_all x0 -> x7, starting transfers between devices: none -> 38.3 us  [spread(): lax.all_to_all(jnp.broadcast_to(value[None], (count, *value.shape)), axes...]
    dot_general x11 -> x0, matrix products: 29.3 us -> none  [the longest x1 14.8 us: per_device(): jnp.einsum('rjab,rjbn->ran', factor_trail, masked_all, preferred_element_...]
    pallas_call x0 -> x7, Pallas kernels: none -> 27.4 us  [the longest x2 19.1 us: trail(): pl.pallas_call(lambda *refs: trail_kernel(first, *refs), grid=(n_rows, he...]
    ppermute x0 -> x16, starting transfers between devices: none -> 19.1 us  [the longest x12 9.9 us: parts_over_x(): lax.ppermute(value, 'x', [(i, (i + k) % n_x) for i in range(n_x)])]
  transfers between devices with their start and end apart: 7 -> 23, of which waited for: 7 -> 16; matrix products, arithmetic and copies ran while one was open for 1% -> 4% of each run, Pallas kernels for 0% -> 11%
where the time goes in v1:
time: 204 us; the launch traced here: 202 us
  waiting for transfers between devices  87.7 us (43%)
  starting transfers between devices  57.3 us (28%)
  Pallas kernels  27.4 us (13%)
  local copies, waits for them, and re-layouts  26.2 us (13%)
  other arithmetic  2.62 us (1%)
    all_to_all x7, waiting for transfers between devices, spread(): lax.all_to_all(jnp.broadcast_to(value[None], (count, *value.shape)), axes...  69.8 us
    all_to_all x7, starting transfers between devices, spread(): lax.all_to_all(jnp.broadcast_to(value[None], (count, *value.shape)), axes...  38.3 us
    pallas_call x2, Pallas kernels, trail(): pl.pallas_call(lambda *refs: trail_kernel(first, *refs), grid=(n_rows, he...  19.1 us
    ppermute x12, waiting for transfers between devices, parts_over_x(): lax.ppermute(value, 'x', [(i, (i + k) % n_x) for i in range(n_x)])  17.1 us
    unnamed x29, local copies, waits for them, and re-layouts  11.6 us
    ppermute x12, starting transfers between devices, parts_over_x(): lax.ppermute(value, 'x', [(i, (i + k) % n_x) for i in range(n_x)])  9.9 us
    broadcast_in_dim x7, local copies, waits for them, and re-layouts, spread(): jnp.broadcast_to(value[None], (count, *value.shape))  9.21 us
    ppermute x4, starting transfers between devices, swap(): lax.ppermute(value, 'core', [(i, n_core - 1 - i) for i in range(n_core)])  9.18 us
  transfers between devices with their start and end apart: 23, of which 16 were waited for; matrix products, arithmetic and copies ran while one was open for 4% of the time, Pallas kernels for 11%

profile of v1, /device:TPU:1, one launch (start us, length us, event | category | flops | bytes accessed | tf_op | source)
XLA Modules:
  0.0 202.0 jit_solution(8449807367852590752)
XLA Ops:
  0.6 0.9 reduce-precision_convert_fusion
  1.6 0.7 constant_dynamic-update-slice_fusion.6
  2.3 0.7 constant_dynamic-update-slice_fusion.5
  3.1 0.7 constant_dynamic-update-slice_fusion.2
  3.8 0.7 constant_dynamic-update-slice_fusion.1
  4.5 0.7 constant_dynamic-update-slice_fusion
  5.2 2.0 broadcast_in_dim.17
  7.2 8.6 %all-to-all-start.3 = ((bf16[16,9,64,128]{3,2,1,0:T(8,128)(2,1)}), bf16[16,9,64,128]{3,2,1,0:T(8,128)(2,1)S(1)}, u32[]{:S(2)}, u32[]{:S(2)}) async-start(bf16[16,9,64,128]{3,2,1,0:T(8,128)(2,1)} %broadcast_in_dim.17), calls=%async_computation.3 | async-start | bytes 4718592 | tf_op jit(solution)/shard_map/all_to_all | solution.py:134
  15.8 0.7 slice_bitcast_fusion.5
  16.6 33.9 %all-to-all-done.3.refs_5_ = bf16[16,9,64,128]{3,2,1,0:T(8,128)(2,1)S(1)} async-done(((bf16[16,9,64,128]{3,2,1,0:T(8,128)(2,1)}), bf16[16,9,64,128]{3,2,1,0:T(8,128)(2,1)S(1)}, u32[]{:S(2)}, u32[]{:S(2)}) %all-to-all-start.3) | async-done | bytes 2359328 | tf_op jit(solution)/shard_map/all_to_all | solution.py:134
  50.5 1.1 broadcast_in_dim.15
  51.5 3.7 %all-to-all-start.1 = ((bf16[16,3,64,128]{3,2,1,0:T(8,128)(2,1)}), bf16[16,3,64,128]{3,2,1,0:T(8,128)(2,1)S(1)}, u32[]{:S(2)}, u32[]{:S(2)}) async-start(bf16[16,3,64,128]{3,2,1,0:T(8,128)(2,1)} %broadcast_in_dim.15), calls=%async_computation.1 | async-start | bytes 1572864 | tf_op jit(solution)/shard_map/all_to_all | solution.py:134
  55.2 2.0 %collective-permute-start.9 = (bf16[16,9,64,128]{3,2,1,0:T(8,128)(2,1)S(1)}, bf16[16,9,64,128]{3,2,1,0:T(8,128)(2,1)}, u32[]{:S(2)}, u32[]{:S(2)}) collective-permute-start(bf16[16,9,64,128]{3,2,1,0:T(8,128)(2,1)S(1)} %all-to-all-done.3.refs_5_), channel_id=1, source_target_pairs={{0,16},{16,0},{1,17},{17,1},{2,18},{18,2},{3,19},{19,3},{4,20},{20... | collective-permute-start | bytes 7077896 | tf_op jit(solution)/shard_map/ppermute | solution.py:131
  57.3 1.9 constant_dynamic-slice_fusion.1
  59.2 1.0 copy.12
  60.2 7.5 %all-to-all-done.1.refs_5_ = bf16[16,3,64,128]{3,2,1,0:T(8,128)(2,1)S(1)} async-done(((bf16[16,3,64,128]{3,2,1,0:T(8,128)(2,1)}), bf16[16,3,64,128]{3,2,1,0:T(8,128)(2,1)S(1)}, u32[]{:S(2)}, u32[]{:S(2)}) %all-to-all-start.1) | async-done | bytes 786464 | tf_op jit(solution)/shard_map/all_to_all | solution.py:134
  67.7 0.9 broadcast_in_dim.14
  68.6 4.2 %all-to-all-start = ((bf16[16,2,64,128]{3,2,1,0:T(8,128)(2,1)}), bf16[16,2,64,128]{3,2,1,0:T(8,128)(2,1)}, u32[]{:S(2)}, u32[]{:S(2)}) async-start(bf16[16,2,64,128]{3,2,1,0:T(8,128)(2,1)} %broadcast_in_dim.14), calls=%async_computation | async-start | bytes 1048576 | tf_op jit(solution)/shard_map/all_to_all | solution.py:134
  72.8 3.0 %collective-permute-start.5 = (bf16[16,3,64,128]{3,2,1,0:T(8,128)(2,1)S(1)}, bf16[16,3,64,128]{3,2,1,0:T(8,128)(2,1)}, u32[]{:S(2)}, u32[]{:S(2)}) collective-permute-start(bf16[16,3,64,128]{3,2,1,0:T(8,128)(2,1)S(1)} %all-to-all-done.1.refs_5_), channel_id=1, source_target_pairs={{0,16},{16,0},{1,17},{17,1},{2,18},{18,2},{3,19},{19,3},{4,20},{20... | collective-permute-start | bytes 2359304 | tf_op jit(solution)/shard_map/ppermute | solution.py:131
  75.9 5.9 %all-to-all-done.inverse_ref = bf16[16,2,64,128]{3,2,1,0:T(8,128)(2,1)} async-done(((bf16[16,2,64,128]{3,2,1,0:T(8,128)(2,1)}), bf16[16,2,64,128]{3,2,1,0:T(8,128)(2,1)}, u32[]{:S(2)}, u32[]{:S(2)}) %all-to-all-start) | async-done | bytes 524320 | tf_op jit(solution)/shard_map/all_to_all | solution.py:134
  81.8 1.4 first.1
  83.3 4.1 %collective-permute-start = (f32[16,1024]{1,0:T(8,128)S(1)}, f32[16,1024]{1,0:T(8,128)S(1)}, u32[]{:S(2)}, u32[]{:S(2)}) collective-permute-start(f32[16,1024]{1,0:T(8,128)S(1)} %slice.89), channel_id=1, source_target_pairs={{0,16},{16,0},{1,17},{17,1},{2,18},{18,2},{3,19},{19,3},{4,20},{20... | collective-permute-start | bytes 196616 | tf_op jit(solution)/shard_map/ppermute | solution.py:131
  87.5 0.8 collective-permute-done
  88.3 2.8 %collective-permute-start.3 = (f32[16,1024]{1,0:T(8,128)S(1)}, f32[16,1024]{1,0:T(8,128)S(1)}, u32[]{:S(2)}, u32[]{:S(2)}) collective-permute-start(f32[16,1024]{1,0:T(8,128)S(1)} %slice_add_fusion.refs_0_), channel_id=1, source_target_pairs={{0,64},{32,96},{64,0},{96,32},{1,65},{33,97},{65,1},{97,33},{2,66}... | collective-permute-start | bytes 196616 | tf_op jit(solution)/shard_map/ppermute | solution.py:140
  91.1 0.9 collective-permute-start.2
  92.0 0.6 collective-permute-start.1
  92.6 0.6 fusion.1
  93.2 1.4 collective-permute-done.2.refs_2_
  94.6 1.7 collective-permute-done.1.refs_1_
  96.3 1.9 step.3
  98.2 1.1 broadcast_in_dim.16
  99.3 5.7 %all-to-all-start.2 = ((bf16[32,16,1024]{2,1,0:T(8,128)(2,1)}), bf16[32,16,1024]{2,1,0:T(8,128)(2,1)S(1)}, u32[]{:S(2)}, u32[]{:S(2)}) async-start(bf16[32,16,1024]{2,1,0:T(8,128)(2,1)} %broadcast_in_dim.16), calls=%async_computation.2 | async-start | bytes 2097152 | tf_op jit(solution)/shard_map/all_to_all | solution.py:134
  105.3 1.6 collective-permute-start.7
  106.9 3.1 %collective-permute-done.8.refs_3_ = f32[16,1024]{1,0:T(8,128)S(1)} collective-permute-done((f32[16,1024]{1,0:T(8,128)S(1)}, f32[16,1024]{1,0:T(8,128)S(1)}, u32[]{:S(2)}, u32[]{:S(2)}) %collective-permute-start.8) | collective-permute-done | bytes 65568 | tf_op jit(solution)/shard_map/ppermute | solution.py:140
  110.1 1.5 collective-permute-done.6.refs_1_
  111.6 0.8 copy-done.3
  112.4 0.7 copy-done.4
  113.1 2.5 %step.4 = (bf16[16,1024]{1,0:T(8,128)(2,1)S(1)}, f32[16,1024]{1,0:T(8,128)S(1)}) custom-call(f32[16,1024]{1,0:T(8,128)S(1)} %copy-done.3, f32[16,1024]{1,0:T(8,128)S(1)} %collective-permute-done.6.refs_1_, f32[16,1024]{1,0:T(8,128)S(1)} %collective-permute-done.7.refs_2_, f32[16,1024]{1,0:T(8,128)S(1)} %collective-permute-done.8.refs_3_, ...), custom_call_target="tpu_custom_call" | custom-call | flops 268435456 | bytes 2097152 | tf_op jit(solution)/shard_map/step/pallas_call | solution.py:112
  115.6 6.0 %all-to-all-done.2 = bf16[32,16,1024]{2,1,0:T(8,128)(2,1)S(1)} async-done(((bf16[32,16,1024]{2,1,0:T(8,128)(2,1)}), bf16[32,16,1024]{2,1,0:T(8,128)(2,1)S(1)}, u32[]{:S(2)}, u32[]{:S(2)}) %all-to-all-start.2) | async-done | bytes 1048608 | tf_op jit(solution)/shard_map/all_to_all | solution.py:134
  121.6 1.1 broadcast_in_dim.18
  122.7 5.8 %all-to-all-start.4 = ((bf16[32,16,1024]{2,1,0:T(8,128)(2,1)}), bf16[32,16,1024]{2,1,0:T(8,128)(2,1)}, u32[]{:S(2)}, u32[]{:S(2)}) async-start(bf16[32,16,1024]{2,1,0:T(8,128)(2,1)} %broadcast_in_dim.18), calls=%async_computation.4 | async-start | bytes 2097152 | tf_op jit(solution)/shard_map/all_to_all | solution.py:134
  128.8 1.6 collective-permute-start.11
  130.4 3.2 %collective-permute-done.12.refs_3_ = f32[16,1024]{1,0:T(8,128)S(1)} collective-permute-done((f32[16,1024]{1,0:T(8,128)S(1)}, f32[16,1024]{1,0:T(8,128)S(1)}, u32[]{:S(2)}, u32[]{:S(2)}) %collective-permute-start.12) | collective-permute-done | bytes 65568 | tf_op jit(solution)/shard_map/ppermute | solution.py:140
  133.6 1.5 collective-permute-done.10.refs_1_
  135.1 2.6 %step.5 = (bf16[16,1024]{1,0:T(8,128)(2,1)S(1)}, f32[16,1024]{1,0:T(8,128)S(1)}) custom-call(f32[16,1024]{1,0:T(8,128)S(1)} %get-tuple-element.11.refs_0_, f32[16,1024]{1,0:T(8,128)S(1)} %collective-permute-done.10.refs_1_, f32[16,1024]{1,0:T(8,128)S(1)} %collective-permute-done.11.refs_2_, f32[16,1024]{1,0:T(8,128)S(1)} %collective-permute-done.12.refs_3_, ...), custom_call_target="tpu_custom_call" | custom-call | flops 268435456 | bytes 2097152 | tf_op jit(solution)/shard_map/step/pallas_call | solution.py:112
  137.7 0.6 copy-done.5
  138.3 0.6 copy-done.7
  138.9 6.2 %all-to-all-done.4 = bf16[32,16,1024]{2,1,0:T(8,128)(2,1)} async-done(((bf16[32,16,1024]{2,1,0:T(8,128)(2,1)}), bf16[32,16,1024]{2,1,0:T(8,128)(2,1)}, u32[]{:S(2)}, u32[]{:S(2)}) %all-to-all-start.4) | async-done | bytes 1048608 | tf_op jit(solution)/shard_map/all_to_all | solution.py:134
  145.2 1.9 broadcast_in_dim.19
  147.0 5.1 %all-to-all-start.5 = ((bf16[32,16,1024]{2,1,0:T(8,128)(2,1)}), bf16[32,16,1024]{2,1,0:T(8,128)(2,1)S(1)}, u32[]{:S(2)}, u32[]{:S(2)}) async-start(bf16[32,16,1024]{2,1,0:T(8,128)(2,1)} %broadcast_in_dim.19), calls=%async_computation.5 | async-start | bytes 2097152 | tf_op jit(solution)/shard_map/all_to_all | solution.py:134
  152.4 1.6 collective-permute-start.14
  154.1 3.1 %collective-permute-done.15.refs_3_ = f32[16,1024]{1,0:T(8,128)S(1)} collective-permute-done((f32[16,1024]{1,0:T(8,128)S(1)}, f32[16,1024]{1,0:T(8,128)S(1)}, u32[]{:S(2)}, u32[]{:S(2)}) %collective-permute-start.15) | collective-permute-done | bytes 65568 | tf_op jit(solution)/shard_map/ppermute | solution.py:140
  157.2 1.5 collective-permute-done.13.refs_1_
  158.7 10.0 %all-to-all-done.5 = bf16[32,16,1024]{2,1,0:T(8,128)(2,1)S(1)} async-done(((bf16[32,16,1024]{2,1,0:T(8,128)(2,1)}), bf16[32,16,1024]{2,1,0:T(8,128)(2,1)S(1)}, u32[]{:S(2)}, u32[]{:S(2)}) %all-to-all-start.5) | async-done | bytes 1048608 | tf_op jit(solution)/shard_map/all_to_all | solution.py:134
  168.7 1.1 broadcast_in_dim.20
  169.9 5.1 %all-to-all-start.6 = ((bf16[32,16,1024]{2,1,0:T(8,128)(2,1)}), bf16[32,16,1024]{2,1,0:T(8,128)(2,1)S(1)}, u32[]{:S(2)}, u32[]{:S(2)}) async-start(bf16[32,16,1024]{2,1,0:T(8,128)(2,1)} %broadcast_in_dim.20), calls=%async_computation.6 | async-start | bytes 2097152 | tf_op jit(solution)/shard_map/all_to_all | solution.py:134
  175.1 1.0 dynamic-slice_bitcast_fusion.2
  176.1 0.8 dynamic-slice_bitcast_fusion.1
  176.9 1.6 copy-done.1
  178.5 12.9 %trail.2.refs_1_ = f32[2,1024,512]{2,1,0:T(8,128)} custom-call(s32[2,4]{1,0:T(2,128)S(1)} %copy-done.6, bf16[2,1024,512]{2,1,0:T(8,128)(2,1)S(1)} %copy-done.1, bf16[2,4,1024,1024]{3,2,1,0:T(8,128)(2,1)} %refs_2_.3, bf16[512,1024]{1,0:T(8,128)(2,1)S(1)} %bitcast.61, bf16[512,1024]{1,0:T(8,128)(2,1)} %bitcast.19.refs_4_, bf16[512,1024]{1,0:T(8,128)(2,1)S(1)} %bitcast.63), custom_call_target="tpu_custom_call" | custom-call | flops 6442450944 | bytes 12582912 | tf_op jit(solution)/shard_map/trail/pallas_call | solution.py:90
  191.7 1.1 pad_maximum_fusion
  192.8 0.9 copy.11
  193.7 2.2 %copy-done = f32[2,1024,512]{2,1,0:T(8,128)S(1)} copy-done((f32[2,1024,512]{2,1,0:T(8,128)S(1)}, f32[2,1024,512]{2,1,0:T(8,128)}, u32[]{:S(2)}) %copy-start) | copy-done | bytes 4194328
  195.8 6.2 %trail.3 = f32[2,1024,512]{2,1,0:T(8,128)} custom-call(s32[2,4]{1,0:T(2,128)S(1)} %copy-done.6, f32[2,1024,512]{2,1,0:T(8,128)S(1)} %copy-done, bf16[2,4,1024,1024]{3,2,1,0:T(8,128)(2,1)} %refs_2_.3, bf16[512,1024]{1,0:T(8,128)(2,1)S(1)} %bitcast.65), custom_call_target="tpu_custom_call" | custom-call | flops 2147483648 | bytes 4194304 | tf_op jit(solution)/shard_map/trail/pallas_call | solution.py:90
  (42 shorter events, 1.4 us)
Async XLA Ops:
  7.2 43.2 %all-to-all-start.3 = ((bf16[16,9,64,128]{3,2,1,0:T(8,128)(2,1)}), bf16[16,9,64,128]{3,2,1,0:T(8,128)(2,1)S(1)}, u32[]{:S(2)}, u32[]{:S(2)}) async-start(bf16[16,9,64,128]{3,2,1,0:T(8,128)(2,1)} %broadcast_in_dim.17), calls=%async_computation.3 | async-start | bytes 4718592 | tf_op jit(solution)/shard_map/all_to_all | solution.py:134
  51.5 16.1 %all-to-all-start.1 = ((bf16[16,3,64,128]{3,2,1,0:T(8,128)(2,1)}), bf16[16,3,64,128]{3,2,1,0:T(8,128)(2,1)S(1)}, u32[]{:S(2)}, u32[]{:S(2)}) async-start(bf16[16,3,64,128]{3,2,1,0:T(8,128)(2,1)} %broadcast_in_dim.15), calls=%async_computation.1 | async-start | bytes 1572864 | tf_op jit(solution)/shard_map/all_to_all | solution.py:134
  55.2 56.3 %collective-permute-start.9 = (bf16[16,9,64,128]{3,2,1,0:T(8,128)(2,1)S(1)}, bf16[16,9,64,128]{3,2,1,0:T(8,128)(2,1)}, u32[]{:S(2)}, u32[]{:S(2)}) collective-permute-start(bf16[16,9,64,128]{3,2,1,0:T(8,128)(2,1)S(1)} %all-to-all-done.3.refs_5_), channel_id=1, source_target_pairs={{0,16},{16,0},{1,17},{17,1},{2,18},{18,2},{3,19},{19,3},{4,20},{20... | collective-permute-start | bytes 7077896 | tf_op jit(solution)/shard_map/ppermute | solution.py:131
  68.6 13.2 %all-to-all-start = ((bf16[16,2,64,128]{3,2,1,0:T(8,128)(2,1)}), bf16[16,2,64,128]{3,2,1,0:T(8,128)(2,1)}, u32[]{:S(2)}, u32[]{:S(2)}) async-start(bf16[16,2,64,128]{3,2,1,0:T(8,128)(2,1)} %broadcast_in_dim.14), calls=%async_computation | async-start | bytes 1048576 | tf_op jit(solution)/shard_map/all_to_all | solution.py:134
  72.8 23.4 %collective-permute-start.5 = (bf16[16,3,64,128]{3,2,1,0:T(8,128)(2,1)S(1)}, bf16[16,3,64,128]{3,2,1,0:T(8,128)(2,1)}, u32[]{:S(2)}, u32[]{:S(2)}) collective-permute-start(bf16[16,3,64,128]{3,2,1,0:T(8,128)(2,1)S(1)} %all-to-all-done.1.refs_5_), channel_id=1, source_target_pairs={{0,16},{16,0},{1,17},{17,1},{2,18},{18,2},{3,19},{19,3},{4,20},{20... | collective-permute-start | bytes 2359304 | tf_op jit(solution)/shard_map/ppermute | solution.py:131
  83.3 5.0 %collective-permute-start = (f32[16,1024]{1,0:T(8,128)S(1)}, f32[16,1024]{1,0:T(8,128)S(1)}, u32[]{:S(2)}, u32[]{:S(2)}) collective-permute-start(f32[16,1024]{1,0:T(8,128)S(1)} %slice.89), channel_id=1, source_target_pairs={{0,16},{16,0},{1,17},{17,1},{2,18},{18,2},{3,19},{19,3},{4,20},{20... | collective-permute-start | bytes 196616 | tf_op jit(solution)/shard_map/ppermute | solution.py:131
  87.4 4.6 %collective-permute-start.4 = (f32[4,16,128]{2,1,0:T(8,128)S(1)}, f32[4,16,128]{2,1,0:T(8,128)S(1)}, u32[]{:S(2)}, u32[]{:S(2)}) collective-permute-start(f32[4,16,128]{2,1,0:T(8,128)S(1)} %bitcast.69), channel_id=1, source_target_pairs={{0,16},{16,0},{1,17},{17,1},{2,18},{18,2},{3,19},{19,3},{4,20},{20... | collective-permute-start | bytes 98312 | tf_op jit(solution)/shard_map/ppermute | solution.py:131
  88.3 4.9 %collective-permute-start.3 = (f32[16,1024]{1,0:T(8,128)S(1)}, f32[16,1024]{1,0:T(8,128)S(1)}, u32[]{:S(2)}, u32[]{:S(2)}) collective-permute-start(f32[16,1024]{1,0:T(8,128)S(1)} %slice_add_fusion.refs_0_), channel_id=1, source_target_pairs={{0,64},{32,96},{64,0},{96,32},{1,65},{33,97},{65,1},{97,33},{2,66}... | collective-permute-start | bytes 196616 | tf_op jit(solution)/shard_map/ppermute | solution.py:140
  91.1 3.5 %collective-permute-start.2 = (f32[16,1024]{1,0:T(8,128)S(1)}, f32[16,1024]{1,0:T(8,128)S(1)}, u32[]{:S(2)}, u32[]{:S(2)}) collective-permute-start(f32[16,1024]{1,0:T(8,128)S(1)} %slice_add_fusion.refs_0_), channel_id=1, source_target_pairs={{0,96},{32,0},{64,32},{96,64},{1,97},{33,1},{65,33},{97,65},{2,98}... | collective-permute-start | bytes 196616 | tf_op jit(solution)/shard_map/ppermute | solution.py:140
  92.0 4.3 %collective-permute-start.1 = (f32[16,1024]{1,0:T(8,128)S(1)}, f32[16,1024]{1,0:T(8,128)S(1)}, u32[]{:S(2)}, u32[]{:S(2)}) collective-permute-start(f32[16,1024]{1,0:T(8,128)S(1)} %slice_add_fusion.refs_0_), channel_id=1, source_target_pairs={{0,32},{32,64},{64,96},{96,0},{1,33},{33,65},{65,97},{97,1},{2,34}... | collective-permute-start | bytes 196616 | tf_op jit(solution)/shard_map/ppermute | solution.py:140
  98.2 13.4 %copy-start.2 = (f32[16,1024]{1,0:T(8,128)}, f32[16,1024]{1,0:T(8,128)S(1)}, u32[]{:S(2)}) copy-start(f32[16,1024]{1,0:T(8,128)S(1)} %get-tuple-element.9.refs_0_) | copy-start | bytes 196612
  99.3 22.3 %all-to-all-start.2 = ((bf16[32,16,1024]{2,1,0:T(8,128)(2,1)}), bf16[32,16,1024]{2,1,0:T(8,128)(2,1)S(1)}, u32[]{:S(2)}, u32[]{:S(2)}) async-start(bf16[32,16,1024]{2,1,0:T(8,128)(2,1)} %broadcast_in_dim.16), calls=%async_computation.2 | async-start | bytes 2097152 | tf_op jit(solution)/shard_map/all_to_all | solution.py:134
  105.1 5.0 %collective-permute-start.8 = (f32[16,1024]{1,0:T(8,128)S(1)}, f32[16,1024]{1,0:T(8,128)S(1)}, u32[]{:S(2)}, u32[]{:S(2)}) collective-permute-start(f32[16,1024]{1,0:T(8,128)S(1)} %get-tuple-element.9.refs_0_), channel_id=1, source_target_pairs={{0,64},{32,96},{64,0},{96,32},{1,65},{33,97},{65,1},{97,33},{2,66}... | collective-permute-start | bytes 196616 | tf_op jit(solution)/shard_map/ppermute | solution.py:140
  105.3 4.8 %collective-permute-start.7 = (f32[16,1024]{1,0:T(8,128)S(1)}, f32[16,1024]{1,0:T(8,128)S(1)}, u32[]{:S(2)}, u32[]{:S(2)}) collective-permute-start(f32[16,1024]{1,0:T(8,128)S(1)} %get-tuple-element.9.refs_0_), channel_id=1, source_target_pairs={{0,96},{32,0},{64,32},{96,64},{1,97},{33,1},{65,33},{97,65},{2,98}... | collective-permute-start | bytes 196616 | tf_op jit(solution)/shard_map/ppermute | solution.py:140
  106.9 4.6 %collective-permute-start.6 = (f32[16,1024]{1,0:T(8,128)S(1)}, f32[16,1024]{1,0:T(8,128)S(1)}, u32[]{:S(2)}, u32[]{:S(2)}) collective-permute-start(f32[16,1024]{1,0:T(8,128)S(1)} %get-tuple-element.9.refs_0_), channel_id=1, source_target_pairs={{0,32},{32,64},{64,96},{96,0},{1,33},{33,65},{65,97},{97,1},{2,34}... | collective-permute-start | bytes 196616 | tf_op jit(solution)/shard_map/ppermute | solution.py:140
  111.5 0.8 copy-start.3
  112.4 0.7 copy-start.4
  122.7 22.4 %all-to-all-start.4 = ((bf16[32,16,1024]{2,1,0:T(8,128)(2,1)}), bf16[32,16,1024]{2,1,0:T(8,128)(2,1)}, u32[]{:S(2)}, u32[]{:S(2)}) async-start(bf16[32,16,1024]{2,1,0:T(8,128)(2,1)} %broadcast_in_dim.18), calls=%async_computation.4 | async-start | bytes 2097152 | tf_op jit(solution)/shard_map/all_to_all | solution.py:134
  128.5 5.1 %collective-permute-start.12 = (f32[16,1024]{1,0:T(8,128)S(1)}, f32[16,1024]{1,0:T(8,128)S(1)}, u32[]{:S(2)}, u32[]{:S(2)}) collective-permute-start(f32[16,1024]{1,0:T(8,128)S(1)} %get-tuple-element.11.refs_0_), channel_id=1, source_target_pairs={{0,64},{32,96},{64,0},{96,32},{1,65},{33,97},{65,1},{97,33},{2,66}... | collective-permute-start | bytes 196616 | tf_op jit(solution)/shard_map/ppermute | solution.py:140
  128.8 4.9 %collective-permute-start.11 = (f32[16,1024]{1,0:T(8,128)S(1)}, f32[16,1024]{1,0:T(8,128)S(1)}, u32[]{:S(2)}, u32[]{:S(2)}) collective-permute-start(f32[16,1024]{1,0:T(8,128)S(1)} %get-tuple-element.11.refs_0_), channel_id=1, source_target_pairs={{0,96},{32,0},{64,32},{96,64},{1,97},{33,1},{65,33},{97,65},{2,98}... | collective-permute-start | bytes 196616 | tf_op jit(solution)/shard_map/ppermute | solution.py:140
  130.4 4.7 %collective-permute-start.10 = (f32[16,1024]{1,0:T(8,128)S(1)}, f32[16,1024]{1,0:T(8,128)S(1)}, u32[]{:S(2)}, u32[]{:S(2)}) collective-permute-start(f32[16,1024]{1,0:T(8,128)S(1)} %get-tuple-element.11.refs_0_), channel_id=1, source_target_pairs={{0,32},{32,64},{64,96},{96,0},{1,33},{33,65},{65,97},{97,1},{2,34}... | collective-permute-start | bytes 196616 | tf_op jit(solution)/shard_map/ppermute | solution.py:140
  137.7 0.6 copy-start.5
  138.3 0.6 copy-start.7
  145.2 7.0 %copy-start.8 = (f32[16,1024]{1,0:T(8,128)S(1)}, f32[16,1024]{1,0:T(8,128)}, u32[]{:S(2)}) copy-start(f32[16,1024]{1,0:T(8,128)} %copy-done.7) | copy-start | bytes 196612
  147.0 21.7 %all-to-all-start.5 = ((bf16[32,16,1024]{2,1,0:T(8,128)(2,1)}), bf16[32,16,1024]{2,1,0:T(8,128)(2,1)S(1)}, u32[]{:S(2)}, u32[]{:S(2)}) async-start(bf16[32,16,1024]{2,1,0:T(8,128)(2,1)} %broadcast_in_dim.19), calls=%async_computation.5 | async-start | bytes 2097152 | tf_op jit(solution)/shard_map/all_to_all | solution.py:134
  152.2 24.7 %copy-start.6 = (s32[2,4]{1,0:T(2,128)S(1)}, s32[2,4]{1,0:T(2,128)}, u32[]{:S(2)}) copy-start(s32[2,4]{1,0:T(2,128)} %refs_0_.3) | copy-start | bytes 100
  152.2 5.0 %collective-permute-start.15 = (f32[16,1024]{1,0:T(8,128)S(1)}, f32[16,1024]{1,0:T(8,128)S(1)}, u32[]{:S(2)}, u32[]{:S(2)}) collective-permute-start(f32[16,1024]{1,0:T(8,128)S(1)} %copy-done.8), channel_id=1, source_target_pairs={{0,64},{32,96},{64,0},{96,32},{1,65},{33,97},{65,1},{97,33},{2,66}... | collective-permute-start | bytes 196616 | tf_op jit(solution)/shard_map/ppermute | solution.py:140
  152.4 4.8 %collective-permute-start.14 = (f32[16,1024]{1,0:T(8,128)S(1)}, f32[16,1024]{1,0:T(8,128)S(1)}, u32[]{:S(2)}, u32[]{:S(2)}) collective-permute-start(f32[16,1024]{1,0:T(8,128)S(1)} %copy-done.8), channel_id=1, source_target_pairs={{0,96},{32,0},{64,32},{96,64},{1,97},{33,1},{65,33},{97,65},{2,98}... | collective-permute-start | bytes 196616 | tf_op jit(solution)/shard_map/ppermute | solution.py:140
  154.1 4.6 %collective-permute-start.13 = (f32[16,1024]{1,0:T(8,128)S(1)}, f32[16,1024]{1,0:T(8,128)S(1)}, u32[]{:S(2)}, u32[]{:S(2)}) collective-permute-start(f32[16,1024]{1,0:T(8,128)S(1)} %copy-done.8), channel_id=1, source_target_pairs={{0,32},{32,64},{64,96},{96,0},{1,33},{33,65},{65,97},{97,1},{2,34}... | collective-permute-start | bytes 196616 | tf_op jit(solution)/shard_map/ppermute | solution.py:140
  169.9 21.7 %all-to-all-start.6 = ((bf16[32,16,1024]{2,1,0:T(8,128)(2,1)}), bf16[32,16,1024]{2,1,0:T(8,128)(2,1)S(1)}, u32[]{:S(2)}, u32[]{:S(2)}) async-start(bf16[32,16,1024]{2,1,0:T(8,128)(2,1)} %broadcast_in_dim.20), calls=%async_computation.6 | async-start | bytes 2097152 | tf_op jit(solution)/shard_map/all_to_all | solution.py:134
  176.9 1.6 copy-start.1
  193.7 2.2 %copy-start = (f32[2,1024,512]{2,1,0:T(8,128)S(1)}, f32[2,1024,512]{2,1,0:T(8,128)}, u32[]{:S(2)}) copy-start(f32[2,1024,512]{2,1,0:T(8,128)} %trail.2.refs_1_) | copy-start | bytes 12582916

commit v2 on v0

v2 whole, which is shorter than its diff:
```python
import jax
import jax.numpy as jnp
from jax import lax
from jax.experimental import pallas as pl
from jax.experimental.pallas import tpu as pltpu
from jax.sharding import Mesh
from jax.sharding import PartitionSpec as P

NT = (((1,), (1,)), ((), ()))
NN = (((1,), (0,)), ((), ()))
MIB = 1024 * 1024
EARLY = ((0, None), (1, None), (1, 0))
LATE = ((2, None), (2, 0), (2, 1), (3, None), (3, 0), (3, 1), (3, 2))


def dot(a, b, dims):
    return lax.dot_general(a, b, dims, preferred_element_type=jnp.float32)


def call(kernel, outs, *operands, name, scalars=0, scratch=(), after=(), limit=24):
    vmem = pl.BlockSpec(memory_space=pltpu.VMEM)
    smem = pl.BlockSpec(memory_space=pltpu.SMEM)
    unread = pl.BlockSpec(memory_space=pl.ANY)
    count = len(operands)
    return pl.pallas_call(
        lambda *refs: kernel(*refs[:count], *refs[count + len(after) :]),
        out_shape=outs,
        in_specs=[smem] * scalars + [vmem] * (count - scalars) + [unread] * len(after),
        out_specs=jax.tree.map(lambda _: vmem, outs),
        scratch_shapes=list(scratch),
        compiler_params=pltpu.CompilerParams(vmem_limit_bytes=limit * MIB),
        cost_estimate=pl.CostEstimate(
            flops=2**28, bytes_accessed=2**21, transcendentals=0
        ),
        name=name,
    )(*operands, *after)


def pack_kernel(members, place_ref, inverse_ref, coupling_ref, out_ref):
    copies = out_ref.shape[0]
    columns, rows, width = inverse_ref.shape
    depth = coupling_ref.shape[3]
    eye = (
        lax.broadcasted_iota(jnp.int32, (depth, depth), 0)
        == lax.broadcasted_iota(jnp.int32, (depth, depth), 1)
    ).astype(jnp.bfloat16)
    blocks = []
    lowest = min(column for column, earlier in members if earlier is not None)
    for column, earlier in members:
        if earlier is None:
            blocks.append(inverse_ref[column].astype(jnp.bfloat16))
        else:
            blocks.append(
                dot(eye, coupling_ref[column - lowest, earlier], NT).astype(jnp.bfloat16)
            )
    if members[0][0] == 0:
        first_row, first_lane = place_ref[0] * rows, place_ref[1] * width
        on_diagonal = (
            lax.broadcasted_iota(jnp.int32, (rows, width), 0) + first_row
            == lax.broadcasted_iota(jnp.int32, (rows, width), 1) + first_lane
        )
        at_row = lax.broadcasted_iota(jnp.int32, (16, width), 0)
        tile = jnp.zeros((16, width), jnp.float32)
        for column in range(columns):
            value = inverse_ref[column]
            rest = value - value.astype(jnp.bfloat16).astype(jnp.float32)
            line = jnp.sum(jnp.where(on_diagonal, rest, 0.0), axis=0, keepdims=True)
            tile = tile + jnp.where(at_row == column, line, 0.0)
        blocks.append(tile.astype(jnp.bfloat16))
    whole = jnp.concatenate(blocks, axis=0)
    for copy in range(copies):
        out_ref[copy] = whole


def pack(members, copies, place, inverse, coupling, after=()):
    count = len(members) * inverse.shape[1] + (16 if members[0][0] == 0 else 0)
    return call(
        lambda *refs: pack_kernel(members, *refs),
        jax.ShapeDtypeStruct((copies, count, inverse.shape[2]), jnp.bfloat16),
        place,
        inverse,
        coupling,
        scalars=1,
        after=after,
        name="pack",
    )


def block_of(ref, at, size):
    return ref[:, at : at + size].reshape(ref.shape[0] * size, ref.shape[2])


def rest_of(early_ref, column):
    tiles = early_ref[:, early_ref.shape[1] - 16 :].astype(jnp.float32)
    return jnp.sum(tiles, axis=0)[column : column + 1]


def apply_inverse(right, inverse, rest, slab, out_ref, add):
    count, width = right.shape
    high = right.astype(jnp.bfloat16)
    low = (right - high.astype(jnp.float32)).astype(jnp.bfloat16)
    both = dot(jnp.concatenate([high, low], axis=0), inverse, NT)
    value = both[:count] + both[count:]
    out_ref[...] = out_ref[...] + value if add else value
    lanes = pl.ds(pl.multiple_of(slab * width, width), width)
    out_ref[:, lanes] = out_ref[:, lanes] + right * rest


def first_kernel(size, place_ref, right_ref, early_ref, keep_ref, give_ref, mark_ref, out_ref):
    apply_inverse(
        right_ref[...],
        block_of(early_ref, 0, size),
        rest_of(early_ref, 0),
        place_ref[1],
        out_ref,
        False,
    )
    core = place_ref[2]
    count = keep_ref.shape[0]
    keep_ref[...] = out_ref[pl.ds(pl.multiple_of(core * count, count), count)]
    give_ref[...] = out_ref[pl.ds(pl.multiple_of((1 - core) * count, count), count)]
    mark_ref[...] = right_ref[: mark_ref.shape[0]]


def halves(solved_ref, core, keep_ref, give_ref):
    half = keep_ref.shape[1]
    keep_ref[...] = solved_ref[:, pl.ds(pl.multiple_of(core * half, half), half)]
    give_ref[...] = solved_ref[:, pl.ds(pl.multiple_of((1 - core) * half, half), half)]


def close_kernel(place_ref, *refs):
    part_refs, (solved_ref, keep_ref, give_ref, mark_ref) = refs[:-4], refs[-4:]
    total = part_refs[0][...]
    for part in part_refs[1:]:
        total = total + part[...]
    solved_ref[...] = total.astype(jnp.bfloat16)
    halves(solved_ref, place_ref[2], keep_ref, give_ref)
    mark_ref[...] = total[: mark_ref.shape[0], : mark_ref.shape[1]]


def step_kernel(column, at, size, place_ref, right_ref, *refs):
    early_refs, group_refs, solved_refs, out_ref = refs[:2], refs[2:4], refs[4:-1], refs[-1]
    slabs = (place_ref[1], place_ref[1] + 1 - 2 * place_ref[2])
    skip = 2 * size if column == 1 else size
    for side in range(2):
        right = right_ref[column, side]
        for i, block_ref in enumerate(solved_refs):
            right = right - dot(
                block_ref[...], block_of(group_refs[side], at + skip + i * size, size), NN
            )
        apply_inverse(
            right,
            block_of(group_refs[side], at + skip - size, size),
            rest_of(early_refs[side], column),
            slabs[side],
            out_ref,
            side > 0,
        )


def bundle_kernel(place_ref, *refs):
    core = place_ref[2]
    out_ref = refs[-1]
    for k in range(len(refs) // 2):
        keep, got = refs[2 * k][...], refs[2 * k + 1][...]
        for copy in range(out_ref.shape[0]):
            out_ref[copy, k, core] = keep
            out_ref[copy, k, 1 - core] = got


def trail_kernel(columns, pattern_ref, place_ref, base_ref, mine_ref, other_ref, *refs):
    count = len(columns)
    factor_refs, (out_ref, own_ref) = refs[:count], refs[count:]
    row = pl.program_id(0)
    core = place_ref[2]
    width, half = out_ref.shape[2], mine_ref.shape[4]
    offsets = [
        pl.multiple_of(core * half, half),
        pl.multiple_of((1 - core) * half, half),
    ]

    def solved(ref, k):
        return ref[:, k].reshape(width, half)

    total = base_ref[0].astype(jnp.float32)
    for k, column in enumerate(columns):
        product = None
        for ref, offset in zip((mine_ref, other_ref), offsets):
            factor = factor_refs[k][0, 0, :, pl.ds(offset, half)]
            term = dot(factor, solved(ref, k), NT)
            product = term if product is None else product + term
        total = total - pattern_ref[row, column].astype(jnp.float32) * product
    out_ref[0] = total

    @pl.when((row == 0) & (pl.program_id(1) == 0))
    def _():
        own = own_ref.shape[1]
        lane = lax.broadcasted_iota(jnp.int32, (own, half), 1)
        wanted = lax.broadcasted_iota(jnp.int32, (own, half), 0) + place_ref[0] * own
        for k in range(count):
            rows = None
            for ref, offset in zip((mine_ref, other_ref), offsets):
                pick = (lane + offset == wanted).astype(jnp.bfloat16)
                term = dot(pick, solved(ref, k), NT)
                rows = term if rows is None else rows + term
            own_ref[k] = rows.astype(jnp.bfloat16)


def trail(columns, pattern, place, base, factor, mine, other, own, tile):
    n_rows, height, width = base.shape
    depth = factor.shape[3]
    count = len(columns)

    def factor_spec(column):
        return pl.BlockSpec((1, 1, tile, depth), lambda r, a: (r, column, a, 0))

    smem = pl.BlockSpec(memory_space=pltpu.SMEM)
    vmem = pl.BlockSpec(memory_space=pltpu.VMEM)
    row_tile = pl.BlockSpec((1, tile, width), lambda r, a: (r, a, 0))
    return pl.pallas_call(
        lambda *refs: trail_kernel(columns, *refs),
        grid=(n_rows, height // tile),
        in_specs=[smem, smem, row_tile, vmem, vmem]
        + [factor_spec(column) for column in columns],
        out_specs=[
            row_tile,
            pl.BlockSpec((count, own, width), lambda r, a: (0, 0, 0)),
        ],
        out_shape=[
            jax.ShapeDtypeStruct(base.shape, jnp.float32),
            jax.ShapeDtypeStruct((count, own, width), jnp.bfloat16),
        ],
        compiler_params=pltpu.CompilerParams(vmem_limit_bytes=40 * MIB),
        cost_estimate=pl.CostEstimate(
            flops=2 * n_rows * height * width * depth * count,
            bytes_accessed=2 * n_rows * height * depth * count,
            transcendentals=0,
        ),
        name="trail",
    )(pattern, place, base, mine, other, *([factor] * count))


def make(sizes):
    n_x, n_core, n_z, n_y = sizes
    n_col = n_z * n_y

    def swap(value):
        return lax.ppermute(value, "core", [(i, n_core - 1 - i) for i in range(n_core)])

    def exchange(value):
        return lax.all_to_all(value, ("z", "y"), 0, 0)

    def parts_over_x(value):
        return [value] + [
            lax.ppermute(value, "x", [(i, (i + k) % n_x) for i in range(n_x)])
            for k in (1, n_x - 1, 2)
        ]

    def per_device(factor, pattern, rhs_trail, coupling, inverse, rhs):
        columns, height, width = rhs.shape
        share = width // (n_core * n_col)
        size = inverse.shape[1]
        block = n_col * size
        core = lax.axis_index("core")
        col = lax.axis_index("z") * n_y + lax.axis_index("y")
        place = jnp.stack([col, lax.axis_index("x") * n_core + core, core])

        tied = lax.optimization_barrier
        packed = pack(EARLY, n_col, place, inverse, coupling[1:2, 0:1])
        early = exchange(packed)
        packed_late = pack(LATE, n_col, place, inverse, coupling[2:], after=[packed])
        right = lax.dynamic_slice(
            rhs, (0, 0, col * n_core * share), (columns, height, n_core * share)
        ).transpose(0, 2, 1)
        rights = [
            lax.dynamic_slice(right, (0, which * share, 0), (columns, share, height))
            for which in (core, 1 - core)
        ]
        rights = jnp.stack([rights[0], swap(rights[1])], axis=1)

        partial_shape = jax.ShapeDtypeStruct((share, block), jnp.float32)
        solved_shape = jax.ShapeDtypeStruct((share, block), jnp.bfloat16)
        half_shape = jax.ShapeDtypeStruct((share, block // n_core), jnp.bfloat16)
        mark_shape = jax.ShapeDtypeStruct((8, 128), jnp.float32)
        early_both = (early, swap(early))
        keep, give, mark = call(
            lambda *refs: first_kernel(size, *refs),
            (partial_shape, partial_shape, mark_shape),
            place,
            right[0],
            early,
            scalars=1,
            scratch=[pltpu.VMEM((n_core * share, block), jnp.float32)],
            after=[rights, packed_late],
            name="first",
        )
        packed_late, mark = tied((packed_late, mark))
        late = exchange(packed_late)
        late_both = None
        partial_sum = keep + swap(give)
        pieces, sent = [], []
        for column in range(1, columns + 1):
            solved, keep, give, mark = call(
                close_kernel,
                (solved_shape, half_shape, half_shape, mark_shape),
                place,
                *parts_over_x(partial_sum),
                scalars=1,
                after=[mark],
                name="close",
            )
            pieces.append(solved)
            sent += [keep, swap(give)]
            if column == columns:
                break
            if column == 2:
                late, mark = tied((late, mark))
                late_both = (late, swap(late))
            group, at = (
                (early_both, 0),
                (late_both, 0),
                (late_both, 3 * size),
            )[column - 1]
            partial_sum = call(
                lambda *refs, c=column, a=at: step_kernel(c, a, size, *refs),
                partial_shape,
                place,
                rights,
                *early_both,
                *group,
                *pieces,
                scalars=1,
                after=[mark],
                name="step",
            )

        def send(halves_of, after):
            shape = (n_col, len(halves_of) // 2, n_core, share, block // n_core)
            return exchange(
                call(
                    bundle_kernel,
                    jax.ShapeDtypeStruct(shape, jnp.bfloat16),
                    place,
                    *halves_of,
                    scalars=1,
                    after=after,
                    name="bundle",
                )
            )

        first_pair, mark = tied((send(sent[:4], []), mark))
        second_pair = send(sent[4:], [mark])
        base, blocks01 = trail(
            (0, 1), pattern, place, rhs_trail, factor, first_pair, swap(first_pair), size, 512
        )
        second_pair, blocks01 = tied((second_pair, blocks01))
        updated, blocks23 = trail(
            (2, 3), pattern, place, base, factor, second_pair, swap(second_pair), size, 512
        )
        return jnp.concatenate([blocks01, blocks23]), updated

    return per_device


def solution(mesh):
    row, col = mesh.shape["row"], mesh.shape["col"]
    sizes = (row // 2, 2, 4, col // 4)
    fine = Mesh(mesh.devices.reshape(sizes), ("x", "core", "z", "y"))
    r, c = ("x", "core"), ("z", "y")
    return jax.shard_map(
        make(sizes),
        mesh=fine,
        in_specs=(
            P(r + c, None, None, None),
            P(r + c, None),
            P(r + c, None, None),
            P(None, None, r, c),
            P(None, c, r),
            P(None, r, None),
        ),
        out_specs=(P(None, c, None), P(r + c, None, None)),
        check_vma=False,
    )
```

time: 560 us -> 145 us (0.26)
  waiting for transfers between devices: 397 us -> 43.6 us
  blocking collectives: 98.6 us -> 0 us
  starting transfers between devices: 0.28 us -> 47.5 us
  Pallas kernels: 0 us -> 31.1 us
  matrix products: 29.3 us -> 0 us
  between operations: 14.3 us -> 1.04 us
    psum x3 -> x0, waiting for transfers between devices: 246 us -> none  [per_device(): right_block = right_block - lax.psum(partial_value, 'col')]
    all_gather x4 -> x0, waiting for transfers between devices: 149 us -> none  [per_device(): whole_block = lax.all_gather(solved_piece, 'col', axis=0, tiled=True)]
    psum x4 -> x0, blocking collectives: 98.6 us -> none  [per_device(): solved_piece = lax.psum(own_part, 'row').astype(jnp.bfloat16)]
    pallas_call x0 -> x14, Pallas kernels: none -> 31.1 us  [the longest x2 17.6 us: trail(): pl.pallas_call(lambda *refs: trail_kernel(columns, *refs), grid=(n_rows,...]
    dot_general x11 -> x0, matrix products: 29.3 us -> none  [the longest x1 14.8 us: per_device(): jnp.einsum('rjab,rjbn->ran', factor_trail, masked_all, preferred_element_...]
    ppermute x0 -> x22, waiting for transfers between devices: none -> 28 us  [the longest x12 18.4 us: parts_over_x(): lax.ppermute(value, 'x', [(i, (i + k) % n_x) for i in range(n_x)])]
    all_to_all x0 -> x4, starting transfers between devices: none -> 26.2 us  [exchange(): return lax.all_to_all(value, ('z', 'y'), 0, 0)]
    ppermute x0 -> x22, starting transfers between devices: none -> 21.3 us  [the longest x10 11.3 us: swap(): lax.ppermute(value, 'core', [(i, n_core - 1 - i) for i in range(n_core)])]
  transfers between devices with their start and end apart: 7 -> 26, of which waited for: 7 -> 16; matrix products, arithmetic and copies ran while one was open for 1% -> 1% of each run, Pallas kernels for 0% -> 13%
where the time goes in v2:
time: 145 us; the launch traced here: 144 us
  starting transfers between devices  47.5 us (33%)
  waiting for transfers between devices  43.6 us (30%)
  Pallas kernels  31.1 us (21%)
  local copies, waits for them, and re-layouts  18.9 us (13%)
  other arithmetic  1.66 us (1%)
    all_to_all x4, starting transfers between devices, exchange(): return lax.all_to_all(value, ('z', 'y'), 0, 0)  26.2 us
    ppermute x12, waiting for transfers between devices, parts_over_x(): lax.ppermute(value, 'x', [(i, (i + k) % n_x) for i in range(n_x)])  18.4 us
    unnamed x59, local copies, waits for them, and re-layouts  17.8 us
    pallas_call x2, Pallas kernels, trail(): pl.pallas_call(lambda *refs: trail_kernel(columns, *refs), grid=(n_rows,...  17.6 us
    all_to_all x4, waiting for transfers between devices, exchange(): return lax.all_to_all(value, ('z', 'y'), 0, 0)  15.6 us
    pallas_call x12, Pallas kernels, call(): pl.pallas_call(lambda *refs: kernel(*refs[:count], *refs[count + len(afte...  13.6 us
    ppermute x10, starting transfers between devices, swap(): lax.ppermute(value, 'core', [(i, n_core - 1 - i) for i in range(n_core)])  11.3 us
    ppermute x12, starting transfers between devices, parts_over_x(): lax.ppermute(value, 'x', [(i, (i + k) % n_x) for i in range(n_x)])  10 us
  transfers between devices with their start and end apart: 26, of which 16 were waited for; matrix products, arithmetic and copies ran while one was open for 1% of the time, Pallas kernels for 13%

profile of v2, /device:TPU:1, one launch (start us, length us, event | category | flops | bytes accessed | tf_op | source)
XLA Modules:
  0.0 143.9 jit_solution(9098487824328201596)
XLA Ops:
  0.6 0.7 slice.9
  1.6 0.9 copy-done.8
  2.5 1.6 %pack.2.refs_3_ = bf16[16,208,128]{2,1,0:T(8,128)(2,1)} custom-call(s32[3]{0:T(128)S(1)} %pad_add_fusion.refs_0_.refs_1_, f32[4,64,128]{2,1,0:T(8,128)S(1)} %copy-done.8, bf16[1,1,128,64]{3,2,1,0:T(8,128)(2,1)S(1)} %copy.15.refs_2_), custom_call_target="tpu_custom_call" | custom-call | flops 268435456 | bytes 2097152 | tf_op jit(solution)/shard_map/pack/pallas_call | solution.py:25
  4.1 8.7 %all-to-all-start = ((bf16[16,208,128]{2,1,0:T(8,128)(2,1)}), bf16[16,208,128]{2,1,0:T(8,128)(2,1)S(1)}, u32[]{:S(2)}, u32[]{:S(2)}) async-start(bf16[16,208,128]{2,1,0:T(8,128)(2,1)} %pack.2.refs_3_), calls=%async_computation | async-start | bytes 1703936 | tf_op jit(solution)/shard_map/all_to_all | solution.py:251
  13.2 1.0 collective-permute-start
  14.8 0.8 pack.3.refs_4_
  15.6 11.1 %all-to-all-done.refs_2_.refs_4_ = bf16[16,208,128]{2,1,0:T(8,128)(2,1)S(1)} async-done(((bf16[16,208,128]{2,1,0:T(8,128)(2,1)}), bf16[16,208,128]{2,1,0:T(8,128)(2,1)S(1)}, u32[]{:S(2)}, u32[]{:S(2)}) %all-to-all-start) | async-done | bytes 852000 | tf_op jit(solution)/shard_map/all_to_all | solution.py:251
  26.7 0.8 first.1
  27.5 0.6 copy-done.14
  28.1 0.6 copy-done.22
  28.8 3.8 %all-to-all-start.1 = ((bf16[16,448,128]{2,1,0:T(8,128)(2,1)}), bf16[16,448,128]{2,1,0:T(8,128)(2,1)S(1)}, u32[]{:S(2)}, u32[]{:S(2)}) async-start(bf16[16,448,128]{2,1,0:T(8,128)(2,1)} %copy-done), calls=%async_computation.1 | async-start | bytes 3670016 | tf_op jit(solution)/shard_map/all_to_all | solution.py:251
  32.6 2.4 %collective-permute-start.1 = (bf16[16,208,128]{2,1,0:T(8,128)(2,1)S(1)}, bf16[16,208,128]{2,1,0:T(8,128)(2,1)S(1)}, u32[]{:S(2)}, u32[]{:S(2)}) collective-permute-start(bf16[16,208,128]{2,1,0:T(8,128)(2,1)S(1)} %all-to-all-done.refs_2_.refs_4_), channel_id=1, source_target_pairs={{0,16},{16,0},{1,17},{17,1},{2,18},{18,2},{3,19},{19,3},{4,20},{20... | collective-permute-start | bytes 2555912 | tf_op jit(solution)/shard_map/ppermute | solution.py:248
  35.0 2.1 %collective-permute-done.2 = f32[16,1024]{1,0:T(8,128)S(1)} collective-permute-done((f32[16,1024]{1,0:T(8,128)}, f32[16,1024]{1,0:T(8,128)S(1)}, u32[]{:S(2)}, u32[]{:S(2)}) %collective-permute-start.2) | collective-permute-done | bytes 65568 | tf_op jit(solution)/shard_map/ppermute | solution.py:248
  37.1 0.9 add.29.refs_1_
  38.0 2.7 %collective-permute-start.5 = (f32[16,1024]{1,0:T(8,128)S(1)}, f32[16,1024]{1,0:T(8,128)S(1)}, u32[]{:S(2)}, u32[]{:S(2)}) collective-permute-start(f32[16,1024]{1,0:T(8,128)S(1)} %add.29.refs_1_), channel_id=1, source_target_pairs={{0,64},{32,96},{64,0},{96,32},{1,65},{33,97},{65,1},{97,33},{2,66}... | collective-permute-start | bytes 196616 | tf_op jit(solution)/shard_map/ppermute | solution.py:255
  40.7 0.9 collective-permute-start.4
  41.6 0.6 collective-permute-start.3
  42.2 0.7 collective-permute-done.5.refs_4_
  42.9 1.6 %collective-permute-done.4.refs_3_ = f32[16,1024]{1,0:T(8,128)S(1)} collective-permute-done((f32[16,1024]{1,0:T(8,128)S(1)}, f32[16,1024]{1,0:T(8,128)S(1)}, u32[]{:S(2)}, u32[]{:S(2)}) %collective-permute-start.4) | collective-permute-done | bytes 65568 | tf_op jit(solution)/shard_map/ppermute | solution.py:255
  44.4 1.8 %collective-permute-done.3.refs_2_ = f32[16,1024]{1,0:T(8,128)S(1)} collective-permute-done((f32[16,1024]{1,0:T(8,128)S(1)}, f32[16,1024]{1,0:T(8,128)S(1)}, u32[]{:S(2)}, u32[]{:S(2)}) %collective-permute-start.3) | collective-permute-done | bytes 65568 | tf_op jit(solution)/shard_map/ppermute | solution.py:255
  46.8 0.8 copy-done.6
  47.6 1.0 step.3.refs_1_
  48.7 1.1 collective-permute-start.8
  49.7 1.1 collective-permute-start.7
  51.2 2.5 %collective-permute-done.8.refs_4_ = f32[16,1024]{1,0:T(8,128)S(1)} collective-permute-done((f32[16,1024]{1,0:T(8,128)S(1)}, f32[16,1024]{1,0:T(8,128)S(1)}, u32[]{:S(2)}, u32[]{:S(2)}) %collective-permute-start.8) | collective-permute-done | bytes 65568 | tf_op jit(solution)/shard_map/ppermute | solution.py:255
  53.7 2.2 %collective-permute-done.6.refs_2_ = f32[16,1024]{1,0:T(8,128)S(1)} collective-permute-done((f32[16,1024]{1,0:T(8,128)S(1)}, f32[16,1024]{1,0:T(8,128)S(1)}, u32[]{:S(2)}, u32[]{:S(2)}) %collective-permute-start.6) | collective-permute-done | bytes 65568 | tf_op jit(solution)/shard_map/ppermute | solution.py:255
  56.5 0.6 copy-done.12
  57.1 0.6 copy-done.19
  57.6 0.6 copy-done.25
  58.2 2.5 %collective-permute-start.9 = (bf16[16,448,128]{2,1,0:T(8,128)(2,1)S(1)}, bf16[16,448,128]{2,1,0:T(8,128)(2,1)}, u32[]{:S(2)}, u32[]{:S(2)}) collective-permute-start(bf16[16,448,128]{2,1,0:T(8,128)(2,1)S(1)} %all-to-all-done.1.refs_4_), channel_id=1, source_target_pairs={{0,16},{16,0},{1,17},{17,1},{2,18},{18,2},{3,19},{19,3},{4,20},{20... | collective-permute-start | bytes 5505032 | tf_op jit(solution)/shard_map/ppermute | solution.py:248
  61.2 3.0 %collective-permute-done.18.refs_2_ = bf16[16,512]{1,0:T(8,128)(2,1)S(1)} collective-permute-done((bf16[16,512]{1,0:T(8,128)(2,1)}, bf16[16,512]{1,0:T(8,128)(2,1)S(1)}, u32[]{:S(2)}, u32[]{:S(2)}) %collective-permute-start.18) | collective-permute-done | bytes 16416 | tf_op jit(solution)/shard_map/ppermute | solution.py:248
  64.4 0.7 copy-done.18
  65.1 0.7 copy-done.20
  65.8 0.6 bundle.2
  66.4 1.0 copy-done.3
  67.4 6.8 %all-to-all-start.2 = ((bf16[16,2,2,16,512]{4,3,2,1,0:T(8,128)(2,1)}), bf16[16,2,2,16,512]{4,3,2,1,0:T(8,128)(2,1)}, u32[]{:S(2)}, u32[]{:S(2)}) async-start(bf16[16,2,2,16,512]{4,3,2,1,0:T(8,128)(2,1)} %copy-done.3), calls=%async_computation.2 | async-start | bytes 2097152 | tf_op jit(solution)/shard_map/all_to_all | solution.py:251
  74.2 0.8 copy-done.7
  75.1 0.8 copy-done.11
  75.8 0.8 copy-done.13
  76.6 2.1 %step.4.refs_1_ = f32[16,1024]{1,0:T(8,128)S(1)} custom-call(s32[3]{0:T(128)S(1)} %pad_add_fusion.refs_0_.refs_1_, f32[4,2,16,128]{3,2,1,0:T(8,128)S(1)} %copy-done.7, bf16[16,208,128]{2,1,0:T(8,128)(2,1)S(1)} %all-to-all-done.refs_2_.refs_4_, bf16[16,208,128]{2,1,0:T(8,128)(2,1)S(1)} %collective-permute-done.1.refs_3_.refs_5_, ...), custom_call_target="tpu_custom_call" | custom-call | flops 268435456 | bytes 2097152 | tf_op jit(solution)/shard_map/step/pallas_call | solution.py:25
  78.7 1.1 collective-permute-start.11
  80.3 3.5 %collective-permute-done.12.refs_4_ = f32[16,1024]{1,0:T(8,128)S(1)} collective-permute-done((f32[16,1024]{1,0:T(8,128)S(1)}, f32[16,1024]{1,0:T(8,128)S(1)}, u32[]{:S(2)}, u32[]{:S(2)}) %collective-permute-start.12) | collective-permute-done | bytes 65568 | tf_op jit(solution)/shard_map/ppermute | solution.py:255
  83.8 1.5 %collective-permute-done.10.refs_2_ = f32[16,1024]{1,0:T(8,128)S(1)} collective-permute-done((f32[16,1024]{1,0:T(8,128)S(1)}, f32[16,1024]{1,0:T(8,128)S(1)}, u32[]{:S(2)}, u32[]{:S(2)}) %collective-permute-start.10) | collective-permute-done | bytes 65568 | tf_op jit(solution)/shard_map/ppermute | solution.py:255
  85.8 0.6 copy-done.15
  86.4 0.6 copy-done.23
  87.0 2.1 %step.5.refs_1_ = f32[16,1024]{1,0:T(8,128)S(1)} custom-call(s32[3]{0:T(128)S(1)} %pad_add_fusion.refs_0_.refs_1_, f32[4,2,16,128]{3,2,1,0:T(8,128)S(1)} %copy-done.7, bf16[16,208,128]{2,1,0:T(8,128)(2,1)S(1)} %all-to-all-done.refs_2_.refs_4_, bf16[16,208,128]{2,1,0:T(8,128)(2,1)S(1)} %collective-permute-done.1.refs_3_.refs_5_, ...), custom_call_target="tpu_custom_call" | custom-call | flops 268435456 | bytes 2097152 | tf_op jit(solution)/shard_map/step/pallas_call | solution.py:25
  89.3 1.5 %collective-permute-start.15 = (f32[16,1024]{1,0:T(8,128)S(1)}, f32[16,1024]{1,0:T(8,128)S(1)}, u32[]{:S(2)}, u32[]{:S(2)}) collective-permute-start(f32[16,1024]{1,0:T(8,128)S(1)} %step.5.refs_1_), channel_id=1, source_target_pairs={{0,96},{32,0},{64,32},{96,64},{1,97},{33,1},{65,33},{97,65},{2,98}... | collective-permute-start | bytes 196616 | tf_op jit(solution)/shard_map/ppermute | solution.py:255
  90.8 3.0 %collective-permute-done.16.refs_4_ = f32[16,1024]{1,0:T(8,128)S(1)} collective-permute-done((f32[16,1024]{1,0:T(8,128)S(1)}, f32[16,1024]{1,0:T(8,128)S(1)}, u32[]{:S(2)}, u32[]{:S(2)}) %collective-permute-start.16) | collective-permute-done | bytes 65568 | tf_op jit(solution)/shard_map/ppermute | solution.py:255
  93.9 1.8 %collective-permute-done.14.refs_2_ = f32[16,1024]{1,0:T(8,128)S(1)} collective-permute-done((f32[16,1024]{1,0:T(8,128)S(1)}, f32[16,1024]{1,0:T(8,128)S(1)}, u32[]{:S(2)}, u32[]{:S(2)}) %collective-permute-start.14) | collective-permute-done | bytes 65568 | tf_op jit(solution)/shard_map/ppermute | solution.py:255
  95.7 1.2 close.7
  96.8 2.3 %collective-permute-start.20 = (bf16[16,2,2,16,512]{4,3,2,1,0:T(8,128)(2,1)}, bf16[16,2,2,16,512]{4,3,2,1,0:T(8,128)(2,1)S(1)}, u32[]{:S(2)}, u32[]{:S(2)}) collective-permute-start(bf16[16,2,2,16,512]{4,3,2,1,0:T(8,128)(2,1)} %all-to-all-done.2.refs_3_), channel_id=1, source_target_pairs={{0,16},{16,0},{1,17},{17,1},{2,18},{18,2},{3,19},{19,3},{4,20},{20... | collective-permute-start | bytes 3145736 | tf_op jit(solution)/shard_map/ppermute | solution.py:248
  99.6 2.0 %collective-permute-done.13.refs_2_ = bf16[16,512]{1,0:T(8,128)(2,1)S(1)} collective-permute-done((bf16[16,512]{1,0:T(8,128)(2,1)}, bf16[16,512]{1,0:T(8,128)(2,1)S(1)}, u32[]{:S(2)}, u32[]{:S(2)}) %collective-permute-start.13) | collective-permute-done | bytes 16416 | tf_op jit(solution)/shard_map/ppermute | solution.py:248
  101.6 0.7 copy-done.16
  102.4 1.6 %bundle.3 = bf16[16,2,2,16,512]{4,3,2,1,0:T(8,128)(2,1)} custom-call(s32[3]{0:T(128)S(1)} %pad_add_fusion.refs_0_.refs_1_, bf16[16,512]{1,0:T(8,128)(2,1)S(1)} %copy-done.16, bf16[16,512]{1,0:T(8,128)(2,1)S(1)} %collective-permute-done.13.refs_2_, bf16[16,512]{1,0:T(8,128)(2,1)S(1)} %get-tuple-element.47.refs_3_, ...), custom_call_target="tpu_custom_call" | custom-call | flops 268435456 | bytes 2097152 | tf_op jit(solution)/shard_map/bundle/pallas_call | solution.py:25
  104.0 6.9 %all-to-all-start.3 = ((bf16[16,2,2,16,512]{4,3,2,1,0:T(8,128)(2,1)}), bf16[16,2,2,16,512]{4,3,2,1,0:T(8,128)(2,1)S(1)}, u32[]{:S(2)}, u32[]{:S(2)}) async-start(bf16[16,2,2,16,512]{4,3,2,1,0:T(8,128)(2,1)} %bundle.3), calls=%async_computation.3 | async-start | bytes 2097152 | tf_op jit(solution)/shard_map/all_to_all | solution.py:251
  110.9 1.6 %copy-done.4 = bf16[2,1024,512]{2,1,0:T(8,128)(2,1)S(1)} copy-done((bf16[2,1024,512]{2,1,0:T(8,128)(2,1)S(1)}, bf16[2,1024,512]{2,1,0:T(8,128)(2,1)}, u32[]{:S(2)}) %copy-start.4) | copy-done | bytes 2097176
  112.5 8.2 %trail.2 = (f32[2,1024,512]{2,1,0:T(8,128)S(1)}, bf16[2,64,512]{2,1,0:T(8,128)(2,1)S(1)}) custom-call(s32[2,4]{1,0:T(2,128)S(1)} %copy-done.21, s32[3]{0:T(128)S(1)} %pad_add_fusion.refs_0_.refs_1_, bf16[2,1024,512]{2,1,0:T(8,128)(2,1)S(1)} %copy-done.4, bf16[16,2,2,16,512]{4,3,2,1,0:T(8,128)(2,1)} %all-to-all-done.2.refs_3_, ...), custom_call_target="tpu_custom_call" | custom-call | flops 4294967296 | bytes 8388608 | tf_op jit(solution)/shard_map/trail/pallas_call | solution.py:220
  120.8 2.0 %copy-done.1 = f32[2,1024,512]{2,1,0:T(8,128)} copy-done((f32[2,1024,512]{2,1,0:T(8,128)}, f32[2,1024,512]{2,1,0:T(8,128)S(1)}, u32[]{:S(2)}) %copy-start.1) | copy-done | bytes 4194328
  122.8 4.5 %all-to-all-done.3.refs_3_ = bf16[16,2,2,16,512]{4,3,2,1,0:T(8,128)(2,1)S(1)} async-done(((bf16[16,2,2,16,512]{4,3,2,1,0:T(8,128)(2,1)}), bf16[16,2,2,16,512]{4,3,2,1,0:T(8,128)(2,1)S(1)}, u32[]{:S(2)}, u32[]{:S(2)}) %all-to-all-start.3) | async-done | bytes 1048608 | tf_op jit(solution)/shard_map/all_to_all | solution.py:251
  127.2 2.1 %collective-permute-start.21 = (bf16[16,2,2,16,512]{4,3,2,1,0:T(8,128)(2,1)S(1)}, bf16[16,2,2,16,512]{4,3,2,1,0:T(8,128)(2,1)S(1)}, u32[]{:S(2)}, u32[]{:S(2)}) collective-permute-start(bf16[16,2,2,16,512]{4,3,2,1,0:T(8,128)(2,1)S(1)} %all-to-all-done.3.refs_3_), channel_id=1, source_target_pairs={{0,16},{16,0},{1,17},{17,1},{2,18},{18,2},{3,19},{19,3},{4,20},{20... | collective-permute-start | bytes 3145736 | tf_op jit(solution)/shard_map/ppermute | solution.py:248
  129.3 2.3 %collective-permute-done.21.refs_4_ = bf16[16,2,2,16,512]{4,3,2,1,0:T(8,128)(2,1)S(1)} collective-permute-done((bf16[16,2,2,16,512]{4,3,2,1,0:T(8,128)(2,1)S(1)}, bf16[16,2,2,16,512]{4,3,2,1,0:T(8,128)(2,1)S(1)}, u32[]{:S(2)}, u32[]{:S(2)}) %collective-permute-start.21) | collective-permute-done | bytes 1048608 | tf_op jit(solution)/shard_map/ppermute | solution.py:248
  131.6 2.2 %copy-done.2 = f32[2,1024,512]{2,1,0:T(8,128)S(1)} copy-done((f32[2,1024,512]{2,1,0:T(8,128)S(1)}, f32[2,1024,512]{2,1,0:T(8,128)}, u32[]{:S(2)}) %copy-start.2) | copy-done | bytes 4194328
  133.8 9.3 %trail.3 = (f32[2,1024,512]{2,1,0:T(8,128)}, bf16[2,64,512]{2,1,0:T(8,128)(2,1)S(1)}) custom-call(s32[2,4]{1,0:T(2,128)S(1)} %copy-done.21, s32[3]{0:T(128)S(1)} %pad_add_fusion.refs_0_.refs_1_, f32[2,1024,512]{2,1,0:T(8,128)S(1)} %copy-done.2, bf16[16,2,2,16,512]{4,3,2,1,0:T(8,128)(2,1)S(1)} %all-to-all-done.3.refs_3_, ...), custom_call_target="tpu_custom_call" | custom-call | flops 4294967296 | bytes 8388608 | tf_op jit(solution)/shard_map/trail/pallas_call | solution.py:220
  143.1 0.7 pad_maximum_fusion
  (71 shorter events, 5.2 us)
Async XLA Ops:
  1.6 0.9 copy-start.8
  2.5 10.4 %copy-start.26 = (f32[4,128,512]{2,1,0:T(8,128)S(1)}, f32[4,128,512]{2,1,0:T(8,128)}, u32[]{:S(2)}) copy-start(f32[4,128,512]{2,1,0:T(8,128)} %param.11) | copy-start | bytes 3145732
  4.1 10.3 %slice-start = ((bf16[4,4,128,64]{2,3,1,0:T(8,128)(2,1)}), bf16[2,4,128,64]{2,3,1,0:T(8,128)(2,1)S(1)}, s32[]{:S(2)}) async-start(bf16[4,4,128,64]{2,3,1,0:T(8,128)(2,1)} %param.9), calls=%async_computation.4 | async-start | bytes 262144 | tf_op jit(solution)/shard_map/slice | solution.py:271
  4.1 10.6 %copy-start.9 = (f32[4,64,128]{2,1,0:T(8,128)S(1)}, f32[4,64,128]{2,1,0:T(8,128)}, u32[]{:S(2)}) copy-start(f32[4,64,128]{2,1,0:T(8,128)} %refs_1_.3) | copy-start | bytes 393220
  4.1 22.6 %all-to-all-start = ((bf16[16,208,128]{2,1,0:T(8,128)(2,1)}), bf16[16,208,128]{2,1,0:T(8,128)(2,1)S(1)}, u32[]{:S(2)}, u32[]{:S(2)}) async-start(bf16[16,208,128]{2,1,0:T(8,128)(2,1)} %pack.2.refs_3_), calls=%async_computation | async-start | bytes 1703936 | tf_op jit(solution)/shard_map/all_to_all | solution.py:251
  13.2 2.4 %collective-permute-start = (f32[4,16,128]{2,1,0:T(8,128)S(1)}, f32[4,16,128]{2,1,0:T(8,128)S(1)}, u32[]{:S(2)}, u32[]{:S(2)}) collective-permute-start(f32[4,16,128]{2,1,0:T(8,128)S(1)} %bitcast.13), channel_id=1, source_target_pairs={{0,16},{16,0},{1,17},{17,1},{2,18},{18,2},{3,19},{19,3},{4,20},{20... | collective-permute-start | bytes 98312 | tf_op jit(solution)/shard_map/ppermute | solution.py:248
  15.6 11.9 %copy-start = (bf16[16,448,128]{2,1,0:T(8,128)(2,1)}, bf16[16,448,128]{2,1,0:T(8,128)(2,1)S(1)}, u32[]{:S(2)}) copy-start(bf16[16,448,128]{2,1,0:T(8,128)(2,1)S(1)} %pack.3.refs_4_) | copy-start | bytes 5505028
  15.6 13.1 %copy-start.5 = (f32[4,2,16,128]{3,2,1,0:T(8,128)}, f32[4,2,16,128]{3,2,1,0:T(8,128)S(1)}, u32[]{:S(2)}) copy-start(f32[4,2,16,128]{3,2,1,0:T(8,128)S(1)} %pad_maximum_fusion.1.refs_3_.refs_1_) | copy-start | bytes 196612
  27.5 0.6 copy-start.14
  28.1 0.6 copy-start.22
  28.8 29.5 %all-to-all-start.1 = ((bf16[16,448,128]{2,1,0:T(8,128)(2,1)}), bf16[16,448,128]{2,1,0:T(8,128)(2,1)S(1)}, u32[]{:S(2)}, u32[]{:S(2)}) async-start(bf16[16,448,128]{2,1,0:T(8,128)(2,1)} %copy-done), calls=%async_computation.1 | async-start | bytes 3670016 | tf_op jit(solution)/shard_map/all_to_all | solution.py:251
  32.6 14.2 %collective-permute-start.1 = (bf16[16,208,128]{2,1,0:T(8,128)(2,1)S(1)}, bf16[16,208,128]{2,1,0:T(8,128)(2,1)S(1)}, u32[]{:S(2)}, u32[]{:S(2)}) collective-permute-start(bf16[16,208,128]{2,1,0:T(8,128)(2,1)S(1)} %all-to-all-done.refs_2_.refs_4_), channel_id=1, source_target_pairs={{0,16},{16,0},{1,17},{17,1},{2,18},{18,2},{3,19},{19,3},{4,20},{20... | collective-permute-start | bytes 2555912 | tf_op jit(solution)/shard_map/ppermute | solution.py:248
  34.9 2.2 %collective-permute-start.2 = (f32[16,1024]{1,0:T(8,128)}, f32[16,1024]{1,0:T(8,128)S(1)}, u32[]{:S(2)}, u32[]{:S(2)}) collective-permute-start(f32[16,1024]{1,0:T(8,128)} %copy-done.22), channel_id=1, source_target_pairs={{0,16},{16,0},{1,17},{17,1},{2,18},{18,2},{3,19},{19,3},{4,20},{20... | collective-permute-start | bytes 196616 | tf_op jit(solution)/shard_map/ppermute | solution.py:248
  38.0 4.9 %collective-permute-start.5 = (f32[16,1024]{1,0:T(8,128)S(1)}, f32[16,1024]{1,0:T(8,128)S(1)}, u32[]{:S(2)}, u32[]{:S(2)}) collective-permute-start(f32[16,1024]{1,0:T(8,128)S(1)} %add.29.refs_1_), channel_id=1, source_target_pairs={{0,64},{32,96},{64,0},{96,32},{1,65},{33,97},{65,1},{97,33},{2,66}... | collective-permute-start | bytes 196616 | tf_op jit(solution)/shard_map/ppermute | solution.py:255
  40.7 3.7 %collective-permute-start.4 = (f32[16,1024]{1,0:T(8,128)S(1)}, f32[16,1024]{1,0:T(8,128)S(1)}, u32[]{:S(2)}, u32[]{:S(2)}) collective-permute-start(f32[16,1024]{1,0:T(8,128)S(1)} %add.29.refs_1_), channel_id=1, source_target_pairs={{0,96},{32,0},{64,32},{96,64},{1,97},{33,1},{65,33},{97,65},{2,98}... | collective-permute-start | bytes 196616 | tf_op jit(solution)/shard_map/ppermute | solution.py:255
  41.6 4.6 %collective-permute-start.3 = (f32[16,1024]{1,0:T(8,128)S(1)}, f32[16,1024]{1,0:T(8,128)S(1)}, u32[]{:S(2)}, u32[]{:S(2)}) collective-permute-start(f32[16,1024]{1,0:T(8,128)S(1)} %add.29.refs_1_), channel_id=1, source_target_pairs={{0,32},{32,64},{64,96},{96,0},{1,33},{33,65},{65,97},{97,1},{2,34}... | collective-permute-start | bytes 196616 | tf_op jit(solution)/shard_map/ppermute | solution.py:255
  46.7 1.9 %copy-start.10 = (bf16[16,1024]{1,0:T(8,128)(2,1)}, bf16[16,1024]{1,0:T(8,128)(2,1)S(1)}, u32[]{:S(2)}) copy-start(bf16[16,1024]{1,0:T(8,128)(2,1)S(1)} %get-tuple-element.37.refs_6_) | copy-start | bytes 98308
  46.8 6.9 %copy-start.17 = (bf16[16,512]{1,0:T(8,128)(2,1)}, bf16[16,512]{1,0:T(8,128)(2,1)S(1)}, u32[]{:S(2)}) copy-start(bf16[16,512]{1,0:T(8,128)(2,1)S(1)} %get-tuple-element.49.refs_1_) | copy-start | bytes 49156
  46.8 6.9 %copy-start.24 = (bf16[16,512]{1,0:T(8,128)(2,1)}, bf16[16,512]{1,0:T(8,128)(2,1)S(1)}, u32[]{:S(2)}) copy-start(bf16[16,512]{1,0:T(8,128)(2,1)S(1)} %get-tuple-element.50) | copy-start | bytes 49156
  46.8 0.8 copy-start.6
  48.7 5.0 %collective-permute-start.8 = (f32[16,1024]{1,0:T(8,128)S(1)}, f32[16,1024]{1,0:T(8,128)S(1)}, u32[]{:S(2)}, u32[]{:S(2)}) collective-permute-start(f32[16,1024]{1,0:T(8,128)S(1)} %step.3.refs_1_), channel_id=1, source_target_pairs={{0,64},{32,96},{64,0},{96,32},{1,65},{33,97},{65,1},{97,33},{2,66}... | collective-permute-start | bytes 196616 | tf_op jit(solution)/shard_map/ppermute | solution.py:255
  49.7 3.9 %collective-permute-start.7 = (f32[16,1024]{1,0:T(8,128)S(1)}, f32[16,1024]{1,0:T(8,128)S(1)}, u32[]{:S(2)}, u32[]{:S(2)}) collective-permute-start(f32[16,1024]{1,0:T(8,128)S(1)} %step.3.refs_1_), channel_id=1, source_target_pairs={{0,96},{32,0},{64,32},{96,64},{1,97},{33,1},{65,33},{97,65},{2,98}... | collective-permute-start | bytes 196616 | tf_op jit(solution)/shard_map/ppermute | solution.py:255
  50.8 5.1 %collective-permute-start.6 = (f32[16,1024]{1,0:T(8,128)S(1)}, f32[16,1024]{1,0:T(8,128)S(1)}, u32[]{:S(2)}, u32[]{:S(2)}) collective-permute-start(f32[16,1024]{1,0:T(8,128)S(1)} %step.3.refs_1_), channel_id=1, source_target_pairs={{0,32},{32,64},{64,96},{96,0},{1,33},{33,65},{65,97},{97,1},{2,34}... | collective-permute-start | bytes 196616 | tf_op jit(solution)/shard_map/ppermute | solution.py:255
  56.4 0.6 copy-start.12
  57.1 0.6 copy-start.19
  57.6 0.6 copy-start.25
  58.2 16.0 %collective-permute-start.9 = (bf16[16,448,128]{2,1,0:T(8,128)(2,1)S(1)}, bf16[16,448,128]{2,1,0:T(8,128)(2,1)}, u32[]{:S(2)}, u32[]{:S(2)}) collective-permute-start(bf16[16,448,128]{2,1,0:T(8,128)(2,1)S(1)} %all-to-all-done.1.refs_4_), channel_id=1, source_target_pairs={{0,16},{16,0},{1,17},{17,1},{2,18},{18,2},{3,19},{19,3},{4,20},{20... | collective-permute-start | bytes 5505032 | tf_op jit(solution)/shard_map/ppermute | solution.py:248
  60.7 3.5 %collective-permute-start.18 = (bf16[16,512]{1,0:T(8,128)(2,1)}, bf16[16,512]{1,0:T(8,128)(2,1)S(1)}, u32[]{:S(2)}, u32[]{:S(2)}) collective-permute-start(bf16[16,512]{1,0:T(8,128)(2,1)} %copy-done.24), channel_id=1, source_target_pairs={{0,16},{16,0},{1,17},{17,1},{2,18},{18,2},{3,19},{19,3},{4,20},{20... | collective-permute-start | bytes 49160 | tf_op jit(solution)/shard_map/ppermute | solution.py:248
  60.7 3.7 %collective-permute-start.19 = (bf16[16,512]{1,0:T(8,128)(2,1)}, bf16[16,512]{1,0:T(8,128)(2,1)S(1)}, u32[]{:S(2)}, u32[]{:S(2)}) collective-permute-start(bf16[16,512]{1,0:T(8,128)(2,1)} %copy-done.25), channel_id=1, source_target_pairs={{0,16},{16,0},{1,17},{17,1},{2,18},{18,2},{3,19},{19,3},{4,20},{20... | collective-permute-start | bytes 49160 | tf_op jit(solution)/shard_map/ppermute | solution.py:248
  64.4 0.7 copy-start.18
  65.1 0.7 copy-start.20
  66.4 1.0 copy-start.3
  67.4 29.4 %all-to-all-start.2 = ((bf16[16,2,2,16,512]{4,3,2,1,0:T(8,128)(2,1)}), bf16[16,2,2,16,512]{4,3,2,1,0:T(8,128)(2,1)}, u32[]{:S(2)}, u32[]{:S(2)}) async-start(bf16[16,2,2,16,512]{4,3,2,1,0:T(8,128)(2,1)} %copy-done.3), calls=%async_computation.2 | async-start | bytes 2097152 | tf_op jit(solution)/shard_map/all_to_all | solution.py:251
  74.2 0.8 copy-start.7
  75.1 0.8 copy-start.11
  75.8 0.8 copy-start.13
  78.7 5.1 %collective-permute-start.12 = (f32[16,1024]{1,0:T(8,128)S(1)}, f32[16,1024]{1,0:T(8,128)S(1)}, u32[]{:S(2)}, u32[]{:S(2)}) collective-permute-start(f32[16,1024]{1,0:T(8,128)S(1)} %step.4.refs_1_), channel_id=1, source_target_pairs={{0,64},{32,96},{64,0},{96,32},{1,65},{33,97},{65,1},{97,33},{2,66}... | collective-permute-start | bytes 196616 | tf_op jit(solution)/shard_map/ppermute | solution.py:255
  78.7 5.0 %collective-permute-start.11 = (f32[16,1024]{1,0:T(8,128)S(1)}, f32[16,1024]{1,0:T(8,128)S(1)}, u32[]{:S(2)}, u32[]{:S(2)}) collective-permute-start(f32[16,1024]{1,0:T(8,128)S(1)} %step.4.refs_1_), channel_id=1, source_target_pairs={{0,96},{32,0},{64,32},{96,64},{1,97},{33,1},{65,33},{97,65},{2,98}... | collective-permute-start | bytes 196616 | tf_op jit(solution)/shard_map/ppermute | solution.py:255
  79.8 5.4 %collective-permute-start.10 = (f32[16,1024]{1,0:T(8,128)S(1)}, f32[16,1024]{1,0:T(8,128)S(1)}, u32[]{:S(2)}, u32[]{:S(2)}) collective-permute-start(f32[16,1024]{1,0:T(8,128)S(1)} %step.4.refs_1_), channel_id=1, source_target_pairs={{0,32},{32,64},{64,96},{96,0},{1,33},{33,65},{65,97},{97,1},{2,34}... | collective-permute-start | bytes 196616 | tf_op jit(solution)/shard_map/ppermute | solution.py:255
  85.8 0.6 copy-start.15
  86.4 0.6 copy-start.23
  89.1 21.8 %copy-start.21 = (s32[2,4]{1,0:T(2,128)S(1)}, s32[2,4]{1,0:T(2,128)}, u32[]{:S(2)}) copy-start(s32[2,4]{1,0:T(2,128)} %refs_0_.3) | copy-start | bytes 100
  89.2 4.7 %collective-permute-start.16 = (f32[16,1024]{1,0:T(8,128)S(1)}, f32[16,1024]{1,0:T(8,128)S(1)}, u32[]{:S(2)}, u32[]{:S(2)}) collective-permute-start(f32[16,1024]{1,0:T(8,128)S(1)} %step.5.refs_1_), channel_id=1, source_target_pairs={{0,64},{32,96},{64,0},{96,32},{1,65},{33,97},{65,1},{97,33},{2,66}... | collective-permute-start | bytes 196616 | tf_op jit(solution)/shard_map/ppermute | solution.py:255
  89.3 4.6 %collective-permute-start.15 = (f32[16,1024]{1,0:T(8,128)S(1)}, f32[16,1024]{1,0:T(8,128)S(1)}, u32[]{:S(2)}, u32[]{:S(2)}) collective-permute-start(f32[16,1024]{1,0:T(8,128)S(1)} %step.5.refs_1_), channel_id=1, source_target_pairs={{0,96},{32,0},{64,32},{96,64},{1,97},{33,1},{65,33},{97,65},{2,98}... | collective-permute-start | bytes 196616 | tf_op jit(solution)/shard_map/ppermute | solution.py:255
  90.8 4.8 %collective-permute-start.14 = (f32[16,1024]{1,0:T(8,128)S(1)}, f32[16,1024]{1,0:T(8,128)S(1)}, u32[]{:S(2)}, u32[]{:S(2)}) collective-permute-start(f32[16,1024]{1,0:T(8,128)S(1)} %step.5.refs_1_), channel_id=1, source_target_pairs={{0,32},{32,64},{64,96},{96,0},{1,33},{33,65},{65,97},{97,1},{2,34}... | collective-permute-start | bytes 196616 | tf_op jit(solution)/shard_map/ppermute | solution.py:255
  96.8 14.1 %collective-permute-start.20 = (bf16[16,2,2,16,512]{4,3,2,1,0:T(8,128)(2,1)}, bf16[16,2,2,16,512]{4,3,2,1,0:T(8,128)(2,1)S(1)}, u32[]{:S(2)}, u32[]{:S(2)}) collective-permute-start(bf16[16,2,2,16,512]{4,3,2,1,0:T(8,128)(2,1)} %all-to-all-done.2.refs_3_), channel_id=1, source_target_pairs={{0,16},{16,0},{1,17},{17,1},{2,18},{18,2},{3,19},{19,3},{4,20},{20... | collective-permute-start | bytes 3145736 | tf_op jit(solution)/shard_map/ppermute | solution.py:248
  99.1 2.5 %collective-permute-start.13 = (bf16[16,512]{1,0:T(8,128)(2,1)}, bf16[16,512]{1,0:T(8,128)(2,1)S(1)}, u32[]{:S(2)}, u32[]{:S(2)}) collective-permute-start(bf16[16,512]{1,0:T(8,128)(2,1)} %copy-done.23), channel_id=1, source_target_pairs={{0,16},{16,0},{1,17},{17,1},{2,18},{18,2},{3,19},{19,3},{4,20},{20... | collective-permute-start | bytes 49160 | tf_op jit(solution)/shard_map/ppermute | solution.py:248
  99.1 2.5 %collective-permute-start.17 = (bf16[16,512]{1,0:T(8,128)(2,1)S(1)}, bf16[16,512]{1,0:T(8,128)(2,1)S(1)}, u32[]{:S(2)}, u32[]{:S(2)}) collective-permute-start(bf16[16,512]{1,0:T(8,128)(2,1)S(1)} %get-tuple-element.48), channel_id=1, source_target_pairs={{0,16},{16,0},{1,17},{17,1},{2,18},{18,2},{3,19},{19,3},{4,20},{20... | collective-permute-start | bytes 49160 | tf_op jit(solution)/shard_map/ppermute | solution.py:248
  101.6 0.7 copy-start.16
  104.0 23.2 %all-to-all-start.3 = ((bf16[16,2,2,16,512]{4,3,2,1,0:T(8,128)(2,1)}), bf16[16,2,2,16,512]{4,3,2,1,0:T(8,128)(2,1)S(1)}, u32[]{:S(2)}, u32[]{:S(2)}) async-start(bf16[16,2,2,16,512]{4,3,2,1,0:T(8,128)(2,1)} %bundle.3), calls=%async_computation.3 | async-start | bytes 2097152 | tf_op jit(solution)/shard_map/all_to_all | solution.py:251
  110.9 1.6 %copy-start.4 = (bf16[2,1024,512]{2,1,0:T(8,128)(2,1)S(1)}, bf16[2,1024,512]{2,1,0:T(8,128)(2,1)}, u32[]{:S(2)}) copy-start(bf16[2,1024,512]{2,1,0:T(8,128)(2,1)} %refs_2_.1) | copy-start | bytes 6291460
  120.7 2.0 %copy-start.1 = (f32[2,1024,512]{2,1,0:T(8,128)}, f32[2,1024,512]{2,1,0:T(8,128)S(1)}, u32[]{:S(2)}) copy-start(f32[2,1024,512]{2,1,0:T(8,128)S(1)} %get-tuple-element.58.refs_2_) | copy-start | bytes 12582916
  127.2 4.4 %collective-permute-start.21 = (bf16[16,2,2,16,512]{4,3,2,1,0:T(8,128)(2,1)S(1)}, bf16[16,2,2,16,512]{4,3,2,1,0:T(8,128)(2,1)S(1)}, u32[]{:S(2)}, u32[]{:S(2)}) collective-permute-start(bf16[16,2,2,16,512]{4,3,2,1,0:T(8,128)(2,1)S(1)} %all-to-all-done.3.refs_3_), channel_id=1, source_target_pairs={{0,16},{16,0},{1,17},{17,1},{2,18},{18,2},{3,19},{19,3},{4,20},{20... | collective-permute-start | bytes 3145736 | tf_op jit(solution)/shard_map/ppermute | solution.py:248
  131.6 2.2 %copy-start.2 = (f32[2,1024,512]{2,1,0:T(8,128)S(1)}, f32[2,1024,512]{2,1,0:T(8,128)}, u32[]{:S(2)}) copy-start(f32[2,1024,512]{2,1,0:T(8,128)} %copy-done.1) | copy-start | bytes 12582916

commit v3 on v2

v3 whole, which is shorter than its diff:
```python
import jax
import jax.numpy as jnp
from jax import lax
from jax.experimental import pallas as pl
from jax.experimental.pallas import tpu as pltpu
from jax.sharding import Mesh
from jax.sharding import PartitionSpec as P

NT = (((1,), (1,)), ((), ()))
NN = (((1,), (0,)), ((), ()))
MIB = 1024 * 1024
EARLY = ((0, None), (1, None), (1, 0))
LATE = ((2, None), (2, 0), (2, 1), (3, None), (3, 0), (3, 1), (3, 2))
REST = 16


def core_of():
    return lax.axis_index("core")


def slab_of(core):
    return lax.axis_index("x") * lax.axis_size("core") + core


def col_of():
    return lax.axis_index("z") * lax.axis_size("y") + lax.axis_index("y")


def dot(a, b, dims):
    return lax.dot_general(a, b, dims, preferred_element_type=jnp.float32)


def call(kernel, outs, *operands, name, scratch=(), after=(), limit=24):
    vmem = pl.BlockSpec(memory_space=pltpu.VMEM)
    unread = pl.BlockSpec(memory_space=pl.ANY)
    count = len(operands)
    return pl.pallas_call(
        lambda *refs: kernel(*refs[:count], *refs[count + len(after) :]),
        out_shape=outs,
        in_specs=[vmem] * count + [unread] * len(after),
        out_specs=jax.tree.map(lambda _: vmem, outs),
        scratch_shapes=list(scratch),
        compiler_params=pltpu.CompilerParams(vmem_limit_bytes=limit * MIB),
        cost_estimate=pl.CostEstimate(
            flops=2**28, bytes_accessed=2**21, transcendentals=0
        ),
        name=name,
    )(*operands, *after)


def pack_kernel(members, inverse_ref, across_ref, out_ref):
    columns, rows, width = inverse_ref.shape
    blocks = []
    for column, earlier in members:
        if earlier is None:
            blocks.append(inverse_ref[column].astype(jnp.bfloat16))
        else:
            blocks.append(across_ref[column, earlier])
    if members[0][0] == 0:
        first_row, first_lane = col_of() * rows, slab_of(core_of()) * width
        on_diagonal = (
            lax.broadcasted_iota(jnp.int32, (rows, width), 0) + first_row
            == lax.broadcasted_iota(jnp.int32, (rows, width), 1) + first_lane
        )
        at_row = lax.broadcasted_iota(jnp.int32, (REST, width), 0)
        tile = jnp.zeros((REST, width), jnp.float32)
        for column in range(columns):
            value = inverse_ref[column]
            rest = value - value.astype(jnp.bfloat16).astype(jnp.float32)
            line = jnp.sum(jnp.where(on_diagonal, rest, 0.0), axis=0, keepdims=True)
            tile = tile + jnp.where(at_row == column, line, 0.0)
        blocks.append(tile.astype(jnp.bfloat16))
    whole = jnp.concatenate(blocks, axis=0)
    for copy in range(out_ref.shape[0]):
        out_ref[copy] = whole


def pack(members, copies, inverse, across, after=()):
    count = len(members) * inverse.shape[1] + (REST if members[0][0] == 0 else 0)
    return call(
        lambda *refs: pack_kernel(members, *refs),
        jax.ShapeDtypeStruct((copies, count, inverse.shape[2]), jnp.bfloat16),
        inverse,
        across,
        after=after,
        name="pack",
    )


def block_of(ref, at, size):
    return ref[:, at : at + size].reshape(ref.shape[0] * size, ref.shape[2])


def rest_of(ref, column):
    tiles = ref[:, ref.shape[1] - REST :].astype(jnp.float32)
    return jnp.sum(tiles, axis=0)[column : column + 1]


def apply_inverse(right, inverse, rest, slab, out_ref, add):
    count, width = right.shape
    high = right.astype(jnp.bfloat16)
    low = (right - high.astype(jnp.float32)).astype(jnp.bfloat16)
    both = dot(jnp.concatenate([high, low], axis=0), inverse, NT)
    value = both[:count] + both[count:]
    out_ref[...] = out_ref[...] + value if add else value
    lanes = pl.ds(pl.multiple_of(slab * width, width), width)
    out_ref[:, lanes] = out_ref[:, lanes] + right * rest


def first_kernel(
    size, right_ref, group_ref, keep_ref, give_ref, mark_ref, out_ref
):
    apply_inverse(
        right_ref[...],
        block_of(group_ref, 0, size),
        rest_of(group_ref, 0),
        slab_of(core_of()),
        out_ref,
        False,
    )
    core = core_of()
    count = keep_ref.shape[0]
    keep_ref[...] = out_ref[pl.ds(pl.multiple_of(core * count, count), count)]
    give_ref[...] = out_ref[pl.ds(pl.multiple_of((1 - core) * count, count), count)]
    mark_ref[...] = right_ref[: mark_ref.shape[0]]


def part_kernel(start, group_ref, out_ref):
    out_ref[...] = group_ref[:, start : start + out_ref.shape[1]]


def part(group, start, length, after):
    shape = (group.shape[0], length, group.shape[2])
    return call(
        lambda *refs: part_kernel(start, *refs),
        jax.ShapeDtypeStruct(shape, group.dtype),
        group,
        after=after,
        name="part",
    )


def halves(solved_ref, core, keep_ref, give_ref):
    half = keep_ref.shape[1]
    keep_ref[...] = solved_ref[:, pl.ds(pl.multiple_of(core * half, half), half)]
    give_ref[...] = solved_ref[:, pl.ds(pl.multiple_of((1 - core) * half, half), half)]


def close_kernel(n_parts, *refs):
    part_refs, before_refs = refs[:n_parts], refs[n_parts:-4]
    solved_ref, keep_ref, give_ref, mark_ref = refs[-4:]
    total = part_refs[0][...]
    for part_ref in part_refs[1:]:
        total = total + part_ref[...]
    last = solved_ref.shape[0] - 1
    for ref in before_refs:
        solved_ref[:last] = ref[...]
    solved_ref[last] = total.astype(jnp.bfloat16)
    halves(solved_ref.at[last], core_of(), keep_ref, give_ref)
    mark_ref[...] = total[: mark_ref.shape[0], : mark_ref.shape[1]]


def step_kernel(column, starts, size, state_ref, solved_ref, *refs):
    group_refs, out_ref = refs[:2], refs[2]
    columns = state_ref.shape[0]
    if column == 1:
        next_ref = refs[3]
        next_ref[:columns] = state_ref[...]
        for side, ref in enumerate(group_refs):
            tiles = ref[:, ref.shape[1] - REST :].astype(jnp.float32)
            next_ref[columns, side] = jnp.sum(tiles, axis=0)
        state_ref, columns = next_ref, columns + 1
    slabs = (slab_of(core_of()), slab_of(1 - core_of()))
    for side, (ref, start) in enumerate(zip(group_refs, starts)):
        right = state_ref[column, side]
        for i in range(column):
            right = right - dot(
                solved_ref[i], block_of(ref, start + (1 + i) * size, size), NN
            )
        apply_inverse(
            right,
            block_of(ref, start, size),
            state_ref[columns - 1, side, column : column + 1],
            slabs[side],
            out_ref,
            side > 0,
        )


def bundle_kernel(*refs):
    core = core_of()
    out_ref, mark_ref = refs[-2:]
    for k in range(len(refs) // 2 - 1):
        keep, got = refs[2 * k][...], refs[2 * k + 1][...]
        for copy in range(out_ref.shape[0]):
            out_ref[copy, k, core] = keep
            out_ref[copy, k, 1 - core] = got
    mark_ref[...] = jnp.zeros(mark_ref.shape, mark_ref.dtype)


def trail_kernel(columns, before, pattern_ref, base_ref, mine_ref, other_ref, *refs):
    count = len(columns)
    factor_refs, (out_ref, own_ref) = refs[:count], refs[-2:]
    row = pl.program_id(0)
    core = core_of()
    width, half = out_ref.shape[2], mine_ref.shape[4]
    offsets = [
        pl.multiple_of(core * half, half),
        pl.multiple_of((1 - core) * half, half),
    ]

    def solved(ref, k):
        return ref[:, k].reshape(width, half)

    total = base_ref[0].astype(jnp.float32)
    for k, column in enumerate(columns):
        product = None
        for ref, offset in zip((mine_ref, other_ref), offsets):
            factor = factor_refs[k][0, 0, :, pl.ds(offset, half)]
            term = dot(factor, solved(ref, k), NT)
            product = term if product is None else product + term
        total = total - pattern_ref[row, column].astype(jnp.float32) * product
    out_ref[0] = total

    @pl.when((row == 0) & (pl.program_id(1) == 0))
    def _():
        own = own_ref.shape[1]
        lane = lax.broadcasted_iota(jnp.int32, (own, half), 1)
        wanted = lax.broadcasted_iota(jnp.int32, (own, half), 0) + col_of() * own
        if before:
            own_ref[:before] = refs[count][...]
        for k in range(count):
            rows = None
            for ref, offset in zip((mine_ref, other_ref), offsets):
                pick = (lane + offset == wanted).astype(jnp.bfloat16)
                term = dot(pick, solved(ref, k), NT)
                rows = term if rows is None else rows + term
            own_ref[before + k] = rows.astype(jnp.bfloat16)


def trail(columns, pattern, base, factor, mine, other, own, tile, done=(), after=()):
    n_rows, height, width = base.shape
    depth = factor.shape[-1]
    count, before = len(columns), sum(d.shape[0] for d in done)
    smem = pl.BlockSpec(memory_space=pltpu.SMEM)
    row_tile = pl.BlockSpec((1, tile, width), lambda r, a: (r, a, 0))

    def factor_spec(column):
        return pl.BlockSpec((1, 1, tile, depth), lambda r, a: (r, column, a, 0))

    def whole(shape):
        return pl.BlockSpec(shape, lambda r, a: (0,) * len(shape))

    held = 4 + count + len(done)
    own_shape = (before + count, own, width)
    return pl.pallas_call(
        lambda *refs: trail_kernel(columns, before, *refs[:held], *refs[-2:]),
        grid=(n_rows, height // tile),
        in_specs=[smem, row_tile, whole(mine.shape), whole(other.shape)]
        + [factor_spec(column) for column in columns]
        + [whole(d.shape) for d in done]
        + [pl.BlockSpec(memory_space=pl.ANY)] * len(after),
        out_specs=[row_tile, whole(own_shape)],
        out_shape=[
            jax.ShapeDtypeStruct(base.shape, jnp.float32),
            jax.ShapeDtypeStruct(own_shape, jnp.bfloat16),
        ],
        compiler_params=pltpu.CompilerParams(vmem_limit_bytes=58 * MIB),
        cost_estimate=pl.CostEstimate(
            flops=2 * n_rows * height * width * depth * count,
            bytes_accessed=2 * n_rows * height * depth * count,
            transcendentals=0,
        ),
        name="trail",
    )(pattern, base, mine, other, *([factor] * count), *done, *after)


def make(sizes):
    n_x, n_core, n_z, n_y = sizes
    n_col = n_z * n_y

    def swap(value):
        return lax.ppermute(value, "core", [(i, n_core - 1 - i) for i in range(n_core)])

    def exchange(value):
        return lax.all_to_all(value, ("z", "y"), 0, 0)

    def parts_over_x(value):
        return [value] + [
            lax.ppermute(value, "x", [(i, (i + k) % n_x) for i in range(n_x)])
            for k in (1, n_x - 1, 2)
        ]

    def per_device(factor, pattern, rhs_trail, coupling, inverse, rhs):
        columns, height, width = rhs.shape
        share = width // (n_core * n_col)
        size = inverse.shape[1]
        block = n_col * size
        core = lax.axis_index("core")
        col = lax.axis_index("z") * n_y + lax.axis_index("y")

        tied = lax.optimization_barrier
        across = coupling.transpose(0, 1, 3, 2)
        packed = pack(EARLY, n_col, inverse, across)
        early = exchange(packed)
        packed_late = pack(LATE, n_col, inverse, across, after=[packed])
        right = lax.dynamic_slice(
            rhs, (0, 0, col * n_core * share), (columns, height, n_core * share)
        ).transpose(0, 2, 1)
        rights = [
            lax.dynamic_slice(right, (0, which * share, 0), (columns, share, height))
            for which in (core, 1 - core)
        ]
        rights = jnp.stack([rights[0], swap(rights[1])], axis=1)

        partial_shape = jax.ShapeDtypeStruct((share, block), jnp.float32)
        half_shape = jax.ShapeDtypeStruct((share, block // n_core), jnp.bfloat16)
        mark_shape = jax.ShapeDtypeStruct((8, 128), jnp.float32)
        early_both = (early, swap(early))
        keep, give, mark = call(
            lambda *refs: first_kernel(size, *refs),
            (partial_shape, partial_shape, mark_shape),
            right[0],
            early,
            scratch=[pltpu.VMEM((n_core * share, block), jnp.float32)],
            after=[rights, packed_late],
            name="first",
        )
        packed_late, mark = tied((packed_late, mark))
        late = exchange(packed_late)
        partial_sum = keep + swap(give)

        def send(halves_of, after):
            shape = (n_col, len(halves_of) // 2, n_core, share, block // n_core)
            bundle, mark = call(
                bundle_kernel,
                (jax.ShapeDtypeStruct(shape, jnp.bfloat16), mark_shape),
                    *halves_of,
                after=after,
                name="bundle",
            )
            return exchange(bundle), mark

        state, solved, sent = rights, [], []
        for column in range(1, columns + 1):
            parts = parts_over_x(partial_sum)
            *solved, keep, give, mark = call(
                lambda *refs: close_kernel(n_x, *refs),
                (
                    jax.ShapeDtypeStruct((column, share, block), jnp.bfloat16),
                    half_shape,
                    half_shape,
                    mark_shape,
                ),
                *parts,
                *solved,
                after=[mark],
                name="close",
            )
            sent += [keep, swap(give)]
            if column == columns:
                break
            if column == 1:
                group, starts = early_both, (size, size)
            elif column == 2:
                first_pair, sent_mark = send(sent, [])
                group = (late, swap(part(late, 0, 3 * size, [mark, sent_mark])))
                starts = (0, 0)
            else:
                group, starts = (late, other), (3 * size, 0)
            outs = [partial_shape]
            if column == 1:
                outs += [jax.ShapeDtypeStruct((columns + 1, *state.shape[1:]), state.dtype)]
            partial_sum, *more = call(
                lambda *refs, c=column, a=starts: step_kernel(c, a, size, *refs),
                outs,
                state,
                *solved,
                *group,
                name="step",
            )
            if column == 1:
                (state,) = more
            if column == 2:
                other = swap(part(late, 3 * size, 4 * size, [partial_sum]))

        second_pair, mark = send(sent[4:], [])
        first_pair, mark = tied((first_pair, mark))
        base, blocks = trail(
            (0, 1),
            pattern,
            rhs_trail,
            factor,
            first_pair,
            swap(first_pair),
            size,
            512,
            after=[mark],
        )
        second_pair, blocks = tied((second_pair, blocks))
        updated, blocks = trail(
            (2, 3),
            pattern,
            base,
            factor,
            second_pair,
            swap(second_pair),
            size,
            512,
            (blocks,),
        )
        return blocks, updated

    return per_device


def solution(mesh):
    row, col = mesh.shape["row"], mesh.shape["col"]
    sizes = (row // 2, 2, 4, col // 4)
    fine = Mesh(mesh.devices.reshape(sizes), ("x", "core", "z", "y"))
    r, c = ("x", "core"), ("z", "y")
    return jax.shard_map(
        make(sizes),
        mesh=fine,
        in_specs=(
            P(r + c, None, None, None),
            P(r + c, None),
            P(r + c, None, None),
            P(None, None, r, c),
            P(None, c, r),
            P(None, r, None),
        ),
        out_specs=(P(None, c, None), P(r + c, None, None)),
        check_vma=False,
    )
```

time: 145 us -> 129 us (0.89)
  local copies, waits for them, and re-layouts: 18.9 us -> 8.32 us
  waiting for transfers between devices: 43.6 us -> 36.7 us
  starting transfers between devices: 47.5 us -> 54 us
  Pallas kernels: 31.1 us -> 28 us
  other arithmetic: 1.66 us -> 0.02 us
    unnamed x59 -> x23, local copies, waits for them, and re-layouts: 17.8 us -> 5.69 us
    pallas_call x12 -> x14, Pallas kernels: 13.6 us -> 6.29 us  [call(): pl.pallas_call(lambda *refs: kernel(*refs[:count], *refs[count + len(afte...]
    ppermute x10 -> x11, starting transfers between devices: 11.3 us -> 16.8 us  [swap(): lax.ppermute(value, 'core', [(i, n_core - 1 - i) for i in range(n_core)])]
    ppermute x12, waiting for transfers between devices: 18.4 us -> 14.2 us  [parts_over_x(): lax.ppermute(value, 'x', [(i, (i + k) % n_x) for i in range(n_x)])]
    pallas_call x2, Pallas kernels: 17.6 us -> 21.7 us  [trail(): pl.pallas_call(lambda *refs: trail_kernel(columns, before, *refs[:held],...]
    ppermute x12, starting transfers between devices: 10 us -> 13.6 us  [parts_over_x(): lax.ppermute(value, 'x', [(i, (i + k) % n_x) for i in range(n_x)])]
    all_to_all x4, starting transfers between devices: 26.2 us -> 23.6 us  [exchange(): return lax.all_to_all(value, ('z', 'y'), 0, 0)]
    ppermute x10 -> x11, waiting for transfers between devices: 9.58 us -> 7.89 us  [swap(): lax.ppermute(value, 'core', [(i, n_core - 1 - i) for i in range(n_core)])]
  transfers between devices with their start and end apart: 26 -> 27, of which waited for: 16 -> 18; matrix products, arithmetic and copies ran while one was open for 1% -> 2% of each run, Pallas kernels for 13% -> 11%
where the time goes in v3:
time: 129 us; the launch traced here: 128 us
  starting transfers between devices  54 us (42%)
  waiting for transfers between devices  36.7 us (28%)
  Pallas kernels  28 us (22%)
  local copies, waits for them, and re-layouts  8.32 us (6%)
    all_to_all x4, starting transfers between devices, exchange(): return lax.all_to_all(value, ('z', 'y'), 0, 0)  23.6 us
    pallas_call x2, Pallas kernels, trail(): pl.pallas_call(lambda *refs: trail_kernel(columns, before, *refs[:held],...  21.7 us
    ppermute x11, starting transfers between devices, swap(): lax.ppermute(value, 'core', [(i, n_core - 1 - i) for i in range(n_core)])  16.8 us
    all_to_all x4, waiting for transfers between devices, exchange(): return lax.all_to_all(value, ('z', 'y'), 0, 0)  14.6 us
    ppermute x12, waiting for transfers between devices, parts_over_x(): lax.ppermute(value, 'x', [(i, (i + k) % n_x) for i in range(n_x)])  14.2 us
    ppermute x12, starting transfers between devices, parts_over_x(): lax.ppermute(value, 'x', [(i, (i + k) % n_x) for i in range(n_x)])  13.6 us
    ppermute x11, waiting for transfers between devices, swap(): lax.ppermute(value, 'core', [(i, n_core - 1 - i) for i in range(n_core)])  7.89 us
    pallas_call x14, Pallas kernels, call(): pl.pallas_call(lambda *refs: kernel(*refs[:count], *refs[count + len(afte...  6.29 us
  transfers between devices with their start and end apart: 27, of which 18 were waited for; matrix products, arithmetic and copies ran while one was open for 2% of the time, Pallas kernels for 11%

profile of v3, /device:TPU:1, one launch (start us, length us, event | category | flops | bytes accessed | tf_op | source)
XLA Modules:
  0.0 127.9 jit_solution(9863051956445220774)
XLA Ops:
  0.6 0.9 copy-done.1
  1.6 0.9 copy-done.4
  2.5 1.0 pack.2.refs_2_
  3.5 8.6 %all-to-all-start = ((bf16[16,208,128]{2,1,0:T(8,128)(2,1)}), bf16[16,208,128]{2,1,0:T(8,128)(2,1)S(1)}, u32[]{:S(2)}, u32[]{:S(2)}) async-start(bf16[16,208,128]{2,1,0:T(8,128)(2,1)} %pack.2.refs_2_), calls=%async_computation | async-start | bytes 1703936 | tf_op jit(solution)/shard_map/all_to_all | solution.py:286
  12.1 1.5 %constant_dynamic-slice_fusion.1 = (f32[4,128,16]{2,1,0:T(8,128)S(1)}, f32[4,128,16]{2,1,0:T(8,128)S(1)}) fusion(f32[4,128,512]{2,1,0:T(8,128)} %param.11, s32[]{:T(128)S(6)} %dynamic_slice.14, s32[]{:T(128)S(6)} %dynamic_slice.16), kind=kLoop, calls=%fused_computation.3 | loop fusion | bytes 131080 | tf_op jit(solution)/shard_map/dynamic-slice
  13.8 1.0 collective-permute-start
  14.8 1.1 constant_dynamic-slice_fusion.2
  15.9 0.1 copy.11
  16.0 0.1 copy.12
  16.1 0.3 pack.3.refs_3_
  16.5 9.5 %all-to-all-done.refs_1_.refs_2_ = bf16[16,208,128]{2,1,0:T(8,128)(2,1)S(1)} async-done(((bf16[16,208,128]{2,1,0:T(8,128)(2,1)}), bf16[16,208,128]{2,1,0:T(8,128)(2,1)S(1)}, u32[]{:S(2)}, u32[]{:S(2)}) %all-to-all-start) | async-done | bytes 852000 | tf_op jit(solution)/shard_map/all_to_all | solution.py:286
  26.0 0.2 first.1
  26.2 3.8 %all-to-all-start.2 = ((bf16[16,448,128]{2,1,0:T(8,128)(2,1)}), bf16[16,448,128]{2,1,0:T(8,128)(2,1)S(1)}, u32[]{:S(2)}, u32[]{:S(2)}) async-start(bf16[16,448,128]{2,1,0:T(8,128)(2,1)} %copy-done), calls=%async_computation.2 | async-start | bytes 3670016 | tf_op jit(solution)/shard_map/all_to_all | solution.py:286
  30.0 2.4 %collective-permute-start.6 = (bf16[16,208,128]{2,1,0:T(8,128)(2,1)S(1)}, bf16[16,208,128]{2,1,0:T(8,128)(2,1)S(1)}, u32[]{:S(2)}, u32[]{:S(2)}) collective-permute-start(bf16[16,208,128]{2,1,0:T(8,128)(2,1)S(1)} %all-to-all-done.refs_1_.refs_2_), channel_id=1, source_target_pairs={{0,16},{16,0},{1,17},{17,1},{2,18},{18,2},{3,19},{19,3},{4,20},{20... | collective-permute-start | bytes 2555912 | tf_op jit(solution)/shard_map/ppermute | solution.py:283
  32.5 2.0 %collective-permute-done.1 = f32[16,1024]{1,0:T(8,128)S(1)} collective-permute-done((f32[16,1024]{1,0:T(8,128)S(1)}, f32[16,1024]{1,0:T(8,128)S(1)}, u32[]{:S(2)}, u32[]{:S(2)}) %collective-permute-start.1) | collective-permute-done | bytes 65568 | tf_op jit(solution)/shard_map/ppermute | solution.py:283
  34.5 2.8 %collective-permute-start.4 = (f32[16,1024]{1,0:T(8,128)S(1)}, f32[16,1024]{1,0:T(8,128)S(1)}, u32[]{:S(2)}, u32[]{:S(2)}) collective-permute-start(f32[16,1024]{1,0:T(8,128)S(1)} %add.25.refs_0_), channel_id=1, source_target_pairs={{0,64},{32,96},{64,0},{96,32},{1,65},{33,97},{65,1},{97,33},{2,66}... | collective-permute-start | bytes 196616 | tf_op jit(solution)/shard_map/ppermute | solution.py:290
  37.3 0.9 collective-permute-start.3
  38.2 0.6 collective-permute-start.2
  38.8 0.4 collective-permute-done.4.refs_3_
  39.2 1.9 %collective-permute-done.3.refs_2_ = f32[16,1024]{1,0:T(8,128)S(1)} collective-permute-done((f32[16,1024]{1,0:T(8,128)S(1)}, f32[16,1024]{1,0:T(8,128)S(1)}, u32[]{:S(2)}, u32[]{:S(2)}) %collective-permute-start.3) | collective-permute-done | bytes 65568 | tf_op jit(solution)/shard_map/ppermute | solution.py:290
  41.1 1.7 %collective-permute-done.2.refs_1_ = f32[16,1024]{1,0:T(8,128)S(1)} collective-permute-done((f32[16,1024]{1,0:T(8,128)S(1)}, f32[16,1024]{1,0:T(8,128)S(1)}, u32[]{:S(2)}, u32[]{:S(2)}) %collective-permute-start.2) | collective-permute-done | bytes 65568 | tf_op jit(solution)/shard_map/ppermute | solution.py:290
  42.9 0.5 step.3
  43.4 1.0 collective-permute-start.9
  44.3 1.1 collective-permute-start.8
  45.4 0.4 collective-permute-start.7
  45.8 1.9 %collective-permute-start.5 = (bf16[16,512]{1,0:T(8,128)(2,1)S(1)}, bf16[16,512]{1,0:T(8,128)(2,1)S(1)}, u32[]{:S(2)}, u32[]{:S(2)}) collective-permute-start(bf16[16,512]{1,0:T(8,128)(2,1)S(1)} %get-tuple-element.40), channel_id=1, source_target_pairs={{0,16},{16,0},{1,17},{17,1},{2,18},{18,2},{3,19},{19,3},{4,20},{20... | collective-permute-start | bytes 49160 | tf_op jit(solution)/shard_map/ppermute | solution.py:283
  47.7 0.7 collective-permute-done.9.refs_3_
  48.3 2.4 %collective-permute-done.7.refs_1_ = f32[16,1024]{1,0:T(8,128)S(1)} collective-permute-done((f32[16,1024]{1,0:T(8,128)S(1)}, f32[16,1024]{1,0:T(8,128)S(1)}, u32[]{:S(2)}, u32[]{:S(2)}) %collective-permute-start.7) | collective-permute-done | bytes 65568 | tf_op jit(solution)/shard_map/ppermute | solution.py:290
  50.7 2.4 %collective-permute-start.10 = (bf16[16,512]{1,0:T(8,128)(2,1)S(1)}, bf16[16,512]{1,0:T(8,128)(2,1)S(1)}, u32[]{:S(2)}, u32[]{:S(2)}) collective-permute-start(bf16[16,512]{1,0:T(8,128)(2,1)S(1)} %get-tuple-element.45), channel_id=1, source_target_pairs={{0,16},{16,0},{1,17},{17,1},{2,18},{18,2},{3,19},{19,3},{4,20},{20... | collective-permute-start | bytes 49160 | tf_op jit(solution)/shard_map/ppermute | solution.py:283
  53.1 0.8 collective-permute-done.10.refs_3_
  54.1 1.0 copy-done.3
  55.1 2.8 %collective-permute-start.11 = (bf16[16,192,128]{2,1,0:T(8,128)(2,1)S(1)}, bf16[16,192,128]{2,1,0:T(8,128)(2,1)S(1)}, u32[]{:S(2)}, u32[]{:S(2)}) collective-permute-start(bf16[16,192,128]{2,1,0:T(8,128)(2,1)S(1)} %part.2), channel_id=1, source_target_pairs={{0,16},{16,0},{1,17},{17,1},{2,18},{18,2},{3,19},{19,3},{4,20},{20... | collective-permute-start | bytes 2359304 | tf_op jit(solution)/shard_map/ppermute | solution.py:283
  58.0 1.9 %collective-permute-done.11.refs_3_ = bf16[16,192,128]{2,1,0:T(8,128)(2,1)S(1)} collective-permute-done((bf16[16,192,128]{2,1,0:T(8,128)(2,1)S(1)}, bf16[16,192,128]{2,1,0:T(8,128)(2,1)S(1)}, u32[]{:S(2)}, u32[]{:S(2)}) %collective-permute-start.11) | collective-permute-done | bytes 786464 | tf_op jit(solution)/shard_map/ppermute | solution.py:283
  59.9 0.6 step.4.refs_0_.refs_1_
  60.5 1.1 part.3
  61.5 0.4 collective-permute-start.16
  61.9 4.4 %all-to-all-start.1 = ((bf16[16,2,2,16,512]{4,3,2,1,0:T(8,128)(2,1)}), bf16[16,2,2,16,512]{4,3,2,1,0:T(8,128)(2,1)}, u32[]{:S(2)}, u32[]{:S(2)}) async-start(bf16[16,2,2,16,512]{4,3,2,1,0:T(8,128)(2,1)} %copy-done.3), calls=%async_computation.1 | async-start | bytes 2097152 | tf_op jit(solution)/shard_map/all_to_all | solution.py:286
  66.3 2.7 %collective-permute-start.14 = (f32[16,1024]{1,0:T(8,128)S(1)}, f32[16,1024]{1,0:T(8,128)S(1)}, u32[]{:S(2)}, u32[]{:S(2)}) collective-permute-start(f32[16,1024]{1,0:T(8,128)S(1)} %step.4.refs_0_.refs_1_), channel_id=1, source_target_pairs={{0,64},{32,96},{64,0},{96,32},{1,65},{33,97},{65,1},{97,33},{2,66}... | collective-permute-start | bytes 196616 | tf_op jit(solution)/shard_map/ppermute | solution.py:290
  69.1 0.8 collective-permute-start.13
  69.9 0.6 collective-permute-start.12
  70.5 0.5 collective-permute-done.14.refs_3_
  71.0 1.9 %collective-permute-done.13.refs_2_ = f32[16,1024]{1,0:T(8,128)S(1)} collective-permute-done((f32[16,1024]{1,0:T(8,128)S(1)}, f32[16,1024]{1,0:T(8,128)S(1)}, u32[]{:S(2)}, u32[]{:S(2)}) %collective-permute-start.13) | collective-permute-done | bytes 65568 | tf_op jit(solution)/shard_map/ppermute | solution.py:290
  72.9 1.7 %collective-permute-done.12.refs_1_ = f32[16,1024]{1,0:T(8,128)S(1)} collective-permute-done((f32[16,1024]{1,0:T(8,128)S(1)}, f32[16,1024]{1,0:T(8,128)S(1)}, u32[]{:S(2)}, u32[]{:S(2)}) %collective-permute-start.12) | collective-permute-done | bytes 65568 | tf_op jit(solution)/shard_map/ppermute | solution.py:290
  74.7 0.6 step.5.refs_0_
  75.3 1.3 collective-permute-start.19
  76.6 1.0 collective-permute-start.18
  77.6 0.4 collective-permute-start.17
  78.0 1.5 %collective-permute-start.15 = (bf16[16,512]{1,0:T(8,128)(2,1)S(1)}, bf16[16,512]{1,0:T(8,128)(2,1)S(1)}, u32[]{:S(2)}, u32[]{:S(2)}) collective-permute-start(bf16[16,512]{1,0:T(8,128)(2,1)S(1)} %get-tuple-element.53), channel_id=1, source_target_pairs={{0,16},{16,0},{1,17},{17,1},{2,18},{18,2},{3,19},{19,3},{4,20},{20... | collective-permute-start | bytes 49160 | tf_op jit(solution)/shard_map/ppermute | solution.py:283
  79.5 0.7 collective-permute-done.19.refs_3_
  80.4 2.3 %collective-permute-done.17.refs_1_ = f32[16,1024]{1,0:T(8,128)S(1)} collective-permute-done((f32[16,1024]{1,0:T(8,128)S(1)}, f32[16,1024]{1,0:T(8,128)S(1)}, u32[]{:S(2)}, u32[]{:S(2)}) %collective-permute-start.17) | collective-permute-done | bytes 65568 | tf_op jit(solution)/shard_map/ppermute | solution.py:290
  82.6 0.7 close.7
  83.3 2.1 %collective-permute-start.20 = (bf16[16,512]{1,0:T(8,128)(2,1)S(1)}, bf16[16,512]{1,0:T(8,128)(2,1)S(1)}, u32[]{:S(2)}, u32[]{:S(2)}) collective-permute-start(bf16[16,512]{1,0:T(8,128)(2,1)S(1)} %get-tuple-element.57), channel_id=1, source_target_pairs={{0,16},{16,0},{1,17},{17,1},{2,18},{18,2},{3,19},{19,3},{4,20},{20... | collective-permute-start | bytes 49160 | tf_op jit(solution)/shard_map/ppermute | solution.py:283
  85.4 0.8 collective-permute-done.20.refs_3_
  86.2 1.1 bundle.3
  87.3 0.6 copy-done.6
  87.9 0.3 collective-permute-start.21
  88.2 6.7 %all-to-all-start.3 = ((bf16[16,2,2,16,512]{4,3,2,1,0:T(8,128)(2,1)}), bf16[16,2,2,16,512]{4,3,2,1,0:T(8,128)(2,1)S(1)}, u32[]{:S(2)}, u32[]{:S(2)}) async-start(bf16[16,2,2,16,512]{4,3,2,1,0:T(8,128)(2,1)} %get-tuple-element.62), calls=%async_computation.3 | async-start | bytes 2097152 | tf_op jit(solution)/shard_map/all_to_all | solution.py:286
  95.0 1.0 copy-done.8
  96.0 10.7 %trail.2 = (f32[2,1024,512]{2,1,0:T(8,128)}, bf16[2,64,512]{2,1,0:T(8,128)(2,1)}) custom-call(s32[2,4]{1,0:T(2,128)} %refs_0_.7, bf16[2,1024,512]{2,1,0:T(8,128)(2,1)} %refs_1_.1, bf16[16,2,2,16,512]{4,3,2,1,0:T(8,128)(2,1)} %all-to-all-done.1.refs_2_, bf16[16,2,2,16,512]{4,3,2,1,0:T(8,128)(2,1)} %copy-done.8, bf16[2,4,1024,1024]{3,2,1,0:T(8,128)(2,1)} %refs_5_.3, ...), custom_call_target="tpu_custom_call" | custom-call | flops 4294967296 | bytes 8388608 | tf_op jit(solution)/shard_map/trail/pallas_call | solution.py:256
  106.7 5.1 %all-to-all-done.3.refs_2_ = bf16[16,2,2,16,512]{4,3,2,1,0:T(8,128)(2,1)S(1)} async-done(((bf16[16,2,2,16,512]{4,3,2,1,0:T(8,128)(2,1)}), bf16[16,2,2,16,512]{4,3,2,1,0:T(8,128)(2,1)S(1)}, u32[]{:S(2)}, u32[]{:S(2)}) %all-to-all-start.3) | async-done | bytes 1048608 | tf_op jit(solution)/shard_map/all_to_all | solution.py:286
  111.7 1.9 %collective-permute-start.22 = (bf16[16,2,2,16,512]{4,3,2,1,0:T(8,128)(2,1)S(1)}, bf16[16,2,2,16,512]{4,3,2,1,0:T(8,128)(2,1)S(1)}, u32[]{:S(2)}, u32[]{:S(2)}) collective-permute-start(bf16[16,2,2,16,512]{4,3,2,1,0:T(8,128)(2,1)S(1)} %all-to-all-done.3.refs_2_), channel_id=1, source_target_pairs={{0,16},{16,0},{1,17},{17,1},{2,18},{18,2},{3,19},{19,3},{4,20},{20... | collective-permute-start | bytes 3145736 | tf_op jit(solution)/shard_map/ppermute | solution.py:283
  113.6 2.3 %collective-permute-done.22.refs_3_ = bf16[16,2,2,16,512]{4,3,2,1,0:T(8,128)(2,1)S(1)} collective-permute-done((bf16[16,2,2,16,512]{4,3,2,1,0:T(8,128)(2,1)S(1)}, bf16[16,2,2,16,512]{4,3,2,1,0:T(8,128)(2,1)S(1)}, u32[]{:S(2)}, u32[]{:S(2)}) %collective-permute-start.22) | collective-permute-done | bytes 1048608 | tf_op jit(solution)/shard_map/ppermute | solution.py:283
  115.9 1.0 copy-done.9
  116.9 11.1 %trail.3 = (f32[2,1024,512]{2,1,0:T(8,128)}, bf16[4,64,512]{2,1,0:T(8,128)(2,1)}) custom-call(s32[2,4]{1,0:T(2,128)} %refs_0_.7, f32[2,1024,512]{2,1,0:T(8,128)} %get-tuple-element.61.refs_1_, bf16[16,2,2,16,512]{4,3,2,1,0:T(8,128)(2,1)} %copy-done.7, bf16[16,2,2,16,512]{4,3,2,1,0:T(8,128)(2,1)} %copy-done.9, bf16[2,4,1024,1024]{3,2,1,0:T(8,128)(2,1)} %refs_5_.3, ...), custom_call_target="tpu_custom_call" | custom-call | flops 4294967296 | bytes 8388608 | tf_op jit(solution)/shard_map/trail/pallas_call | solution.py:256
  (34 shorter events, 0.6 us)
Async XLA Ops:
  0.6 1.0 copy-start.1
  1.6 0.9 copy-start.4
  2.5 13.6 %copy-start.2 = (bf16[4,4,128,64]{2,3,1,0:T(8,128)(2,1)S(1)}, bf16[4,4,128,64]{2,3,1,0:T(8,128)(2,1)}, u32[]{:S(2)}) copy-start(bf16[4,4,128,64]{2,3,1,0:T(8,128)(2,1)} %param.9) | copy-start | bytes 786436
  2.5 13.6 %copy-start.5 = (f32[4,64,128]{2,1,0:T(8,128)S(1)}, f32[4,64,128]{2,1,0:T(8,128)}, u32[]{:S(2)}) copy-start(f32[4,64,128]{2,1,0:T(8,128)} %refs_0_.5) | copy-start | bytes 393220
  3.5 22.5 %all-to-all-start = ((bf16[16,208,128]{2,1,0:T(8,128)(2,1)}), bf16[16,208,128]{2,1,0:T(8,128)(2,1)S(1)}, u32[]{:S(2)}, u32[]{:S(2)}) async-start(bf16[16,208,128]{2,1,0:T(8,128)(2,1)} %pack.2.refs_2_), calls=%async_computation | async-start | bytes 1703936 | tf_op jit(solution)/shard_map/all_to_all | solution.py:286
  13.8 2.6 %collective-permute-start = (f32[4,16,128]{2,1,0:T(8,128)S(1)}, f32[4,16,128]{2,1,0:T(8,128)S(1)}, u32[]{:S(2)}, u32[]{:S(2)}) collective-permute-start(f32[4,16,128]{2,1,0:T(8,128)S(1)} %bitcast.13), channel_id=1, source_target_pairs={{0,16},{16,0},{1,17},{17,1},{2,18},{18,2},{3,19},{19,3},{4,20},{20... | collective-permute-start | bytes 98312 | tf_op jit(solution)/shard_map/ppermute | solution.py:283
  16.4 9.8 %copy-start = (bf16[16,448,128]{2,1,0:T(8,128)(2,1)}, bf16[16,448,128]{2,1,0:T(8,128)(2,1)S(1)}, u32[]{:S(2)}) copy-start(bf16[16,448,128]{2,1,0:T(8,128)(2,1)S(1)} %pack.3.refs_3_) | copy-start | bytes 5505028
  26.2 28.8 %all-to-all-start.2 = ((bf16[16,448,128]{2,1,0:T(8,128)(2,1)}), bf16[16,448,128]{2,1,0:T(8,128)(2,1)S(1)}, u32[]{:S(2)}, u32[]{:S(2)}) async-start(bf16[16,448,128]{2,1,0:T(8,128)(2,1)} %copy-done), calls=%async_computation.2 | async-start | bytes 3670016 | tf_op jit(solution)/shard_map/all_to_all | solution.py:286
  30.0 12.8 %collective-permute-start.6 = (bf16[16,208,128]{2,1,0:T(8,128)(2,1)S(1)}, bf16[16,208,128]{2,1,0:T(8,128)(2,1)S(1)}, u32[]{:S(2)}, u32[]{:S(2)}) collective-permute-start(bf16[16,208,128]{2,1,0:T(8,128)(2,1)S(1)} %all-to-all-done.refs_1_.refs_2_), channel_id=1, source_target_pairs={{0,16},{16,0},{1,17},{17,1},{2,18},{18,2},{3,19},{19,3},{4,20},{20... | collective-permute-start | bytes 2555912 | tf_op jit(solution)/shard_map/ppermute | solution.py:283
  32.4 2.1 %collective-permute-start.1 = (f32[16,1024]{1,0:T(8,128)S(1)}, f32[16,1024]{1,0:T(8,128)S(1)}, u32[]{:S(2)}, u32[]{:S(2)}) collective-permute-start(f32[16,1024]{1,0:T(8,128)S(1)} %get-tuple-element.36), channel_id=1, source_target_pairs={{0,16},{16,0},{1,17},{17,1},{2,18},{18,2},{3,19},{19,3},{4,20},{20... | collective-permute-start | bytes 196616 | tf_op jit(solution)/shard_map/ppermute | solution.py:283
  34.5 4.7 %collective-permute-start.4 = (f32[16,1024]{1,0:T(8,128)S(1)}, f32[16,1024]{1,0:T(8,128)S(1)}, u32[]{:S(2)}, u32[]{:S(2)}) collective-permute-start(f32[16,1024]{1,0:T(8,128)S(1)} %add.25.refs_0_), channel_id=1, source_target_pairs={{0,64},{32,96},{64,0},{96,32},{1,65},{33,97},{65,1},{97,33},{2,66}... | collective-permute-start | bytes 196616 | tf_op jit(solution)/shard_map/ppermute | solution.py:290
  37.3 3.8 %collective-permute-start.3 = (f32[16,1024]{1,0:T(8,128)S(1)}, f32[16,1024]{1,0:T(8,128)S(1)}, u32[]{:S(2)}, u32[]{:S(2)}) collective-permute-start(f32[16,1024]{1,0:T(8,128)S(1)} %add.25.refs_0_), channel_id=1, source_target_pairs={{0,96},{32,0},{64,32},{96,64},{1,97},{33,1},{65,33},{97,65},{2,98}... | collective-permute-start | bytes 196616 | tf_op jit(solution)/shard_map/ppermute | solution.py:290
  38.2 4.6 %collective-permute-start.2 = (f32[16,1024]{1,0:T(8,128)S(1)}, f32[16,1024]{1,0:T(8,128)S(1)}, u32[]{:S(2)}, u32[]{:S(2)}) collective-permute-start(f32[16,1024]{1,0:T(8,128)S(1)} %add.25.refs_0_), channel_id=1, source_target_pairs={{0,32},{32,64},{64,96},{96,0},{1,33},{33,65},{65,97},{97,1},{2,34}... | collective-permute-start | bytes 196616 | tf_op jit(solution)/shard_map/ppermute | solution.py:290
  43.4 5.0 %collective-permute-start.9 = (f32[16,1024]{1,0:T(8,128)S(1)}, f32[16,1024]{1,0:T(8,128)S(1)}, u32[]{:S(2)}, u32[]{:S(2)}) collective-permute-start(f32[16,1024]{1,0:T(8,128)S(1)} %get-tuple-element.42.refs_0_), channel_id=1, source_target_pairs={{0,64},{32,96},{64,0},{96,32},{1,65},{33,97},{65,1},{97,33},{2,66}... | collective-permute-start | bytes 196616 | tf_op jit(solution)/shard_map/ppermute | solution.py:290
  44.3 4.0 %collective-permute-start.8 = (f32[16,1024]{1,0:T(8,128)S(1)}, f32[16,1024]{1,0:T(8,128)S(1)}, u32[]{:S(2)}, u32[]{:S(2)}) collective-permute-start(f32[16,1024]{1,0:T(8,128)S(1)} %get-tuple-element.42.refs_0_), channel_id=1, source_target_pairs={{0,96},{32,0},{64,32},{96,64},{1,97},{33,1},{65,33},{97,65},{2,98}... | collective-permute-start | bytes 196616 | tf_op jit(solution)/shard_map/ppermute | solution.py:290
  45.4 5.3 %collective-permute-start.7 = (f32[16,1024]{1,0:T(8,128)S(1)}, f32[16,1024]{1,0:T(8,128)S(1)}, u32[]{:S(2)}, u32[]{:S(2)}) collective-permute-start(f32[16,1024]{1,0:T(8,128)S(1)} %get-tuple-element.42.refs_0_), channel_id=1, source_target_pairs={{0,32},{32,64},{64,96},{96,0},{1,33},{33,65},{65,97},{97,1},{2,34}... | collective-permute-start | bytes 196616 | tf_op jit(solution)/shard_map/ppermute | solution.py:290
  45.8 7.4 %collective-permute-start.5 = (bf16[16,512]{1,0:T(8,128)(2,1)S(1)}, bf16[16,512]{1,0:T(8,128)(2,1)S(1)}, u32[]{:S(2)}, u32[]{:S(2)}) collective-permute-start(bf16[16,512]{1,0:T(8,128)(2,1)S(1)} %get-tuple-element.40), channel_id=1, source_target_pairs={{0,16},{16,0},{1,17},{17,1},{2,18},{18,2},{3,19},{19,3},{4,20},{20... | collective-permute-start | bytes 49160 | tf_op jit(solution)/shard_map/ppermute | solution.py:283
  50.7 3.2 %collective-permute-start.10 = (bf16[16,512]{1,0:T(8,128)(2,1)S(1)}, bf16[16,512]{1,0:T(8,128)(2,1)S(1)}, u32[]{:S(2)}, u32[]{:S(2)}) collective-permute-start(bf16[16,512]{1,0:T(8,128)(2,1)S(1)} %get-tuple-element.45), channel_id=1, source_target_pairs={{0,16},{16,0},{1,17},{17,1},{2,18},{18,2},{3,19},{19,3},{4,20},{20... | collective-permute-start | bytes 49160 | tf_op jit(solution)/shard_map/ppermute | solution.py:283
  54.1 1.0 copy-start.3
  55.1 4.8 %collective-permute-start.11 = (bf16[16,192,128]{2,1,0:T(8,128)(2,1)S(1)}, bf16[16,192,128]{2,1,0:T(8,128)(2,1)S(1)}, u32[]{:S(2)}, u32[]{:S(2)}) collective-permute-start(bf16[16,192,128]{2,1,0:T(8,128)(2,1)S(1)} %part.2), channel_id=1, source_target_pairs={{0,16},{16,0},{1,17},{17,1},{2,18},{18,2},{3,19},{19,3},{4,20},{20... | collective-permute-start | bytes 2359304 | tf_op jit(solution)/shard_map/ppermute | solution.py:283
  61.5 13.1 %collective-permute-start.16 = (bf16[16,256,128]{2,1,0:T(8,128)(2,1)}, bf16[16,256,128]{2,1,0:T(8,128)(2,1)S(1)}, u32[]{:S(2)}, u32[]{:S(2)}) collective-permute-start(bf16[16,256,128]{2,1,0:T(8,128)(2,1)} %part.3), channel_id=1, source_target_pairs={{0,16},{16,0},{1,17},{17,1},{2,18},{18,2},{3,19},{19,3},{4,20},{20... | collective-permute-start | bytes 3145736 | tf_op jit(solution)/shard_map/ppermute | solution.py:283
  61.9 26.0 %all-to-all-start.1 = ((bf16[16,2,2,16,512]{4,3,2,1,0:T(8,128)(2,1)}), bf16[16,2,2,16,512]{4,3,2,1,0:T(8,128)(2,1)}, u32[]{:S(2)}, u32[]{:S(2)}) async-start(bf16[16,2,2,16,512]{4,3,2,1,0:T(8,128)(2,1)} %copy-done.3), calls=%async_computation.1 | async-start | bytes 2097152 | tf_op jit(solution)/shard_map/all_to_all | solution.py:286
  66.3 4.7 %collective-permute-start.14 = (f32[16,1024]{1,0:T(8,128)S(1)}, f32[16,1024]{1,0:T(8,128)S(1)}, u32[]{:S(2)}, u32[]{:S(2)}) collective-permute-start(f32[16,1024]{1,0:T(8,128)S(1)} %step.4.refs_0_.refs_1_), channel_id=1, source_target_pairs={{0,64},{32,96},{64,0},{96,32},{1,65},{33,97},{65,1},{97,33},{2,66}... | collective-permute-start | bytes 196616 | tf_op jit(solution)/shard_map/ppermute | solution.py:290
  69.1 3.8 %collective-permute-start.13 = (f32[16,1024]{1,0:T(8,128)S(1)}, f32[16,1024]{1,0:T(8,128)S(1)}, u32[]{:S(2)}, u32[]{:S(2)}) collective-permute-start(f32[16,1024]{1,0:T(8,128)S(1)} %step.4.refs_0_.refs_1_), channel_id=1, source_target_pairs={{0,96},{32,0},{64,32},{96,64},{1,97},{33,1},{65,33},{97,65},{2,98}... | collective-permute-start | bytes 196616 | tf_op jit(solution)/shard_map/ppermute | solution.py:290
  69.9 4.7 %collective-permute-start.12 = (f32[16,1024]{1,0:T(8,128)S(1)}, f32[16,1024]{1,0:T(8,128)S(1)}, u32[]{:S(2)}, u32[]{:S(2)}) collective-permute-start(f32[16,1024]{1,0:T(8,128)S(1)} %step.4.refs_0_.refs_1_), channel_id=1, source_target_pairs={{0,32},{32,64},{64,96},{96,0},{1,33},{33,65},{65,97},{97,1},{2,34}... | collective-permute-start | bytes 196616 | tf_op jit(solution)/shard_map/ppermute | solution.py:290
  75.3 5.0 %collective-permute-start.19 = (f32[16,1024]{1,0:T(8,128)S(1)}, f32[16,1024]{1,0:T(8,128)S(1)}, u32[]{:S(2)}, u32[]{:S(2)}) collective-permute-start(f32[16,1024]{1,0:T(8,128)S(1)} %step.5.refs_0_), channel_id=1, source_target_pairs={{0,64},{32,96},{64,0},{96,32},{1,65},{33,97},{65,1},{97,33},{2,66}... | collective-permute-start | bytes 196616 | tf_op jit(solution)/shard_map/ppermute | solution.py:290
  76.6 3.8 %collective-permute-start.18 = (f32[16,1024]{1,0:T(8,128)S(1)}, f32[16,1024]{1,0:T(8,128)S(1)}, u32[]{:S(2)}, u32[]{:S(2)}) collective-permute-start(f32[16,1024]{1,0:T(8,128)S(1)} %step.5.refs_0_), channel_id=1, source_target_pairs={{0,96},{32,0},{64,32},{96,64},{1,97},{33,1},{65,33},{97,65},{2,98}... | collective-permute-start | bytes 196616 | tf_op jit(solution)/shard_map/ppermute | solution.py:290
  77.6 5.0 %collective-permute-start.17 = (f32[16,1024]{1,0:T(8,128)S(1)}, f32[16,1024]{1,0:T(8,128)S(1)}, u32[]{:S(2)}, u32[]{:S(2)}) collective-permute-start(f32[16,1024]{1,0:T(8,128)S(1)} %step.5.refs_0_), channel_id=1, source_target_pairs={{0,32},{32,64},{64,96},{96,0},{1,33},{33,65},{65,97},{97,1},{2,34}... | collective-permute-start | bytes 196616 | tf_op jit(solution)/shard_map/ppermute | solution.py:290
  78.0 7.3 %collective-permute-start.15 = (bf16[16,512]{1,0:T(8,128)(2,1)S(1)}, bf16[16,512]{1,0:T(8,128)(2,1)S(1)}, u32[]{:S(2)}, u32[]{:S(2)}) collective-permute-start(bf16[16,512]{1,0:T(8,128)(2,1)S(1)} %get-tuple-element.53), channel_id=1, source_target_pairs={{0,16},{16,0},{1,17},{17,1},{2,18},{18,2},{3,19},{19,3},{4,20},{20... | collective-permute-start | bytes 49160 | tf_op jit(solution)/shard_map/ppermute | solution.py:283
  83.3 2.9 %collective-permute-start.20 = (bf16[16,512]{1,0:T(8,128)(2,1)S(1)}, bf16[16,512]{1,0:T(8,128)(2,1)S(1)}, u32[]{:S(2)}, u32[]{:S(2)}) collective-permute-start(bf16[16,512]{1,0:T(8,128)(2,1)S(1)} %get-tuple-element.57), channel_id=1, source_target_pairs={{0,16},{16,0},{1,17},{17,1},{2,18},{18,2},{3,19},{19,3},{4,20},{20... | collective-permute-start | bytes 49160 | tf_op jit(solution)/shard_map/ppermute | solution.py:283
  87.3 0.6 copy-start.6
  87.9 7.1 %collective-permute-start.21 = (bf16[16,2,2,16,512]{4,3,2,1,0:T(8,128)(2,1)}, bf16[16,2,2,16,512]{4,3,2,1,0:T(8,128)(2,1)S(1)}, u32[]{:S(2)}, u32[]{:S(2)}) collective-permute-start(bf16[16,2,2,16,512]{4,3,2,1,0:T(8,128)(2,1)} %all-to-all-done.1.refs_2_), channel_id=1, source_target_pairs={{0,16},{16,0},{1,17},{17,1},{2,18},{18,2},{3,19},{19,3},{4,20},{20... | collective-permute-start | bytes 3145736 | tf_op jit(solution)/shard_map/ppermute | solution.py:283
  88.2 23.5 %all-to-all-start.3 = ((bf16[16,2,2,16,512]{4,3,2,1,0:T(8,128)(2,1)}), bf16[16,2,2,16,512]{4,3,2,1,0:T(8,128)(2,1)S(1)}, u32[]{:S(2)}, u32[]{:S(2)}) async-start(bf16[16,2,2,16,512]{4,3,2,1,0:T(8,128)(2,1)} %get-tuple-element.62), calls=%async_computation.3 | async-start | bytes 2097152 | tf_op jit(solution)/shard_map/all_to_all | solution.py:286
  95.0 1.0 copy-start.8
  111.7 4.2 %copy-start.7 = (bf16[16,2,2,16,512]{4,3,2,1,0:T(8,128)(2,1)}, bf16[16,2,2,16,512]{4,3,2,1,0:T(8,128)(2,1)S(1)}, u32[]{:S(2)}) copy-start(bf16[16,2,2,16,512]{4,3,2,1,0:T(8,128)(2,1)S(1)} %all-to-all-done.3.refs_2_) | copy-start | bytes 3145732
  111.7 4.2 %collective-permute-start.22 = (bf16[16,2,2,16,512]{4,3,2,1,0:T(8,128)(2,1)S(1)}, bf16[16,2,2,16,512]{4,3,2,1,0:T(8,128)(2,1)S(1)}, u32[]{:S(2)}, u32[]{:S(2)}) collective-permute-start(bf16[16,2,2,16,512]{4,3,2,1,0:T(8,128)(2,1)S(1)} %all-to-all-done.3.refs_2_), channel_id=1, source_target_pairs={{0,16},{16,0},{1,17},{17,1},{2,18},{18,2},{3,19},{19,3},{4,20},{20... | collective-permute-start | bytes 3145736 | tf_op jit(solution)/shard_map/ppermute | solution.py:283
  115.9 1.0 copy-start.9

commit v4 on v3

--- a/solution.py
+++ b/solution.py
@@ -12,6 +12,7 @@
 EARLY = ((0, None), (1, None), (1, 0))
 LATE = ((2, None), (2, 0), (2, 1), (3, None), (3, 0), (3, 1), (3, 2))
 REST = 16
+LIMITS = (58, 54)
 
 
 def core_of():
@@ -42,7 +43,7 @@
         scratch_shapes=list(scratch),
         compiler_params=pltpu.CompilerParams(vmem_limit_bytes=limit * MIB),
         cost_estimate=pl.CostEstimate(
-            flops=2**28, bytes_accessed=2**21, transcendentals=0
+            flops=2**20, bytes_accessed=2**16, transcendentals=0
         ),
         name=name,
     )(*operands, *after)
@@ -77,14 +78,22 @@
 
 def pack(members, copies, inverse, across, after=()):
     count = len(members) * inverse.shape[1] + (REST if members[0][0] == 0 else 0)
-    return call(
-        lambda *refs: pack_kernel(members, *refs),
-        jax.ShapeDtypeStruct((copies, count, inverse.shape[2]), jnp.bfloat16),
-        inverse,
-        across,
-        after=after,
+    shape = (copies, count, inverse.shape[2])
+
+    def whole(shape):
+        return pl.BlockSpec(shape, lambda i: (0,) * len(shape))
+
+    held = 2
+    return pl.pallas_call(
+        lambda *refs: pack_kernel(members, *refs[:held], refs[-1]),
+        grid=(1,),
+        in_specs=[whole(inverse.shape), whole(across.shape)]
+        + [pl.BlockSpec(memory_space=pl.ANY)] * len(after),
+        out_specs=pl.BlockSpec(memory_space=pltpu.VMEM),
+        out_shape=jax.ShapeDtypeStruct(shape, jnp.bfloat16),
+        compiler_params=pltpu.CompilerParams(vmem_limit_bytes=24 * MIB),
         name="pack",
-    )
+    )(inverse, across, *after)
 
 
 def block_of(ref, at, size):
@@ -118,11 +127,30 @@
         out_ref,
         False,
     )
-    core = core_of()
     count = keep_ref.shape[0]
-    keep_ref[...] = out_ref[pl.ds(pl.multiple_of(core * count, count), count)]
-    give_ref[...] = out_ref[pl.ds(pl.multiple_of((1 - core) * count, count), count)]
+    keep_ref[...] = out_ref[:count]
+    give_ref[...] = out_ref[count:]
     mark_ref[...] = right_ref[: mark_ref.shape[0]]
+
+
+def split_step_kernel(
+    column, size, state_ref, solved_ref, got_ref, right_ref, group_ref, keep_ref, give_ref, out_ref
+):
+    right = right_ref[...]
+    for i in range(column):
+        both = jnp.concatenate([solved_ref[i], got_ref[i]], axis=0)
+        right = right - dot(both, block_of(group_ref, (1 + i) * size, size), NN)
+    apply_inverse(
+        right,
+        block_of(group_ref, 0, size),
+        state_ref[state_ref.shape[0] - 1, 0, column : column + 1],
+        slab_of(core_of()),
+        out_ref,
+        False,
+    )
+    count = keep_ref.shape[0]
+    keep_ref[...] = out_ref[:count]
+    give_ref[...] = out_ref[count:]
 
 
 def part_kernel(start, group_ref, out_ref):
@@ -140,15 +168,9 @@
     )
 
 
-def halves(solved_ref, core, keep_ref, give_ref):
-    half = keep_ref.shape[1]
-    keep_ref[...] = solved_ref[:, pl.ds(pl.multiple_of(core * half, half), half)]
-    give_ref[...] = solved_ref[:, pl.ds(pl.multiple_of((1 - core) * half, half), half)]
-
-
-def close_kernel(n_parts, *refs):
-    part_refs, before_refs = refs[:n_parts], refs[n_parts:-4]
-    solved_ref, keep_ref, give_ref, mark_ref = refs[-4:]
+def close_kernel(n_parts, n_before, *refs):
+    part_refs, before_refs = refs[:n_parts], refs[n_parts : n_parts + n_before]
+    solved_ref, mark_ref, *bundle_refs = refs[n_parts + n_before :]
     total = part_refs[0][...]
     for part_ref in part_refs[1:]:
         total = total + part_ref[...]
@@ -156,8 +178,11 @@
     for ref in before_refs:
         solved_ref[:last] = ref[...]
     solved_ref[last] = total.astype(jnp.bfloat16)
-    halves(solved_ref.at[last], core_of(), keep_ref, give_ref)
     mark_ref[...] = total[: mark_ref.shape[0], : mark_ref.shape[1]]
+    for ref in bundle_refs:
+        both = solved_ref[last - 1 :]
+        for copy in range(ref.shape[0]):
+            ref[copy] = both
 
 
 def step_kernel(column, starts, size, state_ref, solved_ref, *refs):
@@ -187,58 +212,41 @@
         )
 
 
-def bundle_kernel(*refs):
-    core = core_of()
-    out_ref, mark_ref = refs[-2:]
-    for k in range(len(refs) // 2 - 1):
-        keep, got = refs[2 * k][...], refs[2 * k + 1][...]
-        for copy in range(out_ref.shape[0]):
-            out_ref[copy, k, core] = keep
-            out_ref[copy, k, 1 - core] = got
-    mark_ref[...] = jnp.zeros(mark_ref.shape, mark_ref.dtype)
-
-
 def trail_kernel(columns, before, pattern_ref, base_ref, mine_ref, other_ref, *refs):
     count = len(columns)
     factor_refs, (out_ref, own_ref) = refs[:count], refs[-2:]
     row = pl.program_id(0)
-    core = core_of()
-    width, half = out_ref.shape[2], mine_ref.shape[4]
-    offsets = [
-        pl.multiple_of(core * half, half),
-        pl.multiple_of((1 - core) * half, half),
-    ]
+    half, depth = out_ref.shape[2] // 2, mine_ref.shape[3]
+    sides = []
+    for ref, core in ((mine_ref, core_of()), (other_ref, 1 - core_of())):
+        sides.append((ref, pl.ds(pl.multiple_of(core * half, half), half)))
 
     def solved(ref, k):
-        return ref[:, k].reshape(width, half)
-
-    total = base_ref[0].astype(jnp.float32)
-    for k, column in enumerate(columns):
-        product = None
-        for ref, offset in zip((mine_ref, other_ref), offsets):
-            factor = factor_refs[k][0, 0, :, pl.ds(offset, half)]
-            term = dot(factor, solved(ref, k), NT)
-            product = term if product is None else product + term
-        total = total - pattern_ref[row, column].astype(jnp.float32) * product
-    out_ref[0] = total
+        return ref[:, k].reshape(half, depth)
+
+    for ref, lanes in sides:
+        total = base_ref[0, :, lanes].astype(jnp.float32)
+        for k, column in enumerate(columns):
+            product = dot(factor_refs[k][0, 0], solved(ref, k), NT)
+            total = total - pattern_ref[row, column].astype(jnp.float32) * product
+        out_ref[0, :, lanes] = total
 
     @pl.when((row == 0) & (pl.program_id(1) == 0))
     def _():
         own = own_ref.shape[1]
-        lane = lax.broadcasted_iota(jnp.int32, (own, half), 1)
-        wanted = lax.broadcasted_iota(jnp.int32, (own, half), 0) + col_of() * own
+        lane = lax.broadcasted_iota(jnp.int32, (own, depth), 1)
+        wanted = lax.broadcasted_iota(jnp.int32, (own, depth), 0) + col_of() * own
+        pick = (lane == wanted).astype(jnp.bfloat16)
         if before:
             own_ref[:before] = refs[count][...]
         for k in range(count):
-            rows = None
-            for ref, offset in zip((mine_ref, other_ref), offsets):
-                pick = (lane + offset == wanted).astype(jnp.bfloat16)
-                term = dot(pick, solved(ref, k), NT)
-                rows = term if rows is None else rows + term
-            own_ref[before + k] = rows.astype(jnp.bfloat16)
-
-
-def trail(columns, pattern, base, factor, mine, other, own, tile, done=(), after=()):
+            for ref, lanes in sides:
+                own_ref[before + k, :, lanes] = dot(pick, solved(ref, k), NT).astype(
+                    jnp.bfloat16
+                )
+
+
+def trail(columns, pattern, base, factor, mine, other, own, tile, limit, done=(), after=()):
     n_rows, height, width = base.shape
     depth = factor.shape[-1]
     count, before = len(columns), sum(d.shape[0] for d in done)
@@ -256,7 +264,7 @@
     return pl.pallas_call(
         lambda *refs: trail_kernel(columns, before, *refs[:held], *refs[-2:]),
         grid=(n_rows, height // tile),
-        in_specs=[smem, row_tile, whole(mine.shape), whole(other.shape)]
+        in_specs=[smem, row_tile] + [pl.BlockSpec(memory_space=pltpu.VMEM)] * 2
         + [factor_spec(column) for column in columns]
         + [whole(d.shape) for d in done]
         + [pl.BlockSpec(memory_space=pl.ANY)] * len(after),
@@ -265,7 +273,7 @@
             jax.ShapeDtypeStruct(base.shape, jnp.float32),
             jax.ShapeDtypeStruct(own_shape, jnp.bfloat16),
         ],
-        compiler_params=pltpu.CompilerParams(vmem_limit_bytes=58 * MIB),
+        compiler_params=pltpu.CompilerParams(vmem_limit_bytes=limit * MIB),
         cost_estimate=pl.CostEstimate(
             flops=2 * n_rows * height * width * depth * count,
             bytes_accessed=2 * n_rows * height * depth * count,
@@ -304,23 +312,22 @@
         packed = pack(EARLY, n_col, inverse, across)
         early = exchange(packed)
         packed_late = pack(LATE, n_col, inverse, across, after=[packed])
-        right = lax.dynamic_slice(
-            rhs, (0, 0, col * n_core * share), (columns, height, n_core * share)
-        ).transpose(0, 2, 1)
-        rights = [
-            lax.dynamic_slice(right, (0, which * share, 0), (columns, share, height))
-            for which in (core, 1 - core)
-        ]
-        rights = jnp.stack([rights[0], swap(rights[1])], axis=1)
+        def columns_of(which):
+            at = (which * n_col + col) * share
+            return lax.dynamic_slice(
+                rhs, (0, 0, at), (columns, height, share)
+            ).transpose(0, 2, 1)
+
+        mine, theirs = columns_of(core), columns_of(1 - core)
+        rights = jnp.stack([mine, swap(theirs)], axis=1)
+        right = jnp.concatenate([mine[0], theirs[0]])
 
         partial_shape = jax.ShapeDtypeStruct((share, block), jnp.float32)
-        half_shape = jax.ShapeDtypeStruct((share, block // n_core), jnp.bfloat16)
         mark_shape = jax.ShapeDtypeStruct((8, 128), jnp.float32)
-        early_both = (early, swap(early))
         keep, give, mark = call(
             lambda *refs: first_kernel(size, *refs),
             (partial_shape, partial_shape, mark_shape),
-            right[0],
+            right,
             early,
             scratch=[pltpu.VMEM((n_core * share, block), jnp.float32)],
             after=[rights, packed_late],
@@ -329,43 +336,44 @@
         packed_late, mark = tied((packed_late, mark))
         late = exchange(packed_late)
         partial_sum = keep + swap(give)
-
-        def send(halves_of, after):
-            shape = (n_col, len(halves_of) // 2, n_core, share, block // n_core)
-            bundle, mark = call(
-                bundle_kernel,
-                (jax.ShapeDtypeStruct(shape, jnp.bfloat16), mark_shape),
-                    *halves_of,
-                after=after,
-                name="bundle",
-            )
-            return exchange(bundle), mark
-
-        state, solved, sent = rights, [], []
+        early_part = part(early, size, 2 * size + REST, [partial_sum])
+
+        state, solved = rights, []
+        bundle_shape = jax.ShapeDtypeStruct((n_col, 2, share, block), jnp.bfloat16)
         for column in range(1, columns + 1):
             parts = parts_over_x(partial_sum)
-            *solved, keep, give, mark = call(
-                lambda *refs: close_kernel(n_x, *refs),
-                (
-                    jax.ShapeDtypeStruct((column, share, block), jnp.bfloat16),
-                    half_shape,
-                    half_shape,
-                    mark_shape,
-                ),
+            now, mark, *bundle = call(
+                lambda *refs, n=len(solved): close_kernel(n_x, n, *refs),
+                [jax.ShapeDtypeStruct((column, share, block), jnp.bfloat16), mark_shape]
+                + [bundle_shape] * (column % 2 == 0),
                 *parts,
                 *solved,
                 after=[mark],
                 name="close",
             )
-            sent += [keep, swap(give)]
+            solved = [now]
+            if column == 4:
+                first_pair, mark = tied((first_pair, mark))
             if column == columns:
                 break
             if column == 1:
-                group, starts = early_both, (size, size)
+                group, starts = (early, swap(early_part)), (size, 0)
             elif column == 2:
-                first_pair, sent_mark = send(sent, [])
-                group = (late, swap(part(late, 0, 3 * size, [mark, sent_mark])))
-                starts = (0, 0)
+                first_pair = exchange(bundle[0])
+                keep, give = call(
+                    lambda *refs: split_step_kernel(2, size, *refs),
+                    (partial_shape, partial_shape),
+                    state,
+                    now,
+                    swap(now),
+                    jnp.concatenate([mine[2], theirs[2]]),
+                    late,
+                    scratch=[pltpu.VMEM((n_core * share, block), jnp.float32)],
+                    name="split",
+                )
+                partial_sum = keep + swap(give)
+                other = swap(part(late, 3 * size, 4 * size, [partial_sum]))
+                continue
             else:
                 group, starts = (late, other), (3 * size, 0)
             outs = [partial_shape]
@@ -381,11 +389,8 @@
             )
             if column == 1:
                 (state,) = more
-            if column == 2:
-                other = swap(part(late, 3 * size, 4 * size, [partial_sum]))
-
-        second_pair, mark = send(sent[4:], [])
-        first_pair, mark = tied((first_pair, mark))
+
+        second_pair = exchange(bundle[0])
         base, blocks = trail(
             (0, 1),
             pattern,
@@ -395,6 +400,7 @@
             swap(first_pair),
             size,
             512,
+            LIMITS[0],
             after=[mark],
         )
         second_pair, blocks = tied((second_pair, blocks))
@@ -407,6 +413,7 @@
             swap(second_pair),
             size,
             512,
+            LIMITS[1],
             (blocks,),
         )
         return blocks, updated

time: 129 us -> 126 us (0.977)
  waiting for transfers between devices: 36.7 us -> 40.1 us
  starting transfers between devices: 54 us -> 51.3 us
  local copies, waits for them, and re-layouts: 8.32 us -> 5.84 us
    ppermute x12, waiting for transfers between devices: 14.2 us -> 17.6 us  [parts_over_x(): lax.ppermute(value, 'x', [(i, (i + k) % n_x) for i in range(n_x)])]
    ppermute x11 -> x8, starting transfers between devices: 16.8 us -> 14 us  [swap(): lax.ppermute(value, 'core', [(i, n_core - 1 - i) for i in range(n_core)])]
    ppermute x11 -> x8, waiting for transfers between devices: 7.89 us -> 5.4 us  [swap(): lax.ppermute(value, 'core', [(i, n_core - 1 - i) for i in range(n_core)])]
    all_to_all x4, waiting for transfers between devices: 14.6 us -> 17 us  [exchange(): return lax.all_to_all(value, ('z', 'y'), 0, 0)]
    pallas_call x14 -> x10, Pallas kernels: 6.29 us -> 4.05 us  [call(): pl.pallas_call(lambda *refs: kernel(*refs[:count], *refs[count + len(afte...]
    another operation x1, local copies, waits for them, and re-layouts: 1.55 us -> 0.01 us  [per_device(): rights = jnp.stack([mine, swap(theirs)], axis=1)]
    pallas_call x0 -> x2, Pallas kernels: none -> 1.32 us  [pack(): pl.pallas_call(lambda *refs: pack_kernel(members, *refs[:held], refs[-1])...]
    unnamed x23 -> x22, local copies, waits for them, and re-layouts: 5.69 us -> 4.59 us
  transfers between devices with their start and end apart: 27 -> 24, of which waited for: 18 -> 20; matrix products, arithmetic and copies ran while one was open for 2% -> 1% of each run, Pallas kernels for 11% -> 11%
where the time goes in v4:
time: 126 us; the launch traced here: 125 us
  starting transfers between devices  51.3 us (41%)
  waiting for transfers between devices  40.1 us (32%)
  Pallas kernels  27 us (21%)
  local copies, waits for them, and re-layouts  5.84 us (5%)
    all_to_all x4, starting transfers between devices, exchange(): return lax.all_to_all(value, ('z', 'y'), 0, 0)  23.5 us
    pallas_call x2, Pallas kernels, trail(): pl.pallas_call(lambda *refs: trail_kernel(columns, before, *refs[:held],...  21.7 us
    ppermute x12, waiting for transfers between devices, parts_over_x(): lax.ppermute(value, 'x', [(i, (i + k) % n_x) for i in range(n_x)])  17.6 us
    all_to_all x4, waiting for transfers between devices, exchange(): return lax.all_to_all(value, ('z', 'y'), 0, 0)  17 us
    ppermute x8, starting transfers between devices, swap(): lax.ppermute(value, 'core', [(i, n_core - 1 - i) for i in range(n_core)])  14 us
    ppermute x12, starting transfers between devices, parts_over_x(): lax.ppermute(value, 'x', [(i, (i + k) % n_x) for i in range(n_x)])  13.9 us
    ppermute x8, waiting for transfers between devices, swap(): lax.ppermute(value, 'core', [(i, n_core - 1 - i) for i in range(n_core)])  5.4 us
    unnamed x22, local copies, waits for them, and re-layouts  4.59 us
  transfers between devices with their start and end apart: 24, of which 20 were waited for; matrix products, arithmetic and copies ran while one was open for 1% of the time, Pallas kernels for 11%

profile of v4, /device:TPU:1, one launch (start us, length us, event | category | flops | bytes accessed | tf_op | source)
XLA Modules:
  0.0 125.1 jit_solution(3923881626700057046)
XLA Ops:
  0.6 0.9 copy-done.1
  1.6 0.9 copy-done.4
  2.5 1.0 pack.2.refs_2_
  3.5 8.6 %all-to-all-start = ((bf16[16,208,128]{2,1,0:T(8,128)(2,1)}), bf16[16,208,128]{2,1,0:T(8,128)(2,1)S(1)}, u32[]{:S(2)}, u32[]{:S(2)}) async-start(bf16[16,208,128]{2,1,0:T(8,128)(2,1)} %pack.2.refs_2_), calls=%async_computation | async-start | bytes 1703936 | tf_op jit(solution)/shard_map/all_to_all | solution.py:294
  12.1 1.2 constant_dynamic-slice_fusion.1
  13.4 0.1 copy.13
  13.5 1.0 collective-permute-start
  14.5 0.1 copy.12
  14.6 0.3 pack.3.refs_3_
  14.9 0.4 collective-permute-done
  15.4 10.6 %all-to-all-done.refs_1_.refs_0_.refs_2_ = bf16[16,208,128]{2,1,0:T(8,128)(2,1)S(1)} async-done(((bf16[16,208,128]{2,1,0:T(8,128)(2,1)}), bf16[16,208,128]{2,1,0:T(8,128)(2,1)S(1)}, u32[]{:S(2)}, u32[]{:S(2)}) %all-to-all-start) | async-done | bytes 852000 | tf_op jit(solution)/shard_map/all_to_all | solution.py:294
  26.0 0.2 first.1
  26.2 3.8 %all-to-all-start.2 = ((bf16[16,448,128]{2,1,0:T(8,128)(2,1)}), bf16[16,448,128]{2,1,0:T(8,128)(2,1)S(1)}, u32[]{:S(2)}, u32[]{:S(2)}) async-start(bf16[16,448,128]{2,1,0:T(8,128)(2,1)} %copy-done), calls=%async_computation.2 | async-start | bytes 3670016 | tf_op jit(solution)/shard_map/all_to_all | solution.py:294
  30.0 2.4 %collective-permute-start.1 = (f32[16,1024]{1,0:T(8,128)S(1)}, f32[16,1024]{1,0:T(8,128)S(1)}, u32[]{:S(2)}, u32[]{:S(2)}) collective-permute-start(f32[16,1024]{1,0:T(8,128)S(1)} %get-tuple-element.29), channel_id=1, source_target_pairs={{0,16},{16,0},{1,17},{17,1},{2,18},{18,2},{3,19},{19,3},{4,20},{20... | collective-permute-start | bytes 196616 | tf_op jit(solution)/shard_map/ppermute | solution.py:291
  32.4 0.9 collective-permute-done.1
  33.4 0.4 collective-permute-start.5
  33.8 2.7 %collective-permute-start.4 = (f32[16,1024]{1,0:T(8,128)S(1)}, f32[16,1024]{1,0:T(8,128)S(1)}, u32[]{:S(2)}, u32[]{:S(2)}) collective-permute-start(f32[16,1024]{1,0:T(8,128)S(1)} %add.26.refs_0_.refs_1_), channel_id=1, source_target_pairs={{0,64},{32,96},{64,0},{96,32},{1,65},{33,97},{65,1},{97,33},{2,66}... | collective-permute-start | bytes 196616 | tf_op jit(solution)/shard_map/ppermute | solution.py:298
  36.5 0.9 collective-permute-start.3
  37.4 0.6 collective-permute-start.2
  38.0 0.8 collective-permute-done.4.refs_3_
  38.8 1.4 %collective-permute-done.3.refs_2_ = f32[16,1024]{1,0:T(8,128)S(1)} collective-permute-done((f32[16,1024]{1,0:T(8,128)S(1)}, f32[16,1024]{1,0:T(8,128)S(1)}, u32[]{:S(2)}, u32[]{:S(2)}) %collective-permute-start.3) | collective-permute-done | bytes 65568 | tf_op jit(solution)/shard_map/ppermute | solution.py:298
  40.3 1.7 %collective-permute-done.2.refs_1_ = f32[16,1024]{1,0:T(8,128)S(1)} collective-permute-done((f32[16,1024]{1,0:T(8,128)S(1)}, f32[16,1024]{1,0:T(8,128)S(1)}, u32[]{:S(2)}, u32[]{:S(2)}) %collective-permute-start.2) | collective-permute-done | bytes 65568 | tf_op jit(solution)/shard_map/ppermute | solution.py:298
  42.0 0.5 step.2
  42.5 1.2 collective-permute-start.8
  43.8 1.1 collective-permute-start.7
  44.8 0.4 collective-permute-start.6
  45.2 2.3 %collective-permute-done.8.refs_3_ = f32[16,1024]{1,0:T(8,128)S(1)} collective-permute-done((f32[16,1024]{1,0:T(8,128)S(1)}, f32[16,1024]{1,0:T(8,128)S(1)}, u32[]{:S(2)}, u32[]{:S(2)}) %collective-permute-start.8) | collective-permute-done | bytes 65568 | tf_op jit(solution)/shard_map/ppermute | solution.py:298
  47.5 0.2 collective-permute-done.7.refs_2_
  47.8 2.4 %collective-permute-done.6.refs_1_ = f32[16,1024]{1,0:T(8,128)S(1)} collective-permute-done((f32[16,1024]{1,0:T(8,128)S(1)}, f32[16,1024]{1,0:T(8,128)S(1)}, u32[]{:S(2)}, u32[]{:S(2)}) %collective-permute-start.6) | collective-permute-done | bytes 65568 | tf_op jit(solution)/shard_map/ppermute | solution.py:298
  50.2 0.1 close.5
  50.3 1.9 %collective-permute-start.9 = (bf16[2,16,1024]{2,1,0:T(8,128)(2,1)S(1)}, bf16[2,16,1024]{2,1,0:T(8,128)(2,1)S(1)}, u32[]{:S(2)}, u32[]{:S(2)}) collective-permute-start(bf16[2,16,1024]{2,1,0:T(8,128)(2,1)S(1)} %get-tuple-element.37.refs_1_.refs_4_), channel_id=1, source_target_pairs={{0,16},{16,0},{1,17},{17,1},{2,18},{18,2},{3,19},{19,3},{4,20},{20... | collective-permute-start | bytes 196616 | tf_op jit(solution)/shard_map/ppermute | solution.py:291
  52.2 0.9 collective-permute-done.9.refs_2_
  53.1 0.0 all-to-all-done.2.refs_4_.refs_0_.refs_2_
  53.2 0.4 split.1
  53.6 4.8 %collective-permute-start.10 = (f32[16,1024]{1,0:T(8,128)S(1)}, f32[16,1024]{1,0:T(8,128)S(1)}, u32[]{:S(2)}, u32[]{:S(2)}) collective-permute-start(f32[16,1024]{1,0:T(8,128)S(1)} %get-tuple-element.40), channel_id=1, source_target_pairs={{0,16},{16,0},{1,17},{17,1},{2,18},{18,2},{3,19},{19,3},{4,20},{20... | collective-permute-start | bytes 196616 | tf_op jit(solution)/shard_map/ppermute | solution.py:291
  58.3 0.9 collective-permute-done.10
  59.2 1.0 part.3
  60.3 0.4 collective-permute-start.14
  60.6 4.3 %all-to-all-start.1 = ((bf16[16,2,16,1024]{3,2,1,0:T(8,128)(2,1)}), bf16[16,2,16,1024]{3,2,1,0:T(8,128)(2,1)}, u32[]{:S(2)}, u32[]{:S(2)}) async-start(bf16[16,2,16,1024]{3,2,1,0:T(8,128)(2,1)} %copy-done.3), calls=%async_computation.1 | async-start | bytes 2097152 | tf_op jit(solution)/shard_map/all_to_all | solution.py:294
  65.0 2.8 %collective-permute-start.13 = (f32[16,1024]{1,0:T(8,128)S(1)}, f32[16,1024]{1,0:T(8,128)S(1)}, u32[]{:S(2)}, u32[]{:S(2)}) collective-permute-start(f32[16,1024]{1,0:T(8,128)S(1)} %add.27.refs_0_.refs_1_), channel_id=1, source_target_pairs={{0,64},{32,96},{64,0},{96,32},{1,65},{33,97},{65,1},{97,33},{2,66}... | collective-permute-start | bytes 196616 | tf_op jit(solution)/shard_map/ppermute | solution.py:298
  67.8 0.8 collective-permute-start.12
  68.6 0.6 collective-permute-start.11
  69.3 0.8 collective-permute-done.13.refs_3_
  70.1 1.5 %collective-permute-done.12.refs_2_ = f32[16,1024]{1,0:T(8,128)S(1)} collective-permute-done((f32[16,1024]{1,0:T(8,128)S(1)}, f32[16,1024]{1,0:T(8,128)S(1)}, u32[]{:S(2)}, u32[]{:S(2)}) %collective-permute-start.12) | collective-permute-done | bytes 65568 | tf_op jit(solution)/shard_map/ppermute | solution.py:298
  71.6 1.7 %collective-permute-done.11.refs_1_ = f32[16,1024]{1,0:T(8,128)S(1)} collective-permute-done((f32[16,1024]{1,0:T(8,128)S(1)}, f32[16,1024]{1,0:T(8,128)S(1)}, u32[]{:S(2)}, u32[]{:S(2)}) %collective-permute-start.11) | collective-permute-done | bytes 65568 | tf_op jit(solution)/shard_map/ppermute | solution.py:298
  73.4 0.6 step.3.refs_0_
  74.0 1.2 collective-permute-start.17
  75.3 1.0 collective-permute-start.16
  76.3 0.4 collective-permute-start.15
  76.7 2.1 %collective-permute-done.17.refs_3_ = f32[16,1024]{1,0:T(8,128)S(1)} collective-permute-done((f32[16,1024]{1,0:T(8,128)S(1)}, f32[16,1024]{1,0:T(8,128)S(1)}, u32[]{:S(2)}, u32[]{:S(2)}) %collective-permute-start.17) | collective-permute-done | bytes 65568 | tf_op jit(solution)/shard_map/ppermute | solution.py:298
  78.9 0.2 collective-permute-done.16.refs_2_
  79.1 2.3 %collective-permute-done.15.refs_1_ = f32[16,1024]{1,0:T(8,128)S(1)} collective-permute-done((f32[16,1024]{1,0:T(8,128)S(1)}, f32[16,1024]{1,0:T(8,128)S(1)}, u32[]{:S(2)}, u32[]{:S(2)}) %collective-permute-start.15) | collective-permute-done | bytes 65568 | tf_op jit(solution)/shard_map/ppermute | solution.py:298
  81.3 1.1 close.7
  82.5 0.6 copy-done.6
  83.0 0.4 all-to-all-done.1.refs_2_
  83.4 1.7 %collective-permute-start.18 = (bf16[16,2,16,1024]{3,2,1,0:T(8,128)(2,1)}, bf16[16,2,16,1024]{3,2,1,0:T(8,128)(2,1)S(1)}, u32[]{:S(2)}, u32[]{:S(2)}) collective-permute-start(bf16[16,2,16,1024]{3,2,1,0:T(8,128)(2,1)} %all-to-all-done.1.refs_2_), channel_id=1, source_target_pairs={{0,16},{16,0},{1,17},{17,1},{2,18},{18,2},{3,19},{19,3},{4,20},{20... | collective-permute-start | bytes 3145736 | tf_op jit(solution)/shard_map/ppermute | solution.py:291
  85.1 6.7 %all-to-all-start.3 = ((bf16[16,2,16,1024]{3,2,1,0:T(8,128)(2,1)}), bf16[16,2,16,1024]{3,2,1,0:T(8,128)(2,1)S(1)}, u32[]{:S(2)}, u32[]{:S(2)}) async-start(bf16[16,2,16,1024]{3,2,1,0:T(8,128)(2,1)} %get-tuple-element.48), calls=%async_computation.3 | async-start | bytes 2097152 | tf_op jit(solution)/shard_map/all_to_all | solution.py:294
  91.9 1.0 copy-done.8
  92.9 10.6 %trail.2 = (f32[2,1024,512]{2,1,0:T(8,128)}, bf16[2,64,512]{2,1,0:T(8,128)(2,1)}) custom-call(s32[2,4]{1,0:T(2,128)} %refs_0_.7, bf16[2,1024,512]{2,1,0:T(8,128)(2,1)} %refs_1_.1, bf16[16,2,16,1024]{3,2,1,0:T(8,128)(2,1)} %all-to-all-done.1.refs_2_, bf16[16,2,16,1024]{3,2,1,0:T(8,128)(2,1)} %copy-done.8, bf16[2,4,1024,1024]{3,2,1,0:T(8,128)(2,1)} %refs_5_.3, ...), custom_call_target="tpu_custom_call" | custom-call | flops 4294967296 | bytes 8388608 | tf_op jit(solution)/shard_map/trail/pallas_call | solution.py:264
  103.5 5.9 %all-to-all-done.3.refs_2_ = bf16[16,2,16,1024]{3,2,1,0:T(8,128)(2,1)S(1)} async-done(((bf16[16,2,16,1024]{3,2,1,0:T(8,128)(2,1)}), bf16[16,2,16,1024]{3,2,1,0:T(8,128)(2,1)S(1)}, u32[]{:S(2)}, u32[]{:S(2)}) %all-to-all-start.3) | async-done | bytes 1048608 | tf_op jit(solution)/shard_map/all_to_all | solution.py:294
  109.4 1.4 %collective-permute-start.19 = (bf16[16,2,16,1024]{3,2,1,0:T(8,128)(2,1)S(1)}, bf16[16,2,16,1024]{3,2,1,0:T(8,128)(2,1)S(1)}, u32[]{:S(2)}, u32[]{:S(2)}) collective-permute-start(bf16[16,2,16,1024]{3,2,1,0:T(8,128)(2,1)S(1)} %all-to-all-done.3.refs_2_), channel_id=1, source_target_pairs={{0,16},{16,0},{1,17},{17,1},{2,18},{18,2},{3,19},{19,3},{4,20},{20... | collective-permute-start | bytes 3145736 | tf_op jit(solution)/shard_map/ppermute | solution.py:291
  110.8 2.3 %collective-permute-done.19.refs_3_ = bf16[16,2,16,1024]{3,2,1,0:T(8,128)(2,1)S(1)} collective-permute-done((bf16[16,2,16,1024]{3,2,1,0:T(8,128)(2,1)S(1)}, bf16[16,2,16,1024]{3,2,1,0:T(8,128)(2,1)S(1)}, u32[]{:S(2)}, u32[]{:S(2)}) %collective-permute-start.19) | collective-permute-done | bytes 1048608 | tf_op jit(solution)/shard_map/ppermute | solution.py:291
  113.1 1.0 copy-done.9
  114.1 11.0 %trail.3 = (f32[2,1024,512]{2,1,0:T(8,128)}, bf16[4,64,512]{2,1,0:T(8,128)(2,1)}) custom-call(s32[2,4]{1,0:T(2,128)} %refs_0_.7, f32[2,1024,512]{2,1,0:T(8,128)} %get-tuple-element.47.refs_1_, bf16[16,2,16,1024]{3,2,1,0:T(8,128)(2,1)} %copy-done.7, bf16[16,2,16,1024]{3,2,1,0:T(8,128)(2,1)} %copy-done.9, bf16[2,4,1024,1024]{3,2,1,0:T(8,128)(2,1)} %refs_5_.3, ...), custom_call_target="tpu_custom_call" | custom-call | flops 4294967296 | bytes 8388608 | tf_op jit(solution)/shard_map/trail/pallas_call | solution.py:264
  (29 shorter events, 0.2 us)
Async XLA Ops:
  0.6 1.0 copy-start.1
  1.6 0.9 copy-start.4
  2.5 12.1 %copy-start.2 = (bf16[4,4,128,64]{2,3,1,0:T(8,128)(2,1)S(1)}, bf16[4,4,128,64]{2,3,1,0:T(8,128)(2,1)}, u32[]{:S(2)}) copy-start(bf16[4,4,128,64]{2,3,1,0:T(8,128)(2,1)} %param.9) | copy-start | bytes 786436
  2.5 12.1 %copy-start.5 = (f32[4,64,128]{2,1,0:T(8,128)S(1)}, f32[4,64,128]{2,1,0:T(8,128)}, u32[]{:S(2)}) copy-start(f32[4,64,128]{2,1,0:T(8,128)} %refs_0_.5) | copy-start | bytes 393220
  3.5 22.5 %all-to-all-start = ((bf16[16,208,128]{2,1,0:T(8,128)(2,1)}), bf16[16,208,128]{2,1,0:T(8,128)(2,1)S(1)}, u32[]{:S(2)}, u32[]{:S(2)}) async-start(bf16[16,208,128]{2,1,0:T(8,128)(2,1)} %pack.2.refs_2_), calls=%async_computation | async-start | bytes 1703936 | tf_op jit(solution)/shard_map/all_to_all | solution.py:294
  13.5 1.9 %collective-permute-start = (f32[4,16,128]{2,1,0:T(8,128)S(1)}, f32[4,16,128]{2,1,0:T(8,128)S(1)}, u32[]{:S(2)}, u32[]{:S(2)}) collective-permute-start(f32[4,16,128]{2,1,0:T(8,128)S(1)} %bitcast.18), channel_id=1, source_target_pairs={{0,16},{16,0},{1,17},{17,1},{2,18},{18,2},{3,19},{19,3},{4,20},{20... | collective-permute-start | bytes 98312 | tf_op jit(solution)/shard_map/ppermute | solution.py:291
  14.9 11.3 %copy-start = (bf16[16,448,128]{2,1,0:T(8,128)(2,1)}, bf16[16,448,128]{2,1,0:T(8,128)(2,1)S(1)}, u32[]{:S(2)}) copy-start(bf16[16,448,128]{2,1,0:T(8,128)(2,1)S(1)} %pack.3.refs_3_) | copy-start | bytes 5505028
  26.2 26.9 %all-to-all-start.2 = ((bf16[16,448,128]{2,1,0:T(8,128)(2,1)}), bf16[16,448,128]{2,1,0:T(8,128)(2,1)S(1)}, u32[]{:S(2)}, u32[]{:S(2)}) async-start(bf16[16,448,128]{2,1,0:T(8,128)(2,1)} %copy-done), calls=%async_computation.2 | async-start | bytes 3670016 | tf_op jit(solution)/shard_map/all_to_all | solution.py:294
  30.0 3.3 %collective-permute-start.1 = (f32[16,1024]{1,0:T(8,128)S(1)}, f32[16,1024]{1,0:T(8,128)S(1)}, u32[]{:S(2)}, u32[]{:S(2)}) collective-permute-start(f32[16,1024]{1,0:T(8,128)S(1)} %get-tuple-element.29), channel_id=1, source_target_pairs={{0,16},{16,0},{1,17},{17,1},{2,18},{18,2},{3,19},{19,3},{4,20},{20... | collective-permute-start | bytes 196616 | tf_op jit(solution)/shard_map/ppermute | solution.py:291
  33.4 8.7 %collective-permute-start.5 = (bf16[16,144,128]{2,1,0:T(8,128)(2,1)S(1)}, bf16[16,144,128]{2,1,0:T(8,128)(2,1)S(1)}, u32[]{:S(2)}, u32[]{:S(2)}) collective-permute-start(bf16[16,144,128]{2,1,0:T(8,128)(2,1)S(1)} %part.2), channel_id=1, source_target_pairs={{0,16},{16,0},{1,17},{17,1},{2,18},{18,2},{3,19},{19,3},{4,20},{20... | collective-permute-start | bytes 1769480 | tf_op jit(solution)/shard_map/ppermute | solution.py:291
  33.8 5.1 %collective-permute-start.4 = (f32[16,1024]{1,0:T(8,128)S(1)}, f32[16,1024]{1,0:T(8,128)S(1)}, u32[]{:S(2)}, u32[]{:S(2)}) collective-permute-start(f32[16,1024]{1,0:T(8,128)S(1)} %add.26.refs_0_.refs_1_), channel_id=1, source_target_pairs={{0,64},{32,96},{64,0},{96,32},{1,65},{33,97},{65,1},{97,33},{2,66}... | collective-permute-start | bytes 196616 | tf_op jit(solution)/shard_map/ppermute | solution.py:298
  36.5 3.7 %collective-permute-start.3 = (f32[16,1024]{1,0:T(8,128)S(1)}, f32[16,1024]{1,0:T(8,128)S(1)}, u32[]{:S(2)}, u32[]{:S(2)}) collective-permute-start(f32[16,1024]{1,0:T(8,128)S(1)} %add.26.refs_0_.refs_1_), channel_id=1, source_target_pairs={{0,96},{32,0},{64,32},{96,64},{1,97},{33,1},{65,33},{97,65},{2,98}... | collective-permute-start | bytes 196616 | tf_op jit(solution)/shard_map/ppermute | solution.py:298
  37.4 4.6 %collective-permute-start.2 = (f32[16,1024]{1,0:T(8,128)S(1)}, f32[16,1024]{1,0:T(8,128)S(1)}, u32[]{:S(2)}, u32[]{:S(2)}) collective-permute-start(f32[16,1024]{1,0:T(8,128)S(1)} %add.26.refs_0_.refs_1_), channel_id=1, source_target_pairs={{0,32},{32,64},{64,96},{96,0},{1,33},{33,65},{65,97},{97,1},{2,34}... | collective-permute-start | bytes 196616 | tf_op jit(solution)/shard_map/ppermute | solution.py:298
  42.5 5.0 %collective-permute-start.8 = (f32[16,1024]{1,0:T(8,128)S(1)}, f32[16,1024]{1,0:T(8,128)S(1)}, u32[]{:S(2)}, u32[]{:S(2)}) collective-permute-start(f32[16,1024]{1,0:T(8,128)S(1)} %get-tuple-element.33.refs_0_), channel_id=1, source_target_pairs={{0,64},{32,96},{64,0},{96,32},{1,65},{33,97},{65,1},{97,33},{2,66}... | collective-permute-start | bytes 196616 | tf_op jit(solution)/shard_map/ppermute | solution.py:298
  43.8 4.0 %collective-permute-start.7 = (f32[16,1024]{1,0:T(8,128)S(1)}, f32[16,1024]{1,0:T(8,128)S(1)}, u32[]{:S(2)}, u32[]{:S(2)}) collective-permute-start(f32[16,1024]{1,0:T(8,128)S(1)} %get-tuple-element.33.refs_0_), channel_id=1, source_target_pairs={{0,96},{32,0},{64,32},{96,64},{1,97},{33,1},{65,33},{97,65},{2,98}... | collective-permute-start | bytes 196616 | tf_op jit(solution)/shard_map/ppermute | solution.py:298
  44.8 5.3 %collective-permute-start.6 = (f32[16,1024]{1,0:T(8,128)S(1)}, f32[16,1024]{1,0:T(8,128)S(1)}, u32[]{:S(2)}, u32[]{:S(2)}) collective-permute-start(f32[16,1024]{1,0:T(8,128)S(1)} %get-tuple-element.33.refs_0_), channel_id=1, source_target_pairs={{0,32},{32,64},{64,96},{96,0},{1,33},{33,65},{65,97},{97,1},{2,34}... | collective-permute-start | bytes 196616 | tf_op jit(solution)/shard_map/ppermute | solution.py:298
  50.2 2.0 %copy-start.3 = (bf16[16,2,16,1024]{3,2,1,0:T(8,128)(2,1)}, bf16[16,2,16,1024]{3,2,1,0:T(8,128)(2,1)S(1)}, u32[]{:S(2)}) copy-start(bf16[16,2,16,1024]{3,2,1,0:T(8,128)(2,1)S(1)} %get-tuple-element.35) | copy-start | bytes 3145732
  50.3 2.8 %collective-permute-start.9 = (bf16[2,16,1024]{2,1,0:T(8,128)(2,1)S(1)}, bf16[2,16,1024]{2,1,0:T(8,128)(2,1)S(1)}, u32[]{:S(2)}, u32[]{:S(2)}) collective-permute-start(bf16[2,16,1024]{2,1,0:T(8,128)(2,1)S(1)} %get-tuple-element.37.refs_1_.refs_4_), channel_id=1, source_target_pairs={{0,16},{16,0},{1,17},{17,1},{2,18},{18,2},{3,19},{19,3},{4,20},{20... | collective-permute-start | bytes 196616 | tf_op jit(solution)/shard_map/ppermute | solution.py:291
  53.6 5.7 %collective-permute-start.10 = (f32[16,1024]{1,0:T(8,128)S(1)}, f32[16,1024]{1,0:T(8,128)S(1)}, u32[]{:S(2)}, u32[]{:S(2)}) collective-permute-start(f32[16,1024]{1,0:T(8,128)S(1)} %get-tuple-element.40), channel_id=1, source_target_pairs={{0,16},{16,0},{1,17},{17,1},{2,18},{18,2},{3,19},{19,3},{4,20},{20... | collective-permute-start | bytes 196616 | tf_op jit(solution)/shard_map/ppermute | solution.py:291
  60.3 13.1 %collective-permute-start.14 = (bf16[16,256,128]{2,1,0:T(8,128)(2,1)}, bf16[16,256,128]{2,1,0:T(8,128)(2,1)S(1)}, u32[]{:S(2)}, u32[]{:S(2)}) collective-permute-start(bf16[16,256,128]{2,1,0:T(8,128)(2,1)} %part.3), channel_id=1, source_target_pairs={{0,16},{16,0},{1,17},{17,1},{2,18},{18,2},{3,19},{19,3},{4,20},{20... | collective-permute-start | bytes 3145736 | tf_op jit(solution)/shard_map/ppermute | solution.py:291
  60.6 22.8 %all-to-all-start.1 = ((bf16[16,2,16,1024]{3,2,1,0:T(8,128)(2,1)}), bf16[16,2,16,1024]{3,2,1,0:T(8,128)(2,1)}, u32[]{:S(2)}, u32[]{:S(2)}) async-start(bf16[16,2,16,1024]{3,2,1,0:T(8,128)(2,1)} %copy-done.3), calls=%async_computation.1 | async-start | bytes 2097152 | tf_op jit(solution)/shard_map/all_to_all | solution.py:294
  65.0 5.1 %collective-permute-start.13 = (f32[16,1024]{1,0:T(8,128)S(1)}, f32[16,1024]{1,0:T(8,128)S(1)}, u32[]{:S(2)}, u32[]{:S(2)}) collective-permute-start(f32[16,1024]{1,0:T(8,128)S(1)} %add.27.refs_0_.refs_1_), channel_id=1, source_target_pairs={{0,64},{32,96},{64,0},{96,32},{1,65},{33,97},{65,1},{97,33},{2,66}... | collective-permute-start | bytes 196616 | tf_op jit(solution)/shard_map/ppermute | solution.py:298
  67.8 3.8 %collective-permute-start.12 = (f32[16,1024]{1,0:T(8,128)S(1)}, f32[16,1024]{1,0:T(8,128)S(1)}, u32[]{:S(2)}, u32[]{:S(2)}) collective-permute-start(f32[16,1024]{1,0:T(8,128)S(1)} %add.27.refs_0_.refs_1_), channel_id=1, source_target_pairs={{0,96},{32,0},{64,32},{96,64},{1,97},{33,1},{65,33},{97,65},{2,98}... | collective-permute-start | bytes 196616 | tf_op jit(solution)/shard_map/ppermute | solution.py:298
  68.6 4.7 %collective-permute-start.11 = (f32[16,1024]{1,0:T(8,128)S(1)}, f32[16,1024]{1,0:T(8,128)S(1)}, u32[]{:S(2)}, u32[]{:S(2)}) collective-permute-start(f32[16,1024]{1,0:T(8,128)S(1)} %add.27.refs_0_.refs_1_), channel_id=1, source_target_pairs={{0,32},{32,64},{64,96},{96,0},{1,33},{33,65},{65,97},{97,1},{2,34}... | collective-permute-start | bytes 196616 | tf_op jit(solution)/shard_map/ppermute | solution.py:298
  74.0 4.8 %collective-permute-start.17 = (f32[16,1024]{1,0:T(8,128)S(1)}, f32[16,1024]{1,0:T(8,128)S(1)}, u32[]{:S(2)}, u32[]{:S(2)}) collective-permute-start(f32[16,1024]{1,0:T(8,128)S(1)} %step.3.refs_0_), channel_id=1, source_target_pairs={{0,64},{32,96},{64,0},{96,32},{1,65},{33,97},{65,1},{97,33},{2,66}... | collective-permute-start | bytes 196616 | tf_op jit(solution)/shard_map/ppermute | solution.py:298
  75.3 3.8 %collective-permute-start.16 = (f32[16,1024]{1,0:T(8,128)S(1)}, f32[16,1024]{1,0:T(8,128)S(1)}, u32[]{:S(2)}, u32[]{:S(2)}) collective-permute-start(f32[16,1024]{1,0:T(8,128)S(1)} %step.3.refs_0_), channel_id=1, source_target_pairs={{0,96},{32,0},{64,32},{96,64},{1,97},{33,1},{65,33},{97,65},{2,98}... | collective-permute-start | bytes 196616 | tf_op jit(solution)/shard_map/ppermute | solution.py:298
  76.3 5.0 %collective-permute-start.15 = (f32[16,1024]{1,0:T(8,128)S(1)}, f32[16,1024]{1,0:T(8,128)S(1)}, u32[]{:S(2)}, u32[]{:S(2)}) collective-permute-start(f32[16,1024]{1,0:T(8,128)S(1)} %step.3.refs_0_), channel_id=1, source_target_pairs={{0,32},{32,64},{64,96},{96,0},{1,33},{33,65},{65,97},{97,1},{2,34}... | collective-permute-start | bytes 196616 | tf_op jit(solution)/shard_map/ppermute | solution.py:298
  82.5 0.6 copy-start.6
  83.4 8.4 %collective-permute-start.18 = (bf16[16,2,16,1024]{3,2,1,0:T(8,128)(2,1)}, bf16[16,2,16,1024]{3,2,1,0:T(8,128)(2,1)S(1)}, u32[]{:S(2)}, u32[]{:S(2)}) collective-permute-start(bf16[16,2,16,1024]{3,2,1,0:T(8,128)(2,1)} %all-to-all-done.1.refs_2_), channel_id=1, source_target_pairs={{0,16},{16,0},{1,17},{17,1},{2,18},{18,2},{3,19},{19,3},{4,20},{20... | collective-permute-start | bytes 3145736 | tf_op jit(solution)/shard_map/ppermute | solution.py:291
  85.1 24.3 %all-to-all-start.3 = ((bf16[16,2,16,1024]{3,2,1,0:T(8,128)(2,1)}), bf16[16,2,16,1024]{3,2,1,0:T(8,128)(2,1)S(1)}, u32[]{:S(2)}, u32[]{:S(2)}) async-start(bf16[16,2,16,1024]{3,2,1,0:T(8,128)(2,1)} %get-tuple-element.48), calls=%async_computation.3 | async-start | bytes 2097152 | tf_op jit(solution)/shard_map/all_to_all | solution.py:294
  91.9 1.0 copy-start.8
  109.4 3.7 %copy-start.7 = (bf16[16,2,16,1024]{3,2,1,0:T(8,128)(2,1)}, bf16[16,2,16,1024]{3,2,1,0:T(8,128)(2,1)S(1)}, u32[]{:S(2)}) copy-start(bf16[16,2,16,1024]{3,2,1,0:T(8,128)(2,1)S(1)} %all-to-all-done.3.refs_2_) | copy-start | bytes 3145732
  109.4 3.7 %collective-permute-start.19 = (bf16[16,2,16,1024]{3,2,1,0:T(8,128)(2,1)S(1)}, bf16[16,2,16,1024]{3,2,1,0:T(8,128)(2,1)S(1)}, u32[]{:S(2)}, u32[]{:S(2)}) collective-permute-start(bf16[16,2,16,1024]{3,2,1,0:T(8,128)(2,1)S(1)} %all-to-all-done.3.refs_2_), channel_id=1, source_target_pairs={{0,16},{16,0},{1,17},{17,1},{2,18},{18,2},{3,19},{19,3},{4,20},{20... | collective-permute-start | bytes 3145736 | tf_op jit(solution)/shard_map/ppermute | solution.py:291
  113.1 1.0 copy-start.9

commit v5 on v4

--- a/solution.py
+++ b/solution.py
@@ -80,18 +80,30 @@
     count = len(members) * inverse.shape[1] + (REST if members[0][0] == 0 else 0)
     shape = (copies, count, inverse.shape[2])
 
-    def whole(shape):
-        return pl.BlockSpec(shape, lambda i: (0,) * len(shape))
-
-    held = 2
+    def kernel(inverse_from, across_from, *refs):
+        out_ref, inverse_ref, across_ref, sems = refs[-4:]
+        moves = [
+            pltpu.make_async_copy(inverse_from, inverse_ref, sems.at[0]),
+            pltpu.make_async_copy(across_from, across_ref, sems.at[1]),
+        ]
+        for move in moves:
+            move.start()
+        for move in moves:
+            move.wait()
+        pack_kernel(members, inverse_ref, across_ref, out_ref)
+
     return pl.pallas_call(
-        lambda *refs: pack_kernel(members, *refs[:held], refs[-1]),
-        grid=(1,),
-        in_specs=[whole(inverse.shape), whole(across.shape)]
+        kernel,
+        in_specs=[pl.BlockSpec(memory_space=pltpu.HBM)] * 2
         + [pl.BlockSpec(memory_space=pl.ANY)] * len(after),
         out_specs=pl.BlockSpec(memory_space=pltpu.VMEM),
         out_shape=jax.ShapeDtypeStruct(shape, jnp.bfloat16),
-        compiler_params=pltpu.CompilerParams(vmem_limit_bytes=24 * MIB),
+        scratch_shapes=[
+            pltpu.VMEM(inverse.shape, inverse.dtype),
+            pltpu.VMEM(across.shape, across.dtype),
+            pltpu.SemaphoreType.DMA((2,)),
+        ],
+        compiler_params=pltpu.CompilerParams(vmem_limit_bytes=(24 if after else 63) * MIB),
         name="pack",
     )(inverse, across, *after)
 
@@ -231,7 +243,7 @@
             total = total - pattern_ref[row, column].astype(jnp.float32) * product
         out_ref[0, :, lanes] = total
 
-    @pl.when((row == 0) & (pl.program_id(1) == 0))
+    @pl.when((row == 0) & (pl.program_id(1) == 1))
     def _():
         own = own_ref.shape[1]
         lane = lax.broadcasted_iota(jnp.int32, (own, depth), 1)

time: 126 us -> 126 us (level)
  Pallas kernels: 27 us -> 29.1 us
    unnamed x22 -> x20, local copies, waits for them, and re-layouts: 4.59 us -> 3.88 us
  transfers between devices with their start and end apart: 24 -> 24, of which waited for: 20 -> 18; matrix products, arithmetic and copies ran while one was open for 1% -> 1% of each run, Pallas kernels for 11% -> 12%
where the time goes in v5:
time: 126 us; the launch traced here: 125 us
  starting transfers between devices  51.3 us (41%)
  waiting for transfers between devices  38.9 us (31%)
  Pallas kernels  29.1 us (23%)
  local copies, waits for them, and re-layouts  5.13 us (4%)
    all_to_all x4, starting transfers between devices, exchange(): return lax.all_to_all(value, ('z', 'y'), 0, 0)  23.5 us
    pallas_call x2, Pallas kernels, trail(): pl.pallas_call(lambda *refs: trail_kernel(columns, before, *refs[:held],...  21.3 us
    ppermute x12, waiting for transfers between devices, parts_over_x(): lax.ppermute(value, 'x', [(i, (i + k) % n_x) for i in range(n_x)])  18 us
    all_to_all x4, waiting for transfers between devices, exchange(): return lax.all_to_all(value, ('z', 'y'), 0, 0)  15.8 us
    ppermute x8, starting transfers between devices, swap(): lax.ppermute(value, 'core', [(i, n_core - 1 - i) for i in range(n_core)])  14 us
    ppermute x12, starting transfers between devices, parts_over_x(): lax.ppermute(value, 'x', [(i, (i + k) % n_x) for i in range(n_x)])  13.9 us
    pallas_call x10, Pallas kernels, call(): pl.pallas_call(lambda *refs: kernel(*refs[:count], *refs[count + len(afte...  5.26 us
    ppermute x8, waiting for transfers between devices, swap(): lax.ppermute(value, 'core', [(i, n_core - 1 - i) for i in range(n_core)])  5 us
  transfers between devices with their start and end apart: 24, of which 18 were waited for; matrix products, arithmetic and copies ran while one was open for 1% of the time, Pallas kernels for 12%

profile of v5, /device:TPU:1, one launch (start us, length us, event | category | flops | bytes accessed | tf_op | source)
XLA Modules:
  0.0 125.4 jit_solution(9025107462762674401)
XLA Ops:
  0.6 2.1 %pack.2.refs_0_ = bf16[16,208,128]{2,1,0:T(8,128)(2,1)} custom-call(f32[4,64,128]{2,1,0:T(8,128)} %inverse_from.3, bf16[4,4,64,128]{3,2,1,0:T(8,128)(2,1)} %bitcast.14), custom_call_target="tpu_custom_call" | custom-call | tf_op jit(solution)/shard_map/pack/pallas_call | solution.py:95
  2.7 8.6 %all-to-all-start = ((bf16[16,208,128]{2,1,0:T(8,128)(2,1)}), bf16[16,208,128]{2,1,0:T(8,128)(2,1)S(1)}, u32[]{:S(2)}, u32[]{:S(2)}) async-start(bf16[16,208,128]{2,1,0:T(8,128)(2,1)} %pack.2.refs_0_), calls=%async_computation | async-start | bytes 1703936 | tf_op jit(solution)/shard_map/all_to_all | solution.py:306
  11.4 1.2 constant_dynamic-slice_fusion.1
  12.6 0.1 copy.13
  12.7 1.0 collective-permute-start
  13.7 0.1 copy.12
  13.9 1.1 copy-done.1
  15.0 0.5 pack.3.refs_3_
  15.5 0.0 copy-start
  15.5 0.0 collective-permute-done
  15.6 9.7 %all-to-all-done.refs_1_.refs_0_.refs_2_ = bf16[16,208,128]{2,1,0:T(8,128)(2,1)S(1)} async-done(((bf16[16,208,128]{2,1,0:T(8,128)(2,1)}), bf16[16,208,128]{2,1,0:T(8,128)(2,1)S(1)}, u32[]{:S(2)}, u32[]{:S(2)}) %all-to-all-start) | async-done | bytes 852000 | tf_op jit(solution)/shard_map/all_to_all | solution.py:306
  25.2 0.2 first.1
  25.5 3.8 %all-to-all-start.2 = ((bf16[16,448,128]{2,1,0:T(8,128)(2,1)}), bf16[16,448,128]{2,1,0:T(8,128)(2,1)S(1)}, u32[]{:S(2)}, u32[]{:S(2)}) async-start(bf16[16,448,128]{2,1,0:T(8,128)(2,1)} %copy-done), calls=%async_computation.2 | async-start | bytes 3670016 | tf_op jit(solution)/shard_map/all_to_all | solution.py:306
  29.3 2.4 %collective-permute-start.1 = (f32[16,1024]{1,0:T(8,128)S(1)}, f32[16,1024]{1,0:T(8,128)S(1)}, u32[]{:S(2)}, u32[]{:S(2)}) collective-permute-start(f32[16,1024]{1,0:T(8,128)S(1)} %get-tuple-element.29), channel_id=1, source_target_pairs={{0,16},{16,0},{1,17},{17,1},{2,18},{18,2},{3,19},{19,3},{4,20},{20... | collective-permute-start | bytes 196616 | tf_op jit(solution)/shard_map/ppermute | solution.py:303
  31.6 0.9 collective-permute-done.1
  32.6 0.4 collective-permute-start.5
  33.0 2.7 %collective-permute-start.4 = (f32[16,1024]{1,0:T(8,128)S(1)}, f32[16,1024]{1,0:T(8,128)S(1)}, u32[]{:S(2)}, u32[]{:S(2)}) collective-permute-start(f32[16,1024]{1,0:T(8,128)S(1)} %add.26.refs_0_.refs_1_), channel_id=1, source_target_pairs={{0,64},{32,96},{64,0},{96,32},{1,65},{33,97},{65,1},{97,33},{2,66}... | collective-permute-start | bytes 196616 | tf_op jit(solution)/shard_map/ppermute | solution.py:310
  35.8 0.9 collective-permute-start.3
  36.6 0.6 collective-permute-start.2
  37.3 0.8 collective-permute-done.4.refs_3_
  38.1 1.4 %collective-permute-done.3.refs_2_ = f32[16,1024]{1,0:T(8,128)S(1)} collective-permute-done((f32[16,1024]{1,0:T(8,128)S(1)}, f32[16,1024]{1,0:T(8,128)S(1)}, u32[]{:S(2)}, u32[]{:S(2)}) %collective-permute-start.3) | collective-permute-done | bytes 65568 | tf_op jit(solution)/shard_map/ppermute | solution.py:310
  39.5 1.7 %collective-permute-done.2.refs_1_ = f32[16,1024]{1,0:T(8,128)S(1)} collective-permute-done((f32[16,1024]{1,0:T(8,128)S(1)}, f32[16,1024]{1,0:T(8,128)S(1)}, u32[]{:S(2)}, u32[]{:S(2)}) %collective-permute-start.2) | collective-permute-done | bytes 65568 | tf_op jit(solution)/shard_map/ppermute | solution.py:310
  41.3 0.5 step.2
  41.8 1.2 collective-permute-start.8
  43.0 1.1 collective-permute-start.7
  44.1 0.4 collective-permute-start.6
  44.5 2.3 %collective-permute-done.8.refs_3_ = f32[16,1024]{1,0:T(8,128)S(1)} collective-permute-done((f32[16,1024]{1,0:T(8,128)S(1)}, f32[16,1024]{1,0:T(8,128)S(1)}, u32[]{:S(2)}, u32[]{:S(2)}) %collective-permute-start.8) | collective-permute-done | bytes 65568 | tf_op jit(solution)/shard_map/ppermute | solution.py:310
  46.8 0.2 collective-permute-done.7.refs_2_
  47.0 2.4 %collective-permute-done.6.refs_1_ = f32[16,1024]{1,0:T(8,128)S(1)} collective-permute-done((f32[16,1024]{1,0:T(8,128)S(1)}, f32[16,1024]{1,0:T(8,128)S(1)}, u32[]{:S(2)}, u32[]{:S(2)}) %collective-permute-start.6) | collective-permute-done | bytes 65568 | tf_op jit(solution)/shard_map/ppermute | solution.py:310
  49.4 0.1 close.5
  49.5 1.9 %collective-permute-start.9 = (bf16[2,16,1024]{2,1,0:T(8,128)(2,1)S(1)}, bf16[2,16,1024]{2,1,0:T(8,128)(2,1)S(1)}, u32[]{:S(2)}, u32[]{:S(2)}) collective-permute-start(bf16[2,16,1024]{2,1,0:T(8,128)(2,1)S(1)} %get-tuple-element.37.refs_1_.refs_4_), channel_id=1, source_target_pairs={{0,16},{16,0},{1,17},{17,1},{2,18},{18,2},{3,19},{19,3},{4,20},{20... | collective-permute-start | bytes 196616 | tf_op jit(solution)/shard_map/ppermute | solution.py:303
  51.5 0.9 collective-permute-done.9.refs_2_
  52.4 0.0 all-to-all-done.2.refs_4_.refs_0_.refs_2_
  52.4 0.4 split.1
  52.8 4.8 %collective-permute-start.10 = (f32[16,1024]{1,0:T(8,128)S(1)}, f32[16,1024]{1,0:T(8,128)S(1)}, u32[]{:S(2)}, u32[]{:S(2)}) collective-permute-start(f32[16,1024]{1,0:T(8,128)S(1)} %get-tuple-element.40), channel_id=1, source_target_pairs={{0,16},{16,0},{1,17},{17,1},{2,18},{18,2},{3,19},{19,3},{4,20},{20... | collective-permute-start | bytes 196616 | tf_op jit(solution)/shard_map/ppermute | solution.py:303
  57.6 0.9 collective-permute-done.10
  58.5 1.0 part.3
  59.5 0.4 collective-permute-start.14
  59.9 4.3 %all-to-all-start.1 = ((bf16[16,2,16,1024]{3,2,1,0:T(8,128)(2,1)}), bf16[16,2,16,1024]{3,2,1,0:T(8,128)(2,1)}, u32[]{:S(2)}, u32[]{:S(2)}) async-start(bf16[16,2,16,1024]{3,2,1,0:T(8,128)(2,1)} %copy-done.3), calls=%async_computation.1 | async-start | bytes 2097152 | tf_op jit(solution)/shard_map/all_to_all | solution.py:306
  64.2 2.8 %collective-permute-start.13 = (f32[16,1024]{1,0:T(8,128)S(1)}, f32[16,1024]{1,0:T(8,128)S(1)}, u32[]{:S(2)}, u32[]{:S(2)}) collective-permute-start(f32[16,1024]{1,0:T(8,128)S(1)} %add.27.refs_0_.refs_1_), channel_id=1, source_target_pairs={{0,64},{32,96},{64,0},{96,32},{1,65},{33,97},{65,1},{97,33},{2,66}... | collective-permute-start | bytes 196616 | tf_op jit(solution)/shard_map/ppermute | solution.py:310
  67.1 0.8 collective-permute-start.12
  67.9 0.6 collective-permute-start.11
  68.5 0.8 collective-permute-done.13.refs_3_
  69.4 1.5 %collective-permute-done.12.refs_2_ = f32[16,1024]{1,0:T(8,128)S(1)} collective-permute-done((f32[16,1024]{1,0:T(8,128)S(1)}, f32[16,1024]{1,0:T(8,128)S(1)}, u32[]{:S(2)}, u32[]{:S(2)}) %collective-permute-start.12) | collective-permute-done | bytes 65568 | tf_op jit(solution)/shard_map/ppermute | solution.py:310
  70.9 1.7 %collective-permute-done.11.refs_1_ = f32[16,1024]{1,0:T(8,128)S(1)} collective-permute-done((f32[16,1024]{1,0:T(8,128)S(1)}, f32[16,1024]{1,0:T(8,128)S(1)}, u32[]{:S(2)}, u32[]{:S(2)}) %collective-permute-start.11) | collective-permute-done | bytes 65568 | tf_op jit(solution)/shard_map/ppermute | solution.py:310
  72.7 1.8 %step.3.refs_0_ = f32[16,1024]{1,0:T(8,128)S(1)} custom-call(f32[5,2,16,128]{3,2,1,0:T(8,128)S(1)} %get-tuple-element.36.refs_0_, bf16[3,16,1024]{2,1,0:T(8,128)(2,1)S(1)} %get-tuple-element.42.refs_1_.refs_4_, bf16[16,448,128]{2,1,0:T(8,128)(2,1)S(1)} %all-to-all-done.2.refs_4_.refs_0_.refs_2_, bf16[16,256,128]{2,1,0:T(8,128)(2,1)} %collective-permute-done.14.refs_3_), custom_call_target="tpu_custom_call" | custom-call | flops 1048576 | bytes 65536 | tf_op jit(solution)/shard_map/step/pallas_call | solution.py:38
  74.5 1.2 collective-permute-start.17
  75.8 1.0 collective-permute-start.16
  76.8 0.4 collective-permute-start.15
  77.2 2.0 %collective-permute-done.17.refs_3_ = f32[16,1024]{1,0:T(8,128)S(1)} collective-permute-done((f32[16,1024]{1,0:T(8,128)S(1)}, f32[16,1024]{1,0:T(8,128)S(1)}, u32[]{:S(2)}, u32[]{:S(2)}) %collective-permute-start.17) | collective-permute-done | bytes 65568 | tf_op jit(solution)/shard_map/ppermute | solution.py:310
  79.2 0.4 collective-permute-done.16.refs_2_
  79.6 2.6 %collective-permute-done.15.refs_1_ = f32[16,1024]{1,0:T(8,128)S(1)} collective-permute-done((f32[16,1024]{1,0:T(8,128)S(1)}, f32[16,1024]{1,0:T(8,128)S(1)}, u32[]{:S(2)}, u32[]{:S(2)}) %collective-permute-start.15) | collective-permute-done | bytes 65568 | tf_op jit(solution)/shard_map/ppermute | solution.py:310
  82.2 1.1 close.7
  83.3 0.6 copy-done.5
  83.9 1.7 %collective-permute-start.18 = (bf16[16,2,16,1024]{3,2,1,0:T(8,128)(2,1)}, bf16[16,2,16,1024]{3,2,1,0:T(8,128)(2,1)S(1)}, u32[]{:S(2)}, u32[]{:S(2)}) collective-permute-start(bf16[16,2,16,1024]{3,2,1,0:T(8,128)(2,1)} %all-to-all-done.1.refs_2_), channel_id=1, source_target_pairs={{0,16},{16,0},{1,17},{17,1},{2,18},{18,2},{3,19},{19,3},{4,20},{20... | collective-permute-start | bytes 3145736 | tf_op jit(solution)/shard_map/ppermute | solution.py:303
  85.6 6.7 %all-to-all-start.3 = ((bf16[16,2,16,1024]{3,2,1,0:T(8,128)(2,1)}), bf16[16,2,16,1024]{3,2,1,0:T(8,128)(2,1)S(1)}, u32[]{:S(2)}, u32[]{:S(2)}) async-start(bf16[16,2,16,1024]{3,2,1,0:T(8,128)(2,1)} %get-tuple-element.48), calls=%async_computation.3 | async-start | bytes 2097152 | tf_op jit(solution)/shard_map/all_to_all | solution.py:306
  92.3 0.0 copy-start.7
  92.4 1.0 copy-done.7
  93.3 10.5 %trail.2 = (f32[2,1024,512]{2,1,0:T(8,128)}, bf16[2,64,512]{2,1,0:T(8,128)(2,1)}) custom-call(s32[2,4]{1,0:T(2,128)} %refs_0_.3, bf16[2,1024,512]{2,1,0:T(8,128)(2,1)} %refs_1_.1, bf16[16,2,16,1024]{3,2,1,0:T(8,128)(2,1)} %all-to-all-done.1.refs_2_, bf16[16,2,16,1024]{3,2,1,0:T(8,128)(2,1)} %copy-done.7, bf16[2,4,1024,1024]{3,2,1,0:T(8,128)(2,1)} %refs_5_.3, ...), custom_call_target="tpu_custom_call" | custom-call | flops 4294967296 | bytes 8388608 | tf_op jit(solution)/shard_map/trail/pallas_call | solution.py:276
  103.8 6.1 %all-to-all-done.3.refs_2_ = bf16[16,2,16,1024]{3,2,1,0:T(8,128)(2,1)S(1)} async-done(((bf16[16,2,16,1024]{3,2,1,0:T(8,128)(2,1)}), bf16[16,2,16,1024]{3,2,1,0:T(8,128)(2,1)S(1)}, u32[]{:S(2)}, u32[]{:S(2)}) %all-to-all-start.3) | async-done | bytes 1048608 | tf_op jit(solution)/shard_map/all_to_all | solution.py:306
  109.9 1.4 %collective-permute-start.19 = (bf16[16,2,16,1024]{3,2,1,0:T(8,128)(2,1)S(1)}, bf16[16,2,16,1024]{3,2,1,0:T(8,128)(2,1)S(1)}, u32[]{:S(2)}, u32[]{:S(2)}) collective-permute-start(bf16[16,2,16,1024]{3,2,1,0:T(8,128)(2,1)S(1)} %all-to-all-done.3.refs_2_), channel_id=1, source_target_pairs={{0,16},{16,0},{1,17},{17,1},{2,18},{18,2},{3,19},{19,3},{4,20},{20... | collective-permute-start | bytes 3145736 | tf_op jit(solution)/shard_map/ppermute | solution.py:303
  111.3 2.3 %collective-permute-done.19.refs_3_ = bf16[16,2,16,1024]{3,2,1,0:T(8,128)(2,1)S(1)} collective-permute-done((bf16[16,2,16,1024]{3,2,1,0:T(8,128)(2,1)S(1)}, bf16[16,2,16,1024]{3,2,1,0:T(8,128)(2,1)S(1)}, u32[]{:S(2)}, u32[]{:S(2)}) %collective-permute-start.19) | collective-permute-done | bytes 1048608 | tf_op jit(solution)/shard_map/ppermute | solution.py:303
  113.6 1.0 copy-done.8
  114.6 10.8 %trail.3 = (f32[2,1024,512]{2,1,0:T(8,128)}, bf16[4,64,512]{2,1,0:T(8,128)(2,1)}) custom-call(s32[2,4]{1,0:T(2,128)} %refs_0_.3, f32[2,1024,512]{2,1,0:T(8,128)} %get-tuple-element.47.refs_1_, bf16[16,2,16,1024]{3,2,1,0:T(8,128)(2,1)} %copy-done.6, bf16[16,2,16,1024]{3,2,1,0:T(8,128)(2,1)} %copy-done.8, bf16[2,4,1024,1024]{3,2,1,0:T(8,128)(2,1)} %refs_5_.3, ...), custom_call_target="tpu_custom_call" | custom-call | flops 4294967296 | bytes 8388608 | tf_op jit(solution)/shard_map/trail/pallas_call | solution.py:276
  (27 shorter events, 0.2 us)
Async XLA Ops:
  0.6 13.2 %copy-start.4 = (f32[4,64,128]{2,1,0:T(8,128)S(1)}, f32[4,64,128]{2,1,0:T(8,128)}, u32[]{:S(2)}) copy-start(f32[4,64,128]{2,1,0:T(8,128)} %inverse_from.3) | copy-start | bytes 393220
  0.6 13.2 %copy-start.2 = (bf16[4,4,128,64]{2,3,1,0:T(8,128)(2,1)S(1)}, bf16[4,4,128,64]{2,3,1,0:T(8,128)(2,1)}, u32[]{:S(2)}) copy-start(bf16[4,4,128,64]{2,3,1,0:T(8,128)(2,1)} %param.9) | copy-start | bytes 786436
  2.7 22.5 %all-to-all-start = ((bf16[16,208,128]{2,1,0:T(8,128)(2,1)}), bf16[16,208,128]{2,1,0:T(8,128)(2,1)S(1)}, u32[]{:S(2)}, u32[]{:S(2)}) async-start(bf16[16,208,128]{2,1,0:T(8,128)(2,1)} %pack.2.refs_0_), calls=%async_computation | async-start | bytes 1703936 | tf_op jit(solution)/shard_map/all_to_all | solution.py:306
  12.7 2.8 %collective-permute-start = (f32[4,16,128]{2,1,0:T(8,128)S(1)}, f32[4,16,128]{2,1,0:T(8,128)S(1)}, u32[]{:S(2)}, u32[]{:S(2)}) collective-permute-start(f32[4,16,128]{2,1,0:T(8,128)S(1)} %bitcast.18), channel_id=1, source_target_pairs={{0,16},{16,0},{1,17},{17,1},{2,18},{18,2},{3,19},{19,3},{4,20},{20... | collective-permute-start | bytes 98312 | tf_op jit(solution)/shard_map/ppermute | solution.py:303
  13.9 1.2 copy-start.1
  15.5 10.0 %copy-start = (bf16[16,448,128]{2,1,0:T(8,128)(2,1)}, bf16[16,448,128]{2,1,0:T(8,128)(2,1)S(1)}, u32[]{:S(2)}) copy-start(bf16[16,448,128]{2,1,0:T(8,128)(2,1)S(1)} %pack.3.refs_3_) | copy-start | bytes 5505028
  25.5 26.9 %all-to-all-start.2 = ((bf16[16,448,128]{2,1,0:T(8,128)(2,1)}), bf16[16,448,128]{2,1,0:T(8,128)(2,1)S(1)}, u32[]{:S(2)}, u32[]{:S(2)}) async-start(bf16[16,448,128]{2,1,0:T(8,128)(2,1)} %copy-done), calls=%async_computation.2 | async-start | bytes 3670016 | tf_op jit(solution)/shard_map/all_to_all | solution.py:306
  29.3 3.3 %collective-permute-start.1 = (f32[16,1024]{1,0:T(8,128)S(1)}, f32[16,1024]{1,0:T(8,128)S(1)}, u32[]{:S(2)}, u32[]{:S(2)}) collective-permute-start(f32[16,1024]{1,0:T(8,128)S(1)} %get-tuple-element.29), channel_id=1, source_target_pairs={{0,16},{16,0},{1,17},{17,1},{2,18},{18,2},{3,19},{19,3},{4,20},{20... | collective-permute-start | bytes 196616 | tf_op jit(solution)/shard_map/ppermute | solution.py:303
  32.6 8.7 %collective-permute-start.5 = (bf16[16,144,128]{2,1,0:T(8,128)(2,1)S(1)}, bf16[16,144,128]{2,1,0:T(8,128)(2,1)S(1)}, u32[]{:S(2)}, u32[]{:S(2)}) collective-permute-start(bf16[16,144,128]{2,1,0:T(8,128)(2,1)S(1)} %part.2), channel_id=1, source_target_pairs={{0,16},{16,0},{1,17},{17,1},{2,18},{18,2},{3,19},{19,3},{4,20},{20... | collective-permute-start | bytes 1769480 | tf_op jit(solution)/shard_map/ppermute | solution.py:303
  33.0 5.1 %collective-permute-start.4 = (f32[16,1024]{1,0:T(8,128)S(1)}, f32[16,1024]{1,0:T(8,128)S(1)}, u32[]{:S(2)}, u32[]{:S(2)}) collective-permute-start(f32[16,1024]{1,0:T(8,128)S(1)} %add.26.refs_0_.refs_1_), channel_id=1, source_target_pairs={{0,64},{32,96},{64,0},{96,32},{1,65},{33,97},{65,1},{97,33},{2,66}... | collective-permute-start | bytes 196616 | tf_op jit(solution)/shard_map/ppermute | solution.py:310
  35.8 3.7 %collective-permute-start.3 = (f32[16,1024]{1,0:T(8,128)S(1)}, f32[16,1024]{1,0:T(8,128)S(1)}, u32[]{:S(2)}, u32[]{:S(2)}) collective-permute-start(f32[16,1024]{1,0:T(8,128)S(1)} %add.26.refs_0_.refs_1_), channel_id=1, source_target_pairs={{0,96},{32,0},{64,32},{96,64},{1,97},{33,1},{65,33},{97,65},{2,98}... | collective-permute-start | bytes 196616 | tf_op jit(solution)/shard_map/ppermute | solution.py:310
  36.6 4.6 %collective-permute-start.2 = (f32[16,1024]{1,0:T(8,128)S(1)}, f32[16,1024]{1,0:T(8,128)S(1)}, u32[]{:S(2)}, u32[]{:S(2)}) collective-permute-start(f32[16,1024]{1,0:T(8,128)S(1)} %add.26.refs_0_.refs_1_), channel_id=1, source_target_pairs={{0,32},{32,64},{64,96},{96,0},{1,33},{33,65},{65,97},{97,1},{2,34}... | collective-permute-start | bytes 196616 | tf_op jit(solution)/shard_map/ppermute | solution.py:310
  41.8 5.0 %collective-permute-start.8 = (f32[16,1024]{1,0:T(8,128)S(1)}, f32[16,1024]{1,0:T(8,128)S(1)}, u32[]{:S(2)}, u32[]{:S(2)}) collective-permute-start(f32[16,1024]{1,0:T(8,128)S(1)} %get-tuple-element.33.refs_0_), channel_id=1, source_target_pairs={{0,64},{32,96},{64,0},{96,32},{1,65},{33,97},{65,1},{97,33},{2,66}... | collective-permute-start | bytes 196616 | tf_op jit(solution)/shard_map/ppermute | solution.py:310
  43.0 4.0 %collective-permute-start.7 = (f32[16,1024]{1,0:T(8,128)S(1)}, f32[16,1024]{1,0:T(8,128)S(1)}, u32[]{:S(2)}, u32[]{:S(2)}) collective-permute-start(f32[16,1024]{1,0:T(8,128)S(1)} %get-tuple-element.33.refs_0_), channel_id=1, source_target_pairs={{0,96},{32,0},{64,32},{96,64},{1,97},{33,1},{65,33},{97,65},{2,98}... | collective-permute-start | bytes 196616 | tf_op jit(solution)/shard_map/ppermute | solution.py:310
  44.1 5.3 %collective-permute-start.6 = (f32[16,1024]{1,0:T(8,128)S(1)}, f32[16,1024]{1,0:T(8,128)S(1)}, u32[]{:S(2)}, u32[]{:S(2)}) collective-permute-start(f32[16,1024]{1,0:T(8,128)S(1)} %get-tuple-element.33.refs_0_), channel_id=1, source_target_pairs={{0,32},{32,64},{64,96},{96,0},{1,33},{33,65},{65,97},{97,1},{2,34}... | collective-permute-start | bytes 196616 | tf_op jit(solution)/shard_map/ppermute | solution.py:310
  49.5 2.0 %copy-start.3 = (bf16[16,2,16,1024]{3,2,1,0:T(8,128)(2,1)}, bf16[16,2,16,1024]{3,2,1,0:T(8,128)(2,1)S(1)}, u32[]{:S(2)}) copy-start(bf16[16,2,16,1024]{3,2,1,0:T(8,128)(2,1)S(1)} %get-tuple-element.35) | copy-start | bytes 3145732
  49.5 2.8 %collective-permute-start.9 = (bf16[2,16,1024]{2,1,0:T(8,128)(2,1)S(1)}, bf16[2,16,1024]{2,1,0:T(8,128)(2,1)S(1)}, u32[]{:S(2)}, u32[]{:S(2)}) collective-permute-start(bf16[2,16,1024]{2,1,0:T(8,128)(2,1)S(1)} %get-tuple-element.37.refs_1_.refs_4_), channel_id=1, source_target_pairs={{0,16},{16,0},{1,17},{17,1},{2,18},{18,2},{3,19},{19,3},{4,20},{20... | collective-permute-start | bytes 196616 | tf_op jit(solution)/shard_map/ppermute | solution.py:303
  52.8 5.7 %collective-permute-start.10 = (f32[16,1024]{1,0:T(8,128)S(1)}, f32[16,1024]{1,0:T(8,128)S(1)}, u32[]{:S(2)}, u32[]{:S(2)}) collective-permute-start(f32[16,1024]{1,0:T(8,128)S(1)} %get-tuple-element.40), channel_id=1, source_target_pairs={{0,16},{16,0},{1,17},{17,1},{2,18},{18,2},{3,19},{19,3},{4,20},{20... | collective-permute-start | bytes 196616 | tf_op jit(solution)/shard_map/ppermute | solution.py:303
  59.5 13.1 %collective-permute-start.14 = (bf16[16,256,128]{2,1,0:T(8,128)(2,1)}, bf16[16,256,128]{2,1,0:T(8,128)(2,1)}, u32[]{:S(2)}, u32[]{:S(2)}) collective-permute-start(bf16[16,256,128]{2,1,0:T(8,128)(2,1)} %part.3), channel_id=1, source_target_pairs={{0,16},{16,0},{1,17},{17,1},{2,18},{18,2},{3,19},{19,3},{4,20},{20... | collective-permute-start | bytes 3145736 | tf_op jit(solution)/shard_map/ppermute | solution.py:303
  59.9 24.0 %all-to-all-start.1 = ((bf16[16,2,16,1024]{3,2,1,0:T(8,128)(2,1)}), bf16[16,2,16,1024]{3,2,1,0:T(8,128)(2,1)}, u32[]{:S(2)}, u32[]{:S(2)}) async-start(bf16[16,2,16,1024]{3,2,1,0:T(8,128)(2,1)} %copy-done.3), calls=%async_computation.1 | async-start | bytes 2097152 | tf_op jit(solution)/shard_map/all_to_all | solution.py:306
  64.2 5.1 %collective-permute-start.13 = (f32[16,1024]{1,0:T(8,128)S(1)}, f32[16,1024]{1,0:T(8,128)S(1)}, u32[]{:S(2)}, u32[]{:S(2)}) collective-permute-start(f32[16,1024]{1,0:T(8,128)S(1)} %add.27.refs_0_.refs_1_), channel_id=1, source_target_pairs={{0,64},{32,96},{64,0},{96,32},{1,65},{33,97},{65,1},{97,33},{2,66}... | collective-permute-start | bytes 196616 | tf_op jit(solution)/shard_map/ppermute | solution.py:310
  67.1 3.8 %collective-permute-start.12 = (f32[16,1024]{1,0:T(8,128)S(1)}, f32[16,1024]{1,0:T(8,128)S(1)}, u32[]{:S(2)}, u32[]{:S(2)}) collective-permute-start(f32[16,1024]{1,0:T(8,128)S(1)} %add.27.refs_0_.refs_1_), channel_id=1, source_target_pairs={{0,96},{32,0},{64,32},{96,64},{1,97},{33,1},{65,33},{97,65},{2,98}... | collective-permute-start | bytes 196616 | tf_op jit(solution)/shard_map/ppermute | solution.py:310
  67.9 4.7 %collective-permute-start.11 = (f32[16,1024]{1,0:T(8,128)S(1)}, f32[16,1024]{1,0:T(8,128)S(1)}, u32[]{:S(2)}, u32[]{:S(2)}) collective-permute-start(f32[16,1024]{1,0:T(8,128)S(1)} %add.27.refs_0_.refs_1_), channel_id=1, source_target_pairs={{0,32},{32,64},{64,96},{96,0},{1,33},{33,65},{65,97},{97,1},{2,34}... | collective-permute-start | bytes 196616 | tf_op jit(solution)/shard_map/ppermute | solution.py:310
  74.5 4.7 %collective-permute-start.17 = (f32[16,1024]{1,0:T(8,128)S(1)}, f32[16,1024]{1,0:T(8,128)S(1)}, u32[]{:S(2)}, u32[]{:S(2)}) collective-permute-start(f32[16,1024]{1,0:T(8,128)S(1)} %step.3.refs_0_), channel_id=1, source_target_pairs={{0,64},{32,96},{64,0},{96,32},{1,65},{33,97},{65,1},{97,33},{2,66}... | collective-permute-start | bytes 196616 | tf_op jit(solution)/shard_map/ppermute | solution.py:310
  75.8 3.8 %collective-permute-start.16 = (f32[16,1024]{1,0:T(8,128)S(1)}, f32[16,1024]{1,0:T(8,128)S(1)}, u32[]{:S(2)}, u32[]{:S(2)}) collective-permute-start(f32[16,1024]{1,0:T(8,128)S(1)} %step.3.refs_0_), channel_id=1, source_target_pairs={{0,96},{32,0},{64,32},{96,64},{1,97},{33,1},{65,33},{97,65},{2,98}... | collective-permute-start | bytes 196616 | tf_op jit(solution)/shard_map/ppermute | solution.py:310
  76.8 5.4 %collective-permute-start.15 = (f32[16,1024]{1,0:T(8,128)S(1)}, f32[16,1024]{1,0:T(8,128)S(1)}, u32[]{:S(2)}, u32[]{:S(2)}) collective-permute-start(f32[16,1024]{1,0:T(8,128)S(1)} %step.3.refs_0_), channel_id=1, source_target_pairs={{0,32},{32,64},{64,96},{96,0},{1,33},{33,65},{65,97},{97,1},{2,34}... | collective-permute-start | bytes 196616 | tf_op jit(solution)/shard_map/ppermute | solution.py:310
  83.3 0.6 copy-start.5
  83.9 8.4 %collective-permute-start.18 = (bf16[16,2,16,1024]{3,2,1,0:T(8,128)(2,1)}, bf16[16,2,16,1024]{3,2,1,0:T(8,128)(2,1)S(1)}, u32[]{:S(2)}, u32[]{:S(2)}) collective-permute-start(bf16[16,2,16,1024]{3,2,1,0:T(8,128)(2,1)} %all-to-all-done.1.refs_2_), channel_id=1, source_target_pairs={{0,16},{16,0},{1,17},{17,1},{2,18},{18,2},{3,19},{19,3},{4,20},{20... | collective-permute-start | bytes 3145736 | tf_op jit(solution)/shard_map/ppermute | solution.py:303
  85.6 24.3 %all-to-all-start.3 = ((bf16[16,2,16,1024]{3,2,1,0:T(8,128)(2,1)}), bf16[16,2,16,1024]{3,2,1,0:T(8,128)(2,1)S(1)}, u32[]{:S(2)}, u32[]{:S(2)}) async-start(bf16[16,2,16,1024]{3,2,1,0:T(8,128)(2,1)} %get-tuple-element.48), calls=%async_computation.3 | async-start | bytes 2097152 | tf_op jit(solution)/shard_map/all_to_all | solution.py:306
  92.3 1.0 copy-start.7
  109.9 3.7 %copy-start.6 = (bf16[16,2,16,1024]{3,2,1,0:T(8,128)(2,1)}, bf16[16,2,16,1024]{3,2,1,0:T(8,128)(2,1)S(1)}, u32[]{:S(2)}) copy-start(bf16[16,2,16,1024]{3,2,1,0:T(8,128)(2,1)S(1)} %all-to-all-done.3.refs_2_) | copy-start | bytes 3145732
  109.9 3.7 %collective-permute-start.19 = (bf16[16,2,16,1024]{3,2,1,0:T(8,128)(2,1)S(1)}, bf16[16,2,16,1024]{3,2,1,0:T(8,128)(2,1)S(1)}, u32[]{:S(2)}, u32[]{:S(2)}) collective-permute-start(bf16[16,2,16,1024]{3,2,1,0:T(8,128)(2,1)S(1)} %all-to-all-done.3.refs_2_), channel_id=1, source_target_pairs={{0,16},{16,0},{1,17},{17,1},{2,18},{18,2},{3,19},{19,3},{4,20},{20... | collective-permute-start | bytes 3145736 | tf_op jit(solution)/shard_map/ppermute | solution.py:303
  113.6 1.0 copy-start.8
